TPU v7x, 32 devices: a whole 2x2x4 slice. The times are simulated.
32 devices in a mesh: dp: 4 (over x, core), space: 2 (over y), tm: 4 (over z).
Axes of the slice: x: 2, y: 2, z: 4, core: 2. Of those that a mesh axis runs over, the one named last changes fastest.
Arguments:
- inputs: bfloat16 [4, 32, 64, 512], P('dp', 'tm', None, 'space'), may hold values from -6 to 6
- grad_out: bfloat16 [4, 32, 64, 512], P('dp', 'tm', None, 'space'), may hold values from -6 to 6
- conv_w: bfloat16 [2, 128, 64], replicated, may hold values from -0.5 to 0.5
- conv_b: float32 [128], replicated, may hold values from -3 to 3
- mix_w: bfloat16 [3, 64, 64], replicated, may hold values from -0.4375 to 0.4375
- mix_b: float32 [64], replicated, may hold values from -3 to 3
- adj_tiles: bfloat16 [4, 8, 128, 128], P('space'), may hold values from -0.1875 to 0.1875
- tile_cols: int32 [4, 8], P('space'), may hold values from 0 to 2, as said below
- send_rows: int32 [2, 2, 64], P('space'), may hold values from 0 to 255
- counts: int32 [2, 2], P('space'), may hold values from 0 to 64, as said below
Outputs:
- outputs: bfloat16 [4, 32, 64, 512], P('dp', 'tm', None, 'space')
- grad_inputs: bfloat16 [4, 32, 64, 512], P('dp', 'tm', None, 'space')
- grad_conv_w: float32 [2, 128, 64], replicated
- grad_conv_b: float32 [128], replicated
- grad_mix_w: float32 [3, 64, 64], replicated
- grad_mix_b: float32 [64], replicated
Inputs may be any that keep to these rules, and one draw needn't show every extreme that they name: counts[s, s] = 0; counts[0, 1] = 64. `tile_cols`: column blocks below 2 are the part's own sensor blocks, 2 + i the i-th block of 128 received slots in order of source part and slot; in each row block the first 4 ids are below 2, the others are not.
All inputs are finite; a program needn't handle non-finite values.
Results may differ from a plain program's by a relative error of at most 0.0058.
Values may be sent and summed in bfloat16 or wider, within the bound.
No kernel may reach another device: no remote copies, remote signals or barrier semaphores. Data moves between devices by JAX's collectives and lax.ppermute only.
A program may use at most 64 MiB of HBM per device.

v0:
```python
import math

import jax
import jax.numpy as jnp
from jax import lax
from jax.sharding import PartitionSpec as P

DILATION_SIZE = 2


def from_behind(value, axis, steps):
    count = lax.axis_size(axis)
    leading, last = (max(0, -steps), min(count, count - steps))
    return lax.ppermute(value, axis, [(source, source + steps) for source in range(leading, last)])


def slot_mask(counts, slot_count, dtype):
    slots = lax.broadcasted_iota(jnp.int32, (counts.shape[1], slot_count), 1)
    return (slots < counts[0][:, None]).astype(dtype)


def pack_rows(field, send_rows, live_slots):
    picked = field[:, :, send_rows[0]] * live_slots
    return picked.reshape(field.shape[0], field.shape[1], -1)


def tile_product(extended, adj_tiles, tile_cols):
    timestep_count, chan_count = (extended.shape[0], extended.shape[1])
    blocks = extended.reshape(timestep_count, chan_count, -1, adj_tiles.shape[2])
    picked = blocks[:, :, tile_cols]
    return jnp.einsum("tcrkj,rkij->tcri", picked, adj_tiles, preferred_element_type=jnp.float32)


def forward_start(field, send_rows, live_slots):
    packed = pack_rows(field, send_rows, live_slots)
    own_part = None
    return (packed, own_part)


def forward_finish(field, received, adj_tiles, tile_cols):
    total = tile_product(jnp.concatenate([field, received], 2), adj_tiles, tile_cols)
    return total.reshape(field.shape).astype(jnp.bfloat16)


def back_start(grad, adj_tiles, tile_cols, send_rows):
    timestep_count, chan_count, sensor_count = grad.shape
    tile_size = adj_tiles.shape[2]
    row_blocks = sensor_count // tile_size
    half_slots = tile_cols.shape[1] // 2
    halo_blocks = send_rows.shape[1] * send_rows.shape[2] // tile_size
    blocks = grad.reshape(timestep_count, chan_count, row_blocks, tile_size)
    remote_terms = jnp.einsum(
        "tcri,rkij->tcrkj", blocks, adj_tiles[:, half_slots:], preferred_element_type=jnp.float32
    )
    remote_sums = jnp.zeros((timestep_count, chan_count, halo_blocks, tile_size), jnp.float32)
    remote_sums = remote_sums.at[:, :, tile_cols[:, half_slots:] - row_blocks].add(remote_terms)
    return remote_sums.reshape(timestep_count, chan_count, -1).astype(jnp.bfloat16)


def back_finish(grad, returned, adj_tiles, tile_cols, send_rows, live_slots):
    timestep_count, chan_count, sensor_count = grad.shape
    tile_size = adj_tiles.shape[2]
    row_blocks = sensor_count // tile_size
    half_slots = tile_cols.shape[1] // 2
    blocks = grad.reshape(timestep_count, chan_count, row_blocks, tile_size)
    own_terms = jnp.einsum(
        "tcri,rkij->tcrkj", blocks, adj_tiles[:, :half_slots], preferred_element_type=jnp.float32
    )
    total = jnp.zeros((timestep_count, chan_count, row_blocks, tile_size), jnp.float32)
    total = total.at[:, :, tile_cols[:, :half_slots]].add(own_terms).reshape(grad.shape)
    returned = returned.reshape(
        timestep_count, chan_count, send_rows.shape[1], send_rows.shape[2]
    ).astype(jnp.float32)
    return total.at[:, :, send_rows[0]].add(returned * live_slots.astype(jnp.float32))


def mixing_grads(sample_grad, fields):
    grad_mix_w = jnp.stack(
        [
            jnp.einsum("ton,tcn->oc", sample_grad, item, preferred_element_type=jnp.float32)
            for item in fields
        ]
    )
    grad_mix_b = jnp.sum(sample_grad.astype(jnp.float32), axis=(0, 2))
    return (grad_mix_w, grad_mix_b)


def body(inputs, grad_out, conv_w, conv_b, mix_w, mix_b, adj_tiles, tile_cols, send_rows, counts):
    sample_input = inputs[0]
    sample_grad = grad_out[0]
    timestep_count, chan_count, sensor_count = sample_input.shape
    live_slots = slot_mask(counts, send_rows.shape[2], jnp.bfloat16)
    prior_border_slice = from_behind(sample_input[timestep_count - DILATION_SIZE :], "tm", 1)
    preceding_window = jnp.concatenate(
        [prior_border_slice, sample_input[: timestep_count - DILATION_SIZE]], 0
    )
    preact = jnp.einsum("oc,tcn->ton", conv_w[1], sample_input, preferred_element_type=jnp.float32)
    preact = preact + jnp.einsum(
        "oc,tcn->ton", conv_w[0], preceding_window, preferred_element_type=jnp.float32
    )
    preact = preact + conv_b[None, :, None]
    filtered = jnp.tanh(preact[:, :chan_count])
    gating = jax.nn.sigmoid(preact[:, chan_count:])
    hidden = (filtered * gating).astype(jnp.bfloat16)
    grad_float = sample_grad.astype(jnp.float32)
    packed_one, early_one = forward_start(hidden, send_rows, live_slots)
    received_one = lax.all_to_all(packed_one, "space", split_axis=2, concat_axis=2, tiled=True)
    hop_one = forward_finish(hidden, received_one, adj_tiles, tile_cols)
    packed_two, early_two = forward_start(hop_one, send_rows, live_slots)
    received_two = lax.all_to_all(packed_two, "space", split_axis=2, concat_axis=2, tiled=True)
    hop_two = forward_finish(hop_one, received_two, adj_tiles, tile_cols)
    fields = (hidden, hop_one, hop_two)
    grad_mix_w, grad_mix_b = mixing_grads(sample_grad, fields)
    back_two = jnp.einsum(
        "oc,ton->tcn", mix_w[2], sample_grad, preferred_element_type=jnp.float32
    ).astype(jnp.bfloat16)
    returned_two = lax.all_to_all(
        back_start(back_two, adj_tiles, tile_cols, send_rows),
        "space",
        split_axis=2,
        concat_axis=2,
        tiled=True,
    )
    back_one = jnp.einsum("oc,ton->tcn", mix_w[1], sample_grad, preferred_element_type=jnp.float32)
    back_one = (
        back_one + back_finish(back_two, returned_two, adj_tiles, tile_cols, send_rows, live_slots)
    ).astype(jnp.bfloat16)
    returned_one = lax.all_to_all(
        back_start(back_one, adj_tiles, tile_cols, send_rows),
        "space",
        split_axis=2,
        concat_axis=2,
        tiled=True,
    )
    back_hidden = jnp.einsum(
        "oc,ton->tcn", mix_w[0], sample_grad, preferred_element_type=jnp.float32
    )
    back_hidden = back_hidden + back_finish(
        back_one, returned_one, adj_tiles, tile_cols, send_rows, live_slots
    )
    mixed = sample_input.astype(jnp.float32) + mix_b[None, :, None]
    for index in range(3):
        mixed = mixed + jnp.einsum(
            "oc,tcn->ton", mix_w[index], fields[index], preferred_element_type=jnp.float32
        )
    outputs = mixed.astype(jnp.bfloat16)[None]
    grad_filter = back_hidden * (1.0 - filtered * filtered) * gating
    grad_gate = back_hidden * filtered * gating * (1.0 - gating)
    backward_preactivation = jnp.concatenate([grad_filter, grad_gate], 1).astype(jnp.bfloat16)
    next_border_slice = from_behind(backward_preactivation[:DILATION_SIZE], "tm", -1)
    following_window = jnp.concatenate(
        [backward_preactivation[DILATION_SIZE:], next_border_slice], 0
    )
    grad_inputs = grad_float + jnp.einsum(
        "oc,ton->tcn", conv_w[1], backward_preactivation, preferred_element_type=jnp.float32
    )
    grad_inputs = grad_inputs + jnp.einsum(
        "oc,ton->tcn", conv_w[0], following_window, preferred_element_type=jnp.float32
    )
    grad_inputs = grad_inputs.astype(jnp.bfloat16)[None]
    grad_conv_w = jnp.stack(
        [
            jnp.einsum(
                "ton,tcn->oc",
                backward_preactivation,
                preceding_window,
                preferred_element_type=jnp.float32,
            ),
            jnp.einsum(
                "ton,tcn->oc",
                backward_preactivation,
                sample_input,
                preferred_element_type=jnp.float32,
            ),
        ]
    )
    grad_conv_b = jnp.sum(backward_preactivation.astype(jnp.float32), axis=(0, 2))
    grad_conv_w, grad_conv_b, grad_mix_w, grad_mix_b = lax.psum(
        (grad_conv_w, grad_conv_b, grad_mix_w, grad_mix_b), ("dp", "space", "tm")
    )
    cell_count = (
        inputs.shape[0]
        * timestep_count
        * sensor_count
        * lax.axis_size("dp")
        * lax.axis_size("space")
        * lax.axis_size("tm")
    )
    scale = 1.0 / math.sqrt(cell_count)
    return (
        outputs,
        grad_inputs,
        grad_conv_w * scale,
        grad_conv_b * scale,
        grad_mix_w * scale,
        grad_mix_b * scale,
    )


def solution(mesh):
    in_specs = (
        P("dp", "tm", None, "space"),
        P("dp", "tm", None, "space"),
        P(),
        P(),
        P(),
        P(),
        P("space", None, None, None),
        P("space", None),
        P("space", None, None),
        P("space", None),
    )
    out_specs = (P("dp", "tm", None, "space"), P("dp", "tm", None, "space"), P(), P(), P(), P())
    return jax.shard_map(body, mesh=mesh, in_specs=in_specs, out_specs=out_specs, check_vma=False)
```

profile of v0, /device:TPU:0, one launch (start us, length us, event | category | flops | bytes accessed | tf_op | source)
XLA Modules:
  0.0 258.4 jit_solution(1451363456639843032)
XLA Ops:
  7.2 1.2 fusion.17
  8.5 1.4 convolution_bitcast_fusion.2
  10.1 0.4 copy-done.13
  10.7 1.8 scatter_fusion.1
  12.8 0.9 reshape.267
  13.7 4.2 %all-to-all-start.2 = ((bf16[2,2,16384]{2,1,0:T(2,128)(2,1)}), bf16[2,2,16384]{2,1,0:T(2,128)(2,1)S(1)}, u32[]{:S(2)}, u32[]{:S(2)}) async-start(bf16[2,2,16384]{2,1,0:T(2,128)(2,1)} %reshape.267), calls=%async_computation.2 | async-start | bytes 262144 | tf_op jit(solution)/shard_map/all_to_all | solution.py:117
  18.0 0.6 slice_bitcast_fusion.1
  18.6 4.7 %collective-permute-start = (bf16[2,64,256]{2,1,0:T(8,128)(2,1)}, bf16[2,64,256]{2,1,0:T(8,128)(2,1)}, u32[]{:S(2)}, u32[]{:S(2)}) collective-permute-start(bf16[2,64,256]{2,1,0:T(8,128)(2,1)} %slice_bitcast_fusion.1), channel_id=1, source_target_pairs={{0,1},{1,2},{2,3},{4,5},{5,6},{6,7},{8,9},{9,10},{10,11},{12,13},{... | collective-permute-start | bytes 196616 | tf_op jit(solution)/shard_map/ppermute | solution.py:14
  23.3 0.4 convolution_bitcast_fusion.3
  23.7 0.7 slice_bitcast_fusion
  24.4 0.6 compare_select_fusion.2
  25.0 0.7 convert_reduce_fusion.1
  26.1 1.9 scatter_fusion
  28.1 1.0 fusion.5
  29.1 0.4 copy.81
  29.7 1.3 fusion.40
  31.0 0.6 pad_clamp_fusion.1
  31.9 0.5 compare_convert_fusion.1
  32.4 0.6 pad_clamp_fusion
  33.4 4.9 %scatter_fusion.2 = f32[8,64,256]{1,0,2:T(8,128)S(1)} fusion(f32[8,64,256]{1,0,2:T(8,128)S(1)} %copy.81, s32[128]{0:T(128)S(1)} %reshape.131, f32[128,8,64]{2,1,0:T(8,128)S(1)} %bitcast.296), kind=kCustom, calls=%fused_computation.6 | custom fusion | flops 65536 | bytes 786944 | tf_op jit(solution)/shard_map/scatter-add | solution.py:74
  38.4 0.3 copy.102
  38.7 0.4 convolution_bitcast_fusion
  39.2 0.4 convolution_bitcast_fusion.1
  39.6 1.5 copy.86
  41.1 3.3 %scatter_fusion.4 = f32[8,64,128,1]{2,1,3,0:T(8,128)S(1)} fusion(f32[8,64,128,1]{2,1,3,0:T(8,128)S(1)} %broadcast.80, s32[8]{0:T(128)S(1)} %reshape.173, f32[8,8,64,128]{3,2,1,0:T(8,128)} %bitcast.289), kind=kCustom, calls=%fused_computation.8 | custom fusion | flops 524288 | bytes 6291488 | tf_op jit(solution)/shard_map/scatter-add | solution.py:56
  44.6 0.9 reshape.269
  45.5 3.4 %all-to-all-start.3 = ((bf16[2,2,16384]{2,1,0:T(2,128)(2,1)}), bf16[2,2,16384]{2,1,0:T(2,128)(2,1)S(1)}, u32[]{:S(2)}, u32[]{:S(2)}) async-start(bf16[2,2,16384]{2,1,0:T(2,128)(2,1)} %reshape.269), calls=%async_computation.3 | async-start | bytes 262144 | tf_op jit(solution)/shard_map/all_to_all | solution.py:128
  49.1 1.5 copy.83
  50.7 3.3 %scatter_fusion.3 = f32[8,64,2,128]{3,1,2,0:T(8,128)S(1)} fusion(f32[8,64,2,128]{3,1,2,0:T(8,128)S(1)} %broadcast.73, s32[8]{0:T(128)S(1)} %reshape.189, f32[8,8,64,128]{3,2,1,0:T(8,128)} %bitcast.288), kind=kCustom, calls=%fused_computation.7 | custom fusion | flops 524288 | bytes 6291488 | tf_op jit(solution)/shard_map/scatter-add | solution.py:70
  54.0 1.3 fusion.1
  55.3 1.0 fusion.6
  56.3 0.4 copy.88
  56.8 0.9 reshape.270
  57.7 1.1 convert_multiply_fusion
  58.8 4.9 %scatter_fusion.5 = f32[8,64,256]{1,0,2:T(8,128)S(1)} fusion(f32[8,64,256]{1,0,2:T(8,128)S(1)} %copy.88, s32[128]{0:T(128)S(1)} %reshape.131, f32[128,8,64]{2,1,0:T(8,128)S(1)} %bitcast.295), kind=kCustom, calls=%fused_computation.9 | custom fusion | flops 65536 | bytes 786944 | tf_op jit(solution)/shard_map/scatter-add | solution.py:74
  63.7 0.4 copy.89
  65.1 0.8 fusion.26
  65.9 1.0 fusion.7
  67.2 1.0 fusion.4
  68.2 1.1 convolution_bitcast_fusion.14
  69.3 0.6 pad_maximum_fusion.5
  70.0 0.8 gather_fusion
  71.0 0.7 fusion.50
  71.7 0.9 reshape.263
  72.6 3.4 %all-to-all-start = ((bf16[2,2,16384]{2,1,0:T(2,128)(2,1)}), bf16[2,2,16384]{2,1,0:T(2,128)(2,1)S(1)}, u32[]{:S(2)}, u32[]{:S(2)}) async-start(bf16[2,2,16384]{2,1,0:T(2,128)(2,1)} %reshape.263), calls=%async_computation | async-start | bytes 262144 | tf_op jit(solution)/shard_map/all_to_all | solution.py:107
  76.0 1.3 collective-permute-start.1
  77.3 0.7 convert_reduce_fusion
  77.9 109.9 %all-reduce.3.cloned.1.call-done = f32[2,128,64]{1,2,0:T(8,128)} async-done(((f32[2,128,64]{1,2,0:T(8,128)}), f32[2,128,64]{1,2,0:T(8,128)}) %all-reduce.3.cloned.1.call-update) | async-done | bytes 65552 | tf_op jit(solution)/shard_map/psum | solution.py:178
  187.8 1.5 broadcast_multiply_fusion.1
  189.8 1.1 gather_fusion.1
  190.9 0.7 fusion.16
  192.0 0.8 gather_fusion.2
  193.0 0.9 reshape.265
  193.9 3.4 %all-to-all-start.1 = ((bf16[2,2,16384]{2,1,0:T(2,128)(2,1)}), bf16[2,2,16384]{2,1,0:T(2,128)(2,1)S(1)}, u32[]{:S(2)}, u32[]{:S(2)}) async-start(bf16[2,2,16384]{2,1,0:T(2,128)(2,1)} %reshape.265), calls=%async_computation.1 | async-start | bytes 262144 | tf_op jit(solution)/shard_map/all_to_all | solution.py:110
  197.3 1.0 fusion.3
  198.5 3.4 %all-to-all-done.1 = bf16[2,2,16384]{2,1,0:T(2,128)(2,1)S(1)} async-done(((bf16[2,2,16384]{2,1,0:T(2,128)(2,1)}), bf16[2,2,16384]{2,1,0:T(2,128)(2,1)S(1)}, u32[]{:S(2)}, u32[]{:S(2)}) %all-to-all-start.1) | async-done | bytes 131104 | tf_op jit(solution)/shard_map/all_to_all | solution.py:110
  202.4 1.1 gather_fusion.3
  203.5 0.7 fusion.15
  204.5 41.5 %all-reduce = (f32[128]{0:T(128)S(1)}, f32[3,64,64]{1,2,0:T(8,128)S(1)}, f32[64]{0:T(128)S(1)}) all-reduce(f32[128]{0:T(128)S(1)} %copy-done.17, f32[3,64,64]{1,2,0:T(8,128)S(1)} %pad_maximum_fusion.4, f32[64]{0:T(128)S(1)} %copy-done.14), channel_id=1, replica_groups=mesh['dp'=4,'space'=2,'tm'=4] {'dp','space','tm'}, use_global_device_ids=true, to_apply=%region_8.0 | all-reduce | flops 12480 | bytes 99840 | tf_op jit(solution)/shard_map/psum | solution.py:178
  246.0 0.7 copy.91
  246.7 0.5 broadcast_multiply_fusion.2
  247.2 0.5 broadcast_multiply_fusion.3
  247.7 2.0 fusion.14
  249.7 1.8 fusion.13
  (98 shorter events, 5.9 us)
Async XLA Ops:
  9.8 0.7 copy-start.13
  10.7 7.2 %copy-start.3 = (bf16[1,8,64,256]{3,2,1,0:T(8,128)(2,1)S(1)}, bf16[1,8,64,256]{3,2,1,0:T(8,128)(2,1)}, u32[]{:S(2)}) copy-start(bf16[1,8,64,256]{3,2,1,0:T(8,128)(2,1)} %param.10) | copy-start | bytes 786436
  10.7 12.6 %copy-start.1 = (bf16[2,8,128,128]{3,2,1,0:T(8,128)(2,1)S(1)}, bf16[2,8,128,128]{3,2,1,0:T(8,128)(2,1)}, u32[]{:S(2)}) copy-start(bf16[2,8,128,128]{3,2,1,0:T(8,128)(2,1)} %param.16) | copy-start | bytes 1572868
  12.6 12.4 %copy-start = (bf16[1,8,64,256]{3,2,1,0:T(8,128)(2,1)S(1)}, bf16[1,8,64,256]{3,2,1,0:T(8,128)(2,1)}, u32[]{:S(2)}) copy-start(bf16[1,8,64,256]{3,2,1,0:T(8,128)(2,1)} %param.11) | copy-start | bytes 786436
  12.8 12.9 %copy-start.22 = (s32[1,2]{1,0:T(1,128)S(1)}, s32[1,2]{1,0:T(1,128)}, u32[]{:S(2)}) copy-start(s32[1,2]{1,0:T(1,128)} %param.19) | copy-start | bytes 28
  13.7 19.3 %all-to-all-start.2 = ((bf16[2,2,16384]{2,1,0:T(2,128)(2,1)}), bf16[2,2,16384]{2,1,0:T(2,128)(2,1)S(1)}, u32[]{:S(2)}, u32[]{:S(2)}) async-start(bf16[2,2,16384]{2,1,0:T(2,128)(2,1)} %reshape.267), calls=%async_computation.2 | async-start | bytes 262144 | tf_op jit(solution)/shard_map/all_to_all | solution.py:117
  18.6 35.4 %collective-permute-start = (bf16[2,64,256]{2,1,0:T(8,128)(2,1)}, bf16[2,64,256]{2,1,0:T(8,128)(2,1)}, u32[]{:S(2)}, u32[]{:S(2)}) collective-permute-start(bf16[2,64,256]{2,1,0:T(8,128)(2,1)} %slice_bitcast_fusion.1), channel_id=1, source_target_pairs={{0,1},{1,2},{2,3},{4,5},{5,6},{6,7},{8,9},{9,10},{10,11},{12,13},{... | collective-permute-start | bytes 196616 | tf_op jit(solution)/shard_map/ppermute | solution.py:14
  28.0 1.5 copy-start.18
  28.0 1.6 copy-start.4
  28.1 1.6 copy-start.11
  28.1 3.5 %copy-start.23 = (s32[1,2]{1,0:T(1,128)S(1)}, s32[1,2]{1,0:T(1,128)}, u32[]{:S(2)}) copy-start(s32[1,2]{1,0:T(1,128)} %param.19) | copy-start | bytes 28
  28.1 3.7 %copy-start.19 = (s32[2,8]{1,0:T(2,128)S(1)}, s32[2,8]{1,0:T(2,128)}, u32[]{:S(2)}) copy-start(s32[2,8]{1,0:T(2,128)} %compare_select_fusion.2) | copy-start | bytes 196
  45.5 11.3 %all-to-all-start.3 = ((bf16[2,2,16384]{2,1,0:T(2,128)(2,1)}), bf16[2,2,16384]{2,1,0:T(2,128)(2,1)S(1)}, u32[]{:S(2)}, u32[]{:S(2)}) async-start(bf16[2,2,16384]{2,1,0:T(2,128)(2,1)} %reshape.269), calls=%async_computation.3 | async-start | bytes 262144 | tf_op jit(solution)/shard_map/all_to_all | solution.py:128
  48.9 138.9 %all-reduce.3.cloned.1.call-start = ((), (), s32[]{:S(2)}) async-start(), calls=%async_computation.4 | async-start | bytes 131072 | tf_op jit(solution)/shard_map/psum | solution.py:178
  50.6 3.4 %copy-start.2 = (f32[8,256,128]{1,2,0:T(8,128)S(1)}, f32[8,256,128]{1,2,0:T(8,128)}, u32[]{:S(2)}) copy-start(f32[8,256,128]{1,2,0:T(8,128)} %fusion.40) | copy-start | bytes 3145732
  50.6 3.4 %copy-start.21 = (f32[128]{0:T(128)S(1)}, f32[128]{0:T(128)}, u32[]{:S(2)}) copy-start(f32[128]{0:T(128)} %param.13) | copy-start | bytes 1540
  64.1 1.7 copy-start.12
  64.5 2.4 copy-start.5
  64.8 2.4 copy-start.10
  64.8 2.4 copy-start.20
  65.0 3.1 %copy-start.9 = (bf16[6,64,256]{2,1,0:T(8,128)(2,1)S(1)}, bf16[6,64,256]{2,1,0:T(8,128)(2,1)}, u32[]{:S(2)}) copy-start(bf16[6,64,256]{2,1,0:T(8,128)(2,1)} %slice_bitcast_fusion) | copy-start | bytes 589828
  66.9 3.9 %copy-start.15 = (bf16[128]{0:T(256)(128)(2,1)S(1)}, bf16[128]{0:T(256)(128)(2,1)}, u32[]{:S(2)}) copy-start(bf16[128]{0:T(256)(128)(2,1)} %compare_convert_fusion.1) | copy-start | bytes 772
  72.6 116.7 %all-to-all-start = ((bf16[2,2,16384]{2,1,0:T(2,128)(2,1)}), bf16[2,2,16384]{2,1,0:T(2,128)(2,1)S(1)}, u32[]{:S(2)}, u32[]{:S(2)}) async-start(bf16[2,2,16384]{2,1,0:T(2,128)(2,1)} %reshape.263), calls=%async_computation | async-start | bytes 262144 | tf_op jit(solution)/shard_map/all_to_all | solution.py:107
  76.0 173.7 %collective-permute-start.1 = (bf16[2,128,256]{2,1,0:T(8,128)(2,1)}, bf16[2,128,256]{2,1,0:T(8,128)(2,1)}, u32[]{:S(2)}, u32[]{:S(2)}) collective-permute-start(bf16[2,128,256]{2,1,0:T(8,128)(2,1)} %fusion.50), channel_id=1, source_target_pairs={{1,0},{2,1},{3,2},{5,4},{6,5},{7,6},{9,8},{10,9},{11,10},{13,12},{... | collective-permute-start | bytes 393224 | tf_op jit(solution)/shard_map/ppermute | solution.py:14
  190.9 1.9 copy-start.16
  191.6 5.7 %copy-start.7 = (f32[8,64,256]{2,1,0:T(8,128)S(1)}, f32[8,64,256]{2,1,0:T(8,128)}, u32[]{:S(2)}) copy-start(f32[8,64,256]{2,1,0:T(8,128)} %fusion.4) | copy-start | bytes 1572868
  193.9 8.0 %all-to-all-start.1 = ((bf16[2,2,16384]{2,1,0:T(2,128)(2,1)}), bf16[2,2,16384]{2,1,0:T(2,128)(2,1)S(1)}, u32[]{:S(2)}, u32[]{:S(2)}) async-start(bf16[2,2,16384]{2,1,0:T(2,128)(2,1)} %reshape.265), calls=%async_computation.1 | async-start | bytes 262144 | tf_op jit(solution)/shard_map/all_to_all | solution.py:110
  203.5 1.0 copy-start.14
  203.5 1.0 copy-start.17
  204.2 45.5 %copy-start.6 = (f32[8,64,256]{2,1,0:T(8,128)S(1)}, f32[8,64,256]{2,1,0:T(8,128)}, u32[]{:S(2)}) copy-start(f32[8,64,256]{2,1,0:T(8,128)} %fusion.7) | copy-start | bytes 1572868
  204.2 45.5 %copy-start.8 = (bf16[6,128,256]{2,1,0:T(8,128)(2,1)S(1)}, bf16[6,128,256]{2,1,0:T(8,128)(2,1)}, u32[]{:S(2)}) copy-start(bf16[6,128,256]{2,1,0:T(8,128)(2,1)} %fusion.26) | copy-start | bytes 1179652
Sparse Core Ops, SparseCore 0:
  70.1 117.6 all-reduce.2
where the time goes:
time: 259 us; the launch traced here: 258 us
  waiting for transfers between devices  113 us (44%)
  blocking collectives  41.5 us (16%)
  other arithmetic  30.8 us (12%)
  starting transfers between devices  20.6 us (8%)
  local copies, waits for them, and re-layouts  18.8 us (7%)
  matrix products  18.7 us (7%)
  between operations  14.8 us (6%)
    psum x1, waiting for transfers between devices, body(): lax.psum((grad_conv_w, grad_conv_b, grad_mix_w, grad_mix_b), ('dp', 'spac...  110 us
    psum x1, blocking collectives, body(): lax.psum((grad_conv_w, grad_conv_b, grad_mix_w, grad_mix_b), ('dp', 'spac...  41.5 us
    scatter-add x2, other arithmetic, back_finish(): total.at[:, :, send_rows[0]].add(returned * live_slots.astype(jnp.float32))  9.81 us
    unnamed x58, local copies, waits for them, and re-layouts  6.56 us
    ppermute x2, starting transfers between devices, from_behind(): lax.ppermute(value, axis, [(source, source + steps) for source in range(l...  5.99 us
    scatter-add x2, other arithmetic, back_finish(): total.at[:, :, tile_cols[:, :half_slots]].add(own_terms).reshape(grad.shape)  5.21 us
  transfers between devices with their start and end apart: 7, of which 2 were waited for; matrix products, arithmetic and copies ran while one was open for 18% of the time, Pallas kernels for 0%

commit v1 on v0

--- a/solution.py
+++ b/solution.py
@@ -1,8 +1,11 @@
+import functools
 import math
 
 import jax
 import jax.numpy as jnp
 from jax import lax
+from jax.experimental import pallas as pl
+from jax.experimental.pallas import tpu as pltpu
 from jax.sharding import PartitionSpec as P
 
 DILATION_SIZE = 2
@@ -85,7 +88,7 @@
     return (grad_mix_w, grad_mix_b)
 
 
-def body(inputs, grad_out, conv_w, conv_b, mix_w, mix_b, adj_tiles, tile_cols, send_rows, counts):
+def general_body(inputs, grad_out, conv_w, conv_b, mix_w, mix_b, adj_tiles, tile_cols, send_rows, counts):
     sample_input = inputs[0]
     sample_grad = grad_out[0]
     timestep_count, chan_count, sensor_count = sample_input.shape
@@ -197,6 +200,410 @@
     )
 
 
+BF16 = jnp.bfloat16
+F32 = jnp.float32
+NT = (((1,), (1,)), ((), ()))
+VMEM_BYTES = 24 * 1024 * 1024
+
+
+def mm(left, right):
+    return jnp.dot(left, right, preferred_element_type=F32)
+
+
+def mm_nt(left, right):
+    return lax.dot_general(left, right, NT, preferred_element_type=F32)
+
+
+def lane_half(rows, width):
+    lanes = lax.broadcasted_iota(jnp.int32, (rows, width), 1)
+    return (lanes >= width // 2).astype(jnp.int32)
+
+
+def slot_matrix(rows_ref, counts_ref, other, sensor_count):
+    slot_count = rows_ref.shape[2]
+    rows = rows_ref[0, pl.ds(other, 1), :]
+    rows = jnp.concatenate([rows, rows], 1)
+    lanes = lax.broadcasted_iota(jnp.int32, (1, 2 * slot_count), 1)
+    slots = lanes - jnp.where(lanes >= slot_count, slot_count, 0)
+    rows = jnp.where(slots < counts_ref[0, other], rows, -1)
+    sensors = lax.broadcasted_iota(jnp.int32, (sensor_count, 2 * slot_count), 0)
+    return jnp.where(sensors == rows, 1.0, 0.0).astype(F32)
+
+
+def keep_half(matrix, half):
+    return jnp.where(lane_half(*matrix.shape) == half, matrix, jnp.zeros_like(matrix))
+
+
+def link_matrix(packed_ref, field_rows, other):
+    small = packed_ref[field_rows:, :]
+    blank = jnp.zeros_like(small)
+    return jnp.concatenate(
+        [jnp.where(other == 0, small, blank), jnp.where(other == 1, small, blank)], 0
+    )
+
+
+def column(row):
+    size = row.shape[1]
+    first = lax.broadcasted_iota(jnp.int32, (size, size), 0)
+    second = lax.broadcasted_iota(jnp.int32, (size, size), 1)
+    return jnp.sum(jnp.where(first == second, row, 0.0), axis=1, keepdims=True)
+
+
+def prepare_kernel(cols_ref, counts_ref, rows_ref, adj_ref, grad_ref, packed_ref, own_ref, halo_ref):
+    me = lax.axis_index("space")
+    other = 1 - me
+    row_blocks, slots, tile = adj_ref.shape[0], adj_ref.shape[1], adj_ref.shape[2]
+    own_slots = slots // 2
+    field_rows = grad_ref.shape[0]
+    for r in range(row_blocks):
+        at = slice(r * tile, (r + 1) * tile)
+        sums = [jnp.zeros((tile, tile), F32), jnp.zeros((tile, tile), F32)]
+        for k in range(own_slots):
+            item = adj_ref[r, k].astype(F32)
+            for block in range(2):
+                share = jnp.where(cols_ref[r, k] == block, 1.0, 0.0).astype(F32)
+                sums[block] = sums[block] + item * share
+        own_ref[at, :] = jnp.concatenate(sums, 1).astype(BF16)
+        far = adj_ref[r, own_slots].astype(F32)
+        for k in range(own_slots + 1, slots):
+            far = far + adj_ref[r, k].astype(F32)
+        far = jnp.where(lane_half(tile, tile) == other, far, pltpu.roll(far, tile // 2, 1))
+        halo_ref[at, :] = far.astype(BF16)
+    own = own_ref[...]
+    halo = halo_ref[...]
+    halo_other = keep_half(halo, other)
+    halo_mine = keep_half(halo, me)
+    grad = grad_ref[...]
+    first = mm(grad, own).astype(BF16)
+    packed_ref[:field_rows, :] = (mm(grad, halo_other) + mm(first, halo_mine)).astype(BF16)
+    chosen = slot_matrix(rows_ref, counts_ref, other, own.shape[0])
+    chosen = jnp.transpose(chosen)[: chosen.shape[1] // 2].astype(BF16)
+    packed_ref[field_rows:, :] = mm(chosen, halo_mine).astype(BF16)
+
+
+def main_kernel(
+    counts_ref,
+    rows_ref,
+    input_ref,
+    border_ref,
+    grad_ref,
+    own_packed_ref,
+    packed_ref,
+    own_ref,
+    halo_ref,
+    conv_w_ref,
+    conv_b_ref,
+    mix_w_ref,
+    kept_ref,
+    given_ref,
+    boundary_ref,
+    hidden_ref,
+    back_ref,
+    border_out_ref,
+    left_scr,
+    right_scr,
+    one_scr,
+    two_scr,
+):
+    me = lax.axis_index("space")
+    other = 1 - me
+    core = lax.axis_index("dp") % 2
+    steps, chans, sensors = input_ref.shape
+    field_rows = steps * chans
+    own = own_ref[...]
+    halo = halo_ref[...]
+    chosen = slot_matrix(rows_ref, counts_ref, other, sensors).astype(BF16)
+    chosen_mine = keep_half(chosen, me)
+    chosen_other = keep_half(chosen, other)
+    link = link_matrix(packed_ref, field_rows, other)
+    packed = packed_ref[:field_rows, :]
+    grad = grad_ref[...]
+    one = (mm(grad, own) + mm_nt(packed, chosen_mine)).astype(BF16)
+    back = (packed.astype(F32) + mm(own_packed_ref[:field_rows, :], link)).astype(BF16)
+    two = (mm(one, own) + mm_nt(back, chosen_other)).astype(BF16)
+    one_scr[...] = one
+    two_scr[...] = two
+    taps = jnp.concatenate([conv_w_ref[0], conv_w_ref[1]], 1)
+    bias = column(conv_b_ref[...])
+    mixing = jnp.transpose(mix_w_ref[...].reshape(3 * chans, chans).astype(F32)).astype(BF16)
+    ones = jnp.ones((chans, sensors), BF16)
+    for t in range(steps):
+        at = slice(t * chans, (t + 1) * chans)
+        earlier = border_ref[t] if t < DILATION_SIZE else input_ref[t - DILATION_SIZE]
+        window = jnp.concatenate([earlier, input_ref[t]], 0)
+        preact = mm(taps, window) + bias
+        filtered = jnp.tanh(preact[:chans])
+        gating = 0.5 * jnp.tanh(0.5 * preact[chans:]) + 0.5
+        hidden = (filtered * gating).astype(BF16)
+        hidden_ref[at, :] = hidden
+        fields = jnp.concatenate([grad_ref[at, :], one_scr[at, :], two_scr[at, :]], 0)
+        back_hidden = mm(mixing, fields)
+        back_pre = jnp.concatenate(
+            [
+                back_hidden * (1.0 - filtered * filtered) * gating,
+                back_hidden * filtered * gating * (1.0 - gating),
+            ],
+            0,
+        ).astype(BF16)
+        back_ref[t] = back_pre
+        if t < DILATION_SIZE:
+            border_out_ref[t] = back_pre
+        span = slice(t * sensors, (t + 1) * sensors)
+        left_scr[: 2 * chans, span] = back_pre
+        left_scr[2 * chans :, span] = fields
+        right_scr[: 2 * chans, span] = window
+        right_scr[2 * chans :, span] = jnp.concatenate([hidden, ones], 0)
+    hidden_all = hidden_ref[...]
+    hop = mm_nt(hidden_all, own).astype(BF16)
+    boundary_ref[...] = (mm(hidden_all, chosen_other) + mm(hop, chosen_mine)).astype(BF16)
+    sums = mm_nt(left_scr[...], right_scr[...])
+    conv = sums[: 2 * chans, : 2 * chans]
+    wide = 2 * chans
+    zero, first, second = [
+        sums[wide + k * chans : wide + (k + 1) * chans, wide:] for k in range(3)
+    ]
+    lanes = lax.broadcasted_iota(jnp.int32, (chans, wide), 1)
+    top = jnp.where(lanes < chans, zero, pltpu.roll(first, chans, 1))
+    bottom = jnp.where(lanes < chans, second, zero)
+    bottom = jnp.where(lanes >= chans + chans // 4, sums[:chans, wide:], bottom)
+    bottom = jnp.where(lanes >= chans + chans // 2, sums[chans:wide, wide:], bottom)
+    mixes = jnp.concatenate([top, bottom], 0)
+    kept_ref[...] = jnp.where(core == 0, conv, mixes)
+    given_ref[...] = jnp.where(core == 0, mixes, conv)
+
+
+def outputs_kernel(
+    input_ref,
+    hidden_ref,
+    own_boundary_ref,
+    boundary_ref,
+    packed_ref,
+    own_ref,
+    halo_ref,
+    mix_w_ref,
+    mix_b_ref,
+    out_ref,
+):
+    me = lax.axis_index("space")
+    other = 1 - me
+    steps, chans, sensors = input_ref.shape
+    own = own_ref[...]
+    halo = halo_ref[...]
+    link = link_matrix(packed_ref, steps * chans, other)
+    boundary = boundary_ref[...]
+    hidden = hidden_ref[...]
+    one = (mm_nt(hidden, own) + mm_nt(boundary, keep_half(halo, me))).astype(BF16)
+    far = (boundary.astype(F32) + mm_nt(own_boundary_ref[...], link)).astype(BF16)
+    two = (mm_nt(one, own) + mm_nt(far, keep_half(halo, other))).astype(BF16)
+    bias = column(mix_b_ref[...])
+    for t in range(steps):
+        at = slice(t * chans, (t + 1) * chans)
+        mixed = mm(mix_w_ref[0], hidden[at]) + mm(mix_w_ref[1], one[at]) + mm(mix_w_ref[2], two[at])
+        out_ref[t] = (mixed + bias + input_ref[t].astype(F32)).astype(BF16)
+
+
+def input_grad_kernel(grad_ref, back_ref, border_ref, conv_w_ref, out_ref):
+    steps, chans, sensors = grad_ref.shape
+    taps = conv_w_ref[...].reshape(4 * chans, chans).astype(F32)
+    taps = jnp.transpose(taps).astype(BF16)
+    for t in range(steps):
+        later = t + DILATION_SIZE
+        following = back_ref[later] if later < steps else border_ref[later - steps]
+        both = jnp.concatenate([following, back_ref[t]], 0)
+        out_ref[t] = (mm(taps, both) + grad_ref[t].astype(F32)).astype(BF16)
+
+
+def final_kernel(scale, kept_ref, other_ref, conv_w_ref, conv_b_ref, mix_w_ref, mix_b_ref):
+    core = lax.axis_index("dp") % 2
+    kept = kept_ref[...] * scale
+    other = other_ref[...] * scale
+    conv = jnp.where(core == 0, kept, other)
+    mixes = jnp.where(core == 0, other, kept)
+    chans = conv.shape[1] // 2
+    conv_w_ref[0] = conv[:, :chans]
+    conv_w_ref[1] = pltpu.roll(conv, chans, 1)[:, :chans]
+    mix_w_ref[0] = mixes[:chans, :chans]
+    mix_w_ref[1] = pltpu.roll(mixes[:chans], chans, 1)[:, :chans]
+    mix_w_ref[2] = mixes[chans:, :chans]
+    turned = jnp.transpose(mixes)
+    mix_b_ref[...] = turned[chans : chans + 1, chans:]
+    half, quarter = chans + chans // 2, chans + chans // 4
+    conv_b_ref[...] = jnp.concatenate(
+        [turned[quarter : quarter + 1, chans:], turned[half : half + 1, chans:]], 1
+    )
+
+
+VMEM = pl.BlockSpec(memory_space=pltpu.VMEM)
+SMEM = pl.BlockSpec(memory_space=pltpu.SMEM)
+
+
+def call(kernel, name, in_specs, out_shape, args, scratch=(), flops=0, moved=0):
+    return pl.pallas_call(
+        kernel,
+        out_shape=out_shape,
+        in_specs=in_specs,
+        out_specs=jax.tree.map(lambda _: VMEM, out_shape),
+        scratch_shapes=list(scratch),
+        compiler_params=pltpu.CompilerParams(vmem_limit_bytes=VMEM_BYTES),
+        cost_estimate=pl.CostEstimate(flops=flops, bytes_accessed=moved, transcendentals=0),
+        name=name,
+    )(*args)
+
+
+def swap(value, axis, bit):
+    count = lax.axis_size(axis)
+    return lax.ppermute(value, axis, [(source, source ^ bit) for source in range(count)])
+
+
+def bits(count):
+    return [1 << place for place in range(count.bit_length() - 1)]
+
+
+def pair_body(inputs, grad_out, conv_w, conv_b, mix_w, mix_b, adj_tiles, tile_cols, send_rows, counts):
+    sample_input = inputs[0]
+    sample_grad = grad_out[0]
+    steps, chans, sensors = sample_input.shape
+    field_rows = steps * chans
+    wide = 2 * chans
+    shape = jax.ShapeDtypeStruct
+    grad_flat = sample_grad.reshape(field_rows, sensors)
+    packed, own, halo = call(
+        prepare_kernel,
+        "prepare",
+        [SMEM, SMEM, VMEM, VMEM, VMEM],
+        (
+            shape((field_rows + chans, wide), BF16),
+            shape((sensors, sensors), BF16),
+            shape((sensors, wide), BF16),
+        ),
+        (tile_cols, counts, send_rows, adj_tiles, grad_flat),
+    )
+    border = from_behind(sample_input[steps - DILATION_SIZE :], "tm", 1)
+    packed_far = swap(packed, "space", 1)
+    kept, given, boundary, hidden, back, back_border = call(
+        main_kernel,
+        "main",
+        [SMEM] + [VMEM] * 11,
+        (
+            shape((wide, wide), F32),
+            shape((wide, wide), F32),
+            shape((field_rows, wide), BF16),
+            shape((field_rows, sensors), BF16),
+            shape((steps, wide, sensors), BF16),
+            shape((DILATION_SIZE, wide, sensors), BF16),
+        ),
+        (
+            counts,
+            send_rows,
+            sample_input,
+            border,
+            grad_flat,
+            packed,
+            packed_far,
+            own,
+            halo,
+            conv_w,
+            conv_b.reshape(1, wide),
+            mix_w,
+        ),
+        scratch=(
+            pltpu.VMEM((5 * chans, steps * sensors), BF16),
+            pltpu.VMEM((4 * chans, steps * sensors), BF16),
+            pltpu.VMEM((field_rows, sensors), BF16),
+            pltpu.VMEM((field_rows, sensors), BF16),
+        ),
+    )
+    total = kept + swap(given, "dp", 1)
+    boundary_far = swap(boundary, "space", 1)
+    back_border_far = from_behind(back_border, "tm", -1)
+    for axis, bit in (
+        [("dp", bit) for bit in bits(lax.axis_size("dp"))[1:]]
+        + [("space", bit) for bit in bits(lax.axis_size("space"))]
+        + [("tm", bit) for bit in bits(lax.axis_size("tm"))]
+    ):
+        total = total + swap(total, axis, bit)
+    total_far = swap(total, "dp", 1)
+    outputs = call(
+        outputs_kernel,
+        "outputs",
+        [VMEM] * 9,
+        shape(sample_input.shape, BF16),
+        (
+            sample_input,
+            hidden,
+            boundary,
+            boundary_far,
+            packed_far,
+            own,
+            halo,
+            mix_w,
+            mix_b.reshape(1, chans),
+        ),
+        flops=2 * field_rows * sensors * 1000,
+        moved=8 * field_rows * sensors,
+    )
+    grad_inputs = call(
+        input_grad_kernel,
+        "input_grad",
+        [VMEM] * 4,
+        shape(sample_grad.shape, BF16),
+        (sample_grad, back, back_border_far, conv_w),
+        flops=2 * field_rows * sensors * 256,
+        moved=8 * field_rows * sensors,
+    )
+    cell_count = (
+        inputs.shape[0]
+        * steps
+        * sensors
+        * lax.axis_size("dp")
+        * lax.axis_size("space")
+        * lax.axis_size("tm")
+    )
+    scale = 1.0 / math.sqrt(cell_count)
+    grad_conv_w, grad_conv_b, grad_mix_w, grad_mix_b = call(
+        functools.partial(final_kernel, scale),
+        "final",
+        [VMEM] * 2,
+        (
+            shape((2, wide, chans), F32),
+            shape((1, wide), F32),
+            shape((3, chans, chans), F32),
+            shape((1, chans), F32),
+        ),
+        (total, total_far),
+    )
+    return (
+        outputs[None],
+        grad_inputs[None],
+        grad_conv_w,
+        grad_conv_b.reshape(wide),
+        grad_mix_w,
+        grad_mix_b.reshape(chans),
+    )
+
+
+def power_of_two(count):
+    return count & (count - 1) == 0
+
+
+def body(inputs, grad_out, conv_w, conv_b, mix_w, mix_b, adj_tiles, tile_cols, send_rows, counts):
+    tile = adj_tiles.shape[2]
+    axes = [lax.axis_size(axis) for axis in ("dp", "space", "tm")]
+    fits = (
+        axes[1] == 2
+        and axes[0] % 2 == 0
+        and all(power_of_two(count) for count in axes)
+        and inputs.shape[0] == 1
+        and inputs.shape[3] == 2 * tile
+        and inputs.shape[2] * 2 == tile
+        and send_rows.shape[2] * 2 == tile
+    )
+    chosen = pair_body if fits else general_body
+    return chosen(
+        inputs, grad_out, conv_w, conv_b, mix_w, mix_b, adj_tiles, tile_cols, send_rows, counts
+    )
+
+
 def solution(mesh):
     in_specs = (
         P("dp", "tm", None, "space"),

time: 259 us -> 43.4 us (0.17)
  waiting for transfers between devices: 113 us -> 13 us
  blocking collectives: 41.5 us -> 0 us
  other arithmetic: 30.8 us -> 0.05 us
  matrix products: 18.7 us -> 0 us
  between operations: 14.8 us -> 0.77 us
  local copies, waits for them, and re-layouts: 18.8 us -> 5.51 us
  Pallas kernels: 0 us -> 7.01 us
  starting transfers between devices: 20.6 us -> 16.6 us
    psum x1 -> x0, waiting for transfers between devices: 110 us -> none  [body(): lax.psum((grad_conv_w, grad_conv_b, grad_mix_w, grad_mix_b), ('dp', 'spac...]
    psum x1 -> x0, blocking collectives: 41.5 us -> none  [body(): lax.psum((grad_conv_w, grad_conv_b, grad_mix_w, grad_mix_b), ('dp', 'spac...]
    scatter-add x6 -> x0, other arithmetic: 20.1 us -> none  [the longest x2 9.81 us: back_finish(): total.at[:, :, send_rows[0]].add(returned * live_slots.astype(jnp.float32))]
    dot_general x21 -> x0, matrix products: 18.7 us -> none  [the longest x3 3.95 us: body(): jnp.einsum('oc,tcn->ton', mix_w[index], fields[index], preferred_element_...]
    all_to_all x4 -> x0, starting transfers between devices: 14.4 us -> none  [the longest x1 4.23 us: body(): lax.all_to_all(back_start(back_two, adj_tiles, tile_cols, send_rows), 'sp...]
    ppermute x0 -> x8, starting transfers between devices: none -> 11.8 us  [swap(): lax.ppermute(value, axis, [(source, source ^ bit) for source in range(cou...]
    ppermute x0 -> x8, waiting for transfers between devices: none -> 11.3 us  [swap(): lax.ppermute(value, axis, [(source, source ^ bit) for source in range(cou...]
    pallas_call x0 -> x5, Pallas kernels: none -> 7.01 us  [call(): pl.pallas_call(kernel, out_shape=out_shape, in_specs=in_specs, out_specs=...]
  transfers between devices with their start and end apart: 7 -> 10, of which waited for: 2 -> 6; matrix products, arithmetic and copies ran while one was open for 18% -> 0% of each run, Pallas kernels for 0% -> 6%
where the time goes in v1:
time: 43.4 us; the launch traced here: 43 us
  starting transfers between devices  16.6 us (38%)
  waiting for transfers between devices  13 us (30%)
  Pallas kernels  7.01 us (16%)
  local copies, waits for them, and re-layouts  5.51 us (13%)
  between operations  0.77 us (2%)
    ppermute x8, starting transfers between devices, swap(): lax.ppermute(value, axis, [(source, source ^ bit) for source in range(cou...  11.8 us
    ppermute x8, waiting for transfers between devices, swap(): lax.ppermute(value, axis, [(source, source ^ bit) for source in range(cou...  11.3 us
    pallas_call x5, Pallas kernels, call(): pl.pallas_call(kernel, out_shape=out_shape, in_specs=in_specs, out_specs=...  7.01 us
    unnamed x24, local copies, waits for them, and re-layouts  5.5 us
    ppermute x2, starting transfers between devices, from_behind(): lax.ppermute(value, axis, [(source, source + steps) for source in range(l...  4.9 us
    ppermute x2, waiting for transfers between devices, from_behind(): lax.ppermute(value, axis, [(source, source + steps) for source in range(l...  1.75 us
  transfers between devices with their start and end apart: 10, of which 6 were waited for; matrix products, arithmetic and copies ran while one was open for 0% of the time, Pallas kernels for 6%

profile of v1, /device:TPU:0, one launch (start us, length us, event | category | flops | bytes accessed | tf_op | source)
XLA Modules:
  0.0 43.0 jit_solution(7634688281964404095)
XLA Ops:
  0.6 0.0 copy-start.6
  0.6 0.0 copy-start.5
  0.7 0.6 %copy-done.6 = s32[1,2]{1,0:T(1,128)S(1)} copy-done((s32[1,2]{1,0:T(1,128)S(1)}, s32[1,2]{1,0:T(1,128)}, u32[]{:S(2)}) %copy-start.6) | copy-done | bytes 32
  1.3 0.0 copy-done.5
  1.3 0.0 copy-start
  1.3 0.9 %copy-done = bf16[1,8,64,256]{3,2,1,0:T(8,128)(2,1)S(1)} copy-done((bf16[1,8,64,256]{3,2,1,0:T(8,128)(2,1)S(1)}, bf16[1,8,64,256]{3,2,1,0:T(8,128)(2,1)}, u32[]{:S(2)}) %copy-start) | copy-done | bytes 262168
  2.3 0.0 copy-start.3
  2.3 1.0 %copy-done.3 = bf16[2,8,128,128]{3,2,1,0:T(8,128)(2,1)S(1)} copy-done((bf16[2,8,128,128]{3,2,1,0:T(8,128)(2,1)S(1)}, bf16[2,8,128,128]{3,2,1,0:T(8,128)(2,1)}, u32[]{:S(2)}) %copy-start.3) | copy-done | bytes 524312
  3.3 0.0 copy-start.7
  3.3 0.7 %copy-done.7 = s32[2,8]{1,0:T(2,128)S(1)} copy-done((s32[2,8]{1,0:T(2,128)S(1)}, s32[2,8]{1,0:T(2,128)}, u32[]{:S(2)}) %copy-start.7) | copy-done | bytes 88
  4.0 0.0 copy-start.2
  4.0 0.0 copy-start.1
  4.0 1.2 %prepare.1 = (bf16[576,128]{1,0:T(8,128)(2,1)S(1)}, bf16[256,256]{1,0:T(8,128)(2,1)S(1)}, bf16[256,128]{1,0:T(8,128)(2,1)S(1)}) custom-call(s32[2,8]{1,0:T(2,128)S(1)} %copy-done.7, s32[1,2]{1,0:T(1,128)S(1)} %copy-done.6, s32[1,2,64]{2,1,0:T(2,128)S(1)} %copy-done.5, bf16[2,8,128,128]{3,2,1,0:T(8,128)(2,1)S(1)} %copy-done.3, bf16[512,256]{1,0:T(8,128)(2,1)S(1)} %bitcast.11), custom_call_target="tpu_custom_call" | custom-call | tf_op jit(solution)/shard_map/prepare/pallas_call | solution.py:441
  5.2 0.0 copy-start.10
  5.2 3.0 %collective-permute-start.1 = (bf16[576,128]{1,0:T(8,128)(2,1)S(1)}, bf16[576,128]{1,0:T(8,128)(2,1)S(1)}, u32[]{:S(2)}, u32[]{:S(2)}) collective-permute-start(bf16[576,128]{1,0:T(8,128)(2,1)S(1)} %get-tuple-element.19.own_packed_ref), channel_id=1, source_target_pairs={{0,4},{4,0},{1,5},{5,1},{2,6},{6,2},{3,7},{7,3},{8,12},{12,8},{9,1... | collective-permute-start | bytes 442376 | tf_op jit(solution)/shard_map/ppermute | solution.py:455
  8.2 0.0 copy-done.2
  8.2 0.0 copy-start.4
  8.2 3.6 %collective-permute-start = (bf16[2,64,256]{2,1,0:T(8,128)(2,1)S(1)}, bf16[2,64,256]{2,1,0:T(8,128)(2,1)S(1)}, u32[]{:S(2)}, u32[]{:S(2)}) collective-permute-start(bf16[2,64,256]{2,1,0:T(8,128)(2,1)S(1)} %slice_bitcast_fusion), channel_id=1, source_target_pairs={{0,1},{1,2},{2,3},{4,5},{5,6},{6,7},{8,9},{9,10},{10,11},{12,13},{... | collective-permute-start | bytes 196616 | tf_op jit(solution)/shard_map/ppermute | solution.py:17
  11.9 0.0 copy-done.10
  11.9 0.1 copy.16.conv_w_ref
  12.0 1.8 %collective-permute-done.border_ref = bf16[2,64,256]{2,1,0:T(8,128)(2,1)S(1)} collective-permute-done((bf16[2,64,256]{2,1,0:T(8,128)(2,1)S(1)}, bf16[2,64,256]{2,1,0:T(8,128)(2,1)S(1)}, u32[]{:S(2)}, u32[]{:S(2)}) %collective-permute-start) | collective-permute-done | bytes 65568 | tf_op jit(solution)/shard_map/ppermute | solution.py:17
  13.7 0.0 collective-permute-done.1.packed_ref
  13.7 0.0 copy-start.8
  13.8 0.0 copy-done.1
  13.8 0.0 copy-done.4
  13.8 0.6 %copy-done.8 = f32[128]{0:T(128)S(1)} copy-done((f32[128]{0:T(128)S(1)}, f32[128]{0:T(128)}, u32[]{:S(2)}) %copy-start.8) | copy-done | bytes 536
  14.4 2.6 %main.1 = (f32[128,128]{1,0:T(8,128)S(1)}, f32[128,128]{1,0:T(8,128)S(1)}, bf16[512,128]{1,0:T(8,128)(2,1)S(1)}, bf16[512,256]{1,0:T(8,128)(2,1)S(1)}, bf16[8,12...) custom-call(s32[1,2]{1,0:T(1,128)S(1)} %copy-done.6, s32[1,2,64]{2,1,0:T(2,128)S(1)} %copy-done.5, ...), custom_call_target="tpu_custom_call" | custom-call | tf_op jit(solution)/shard_map/main/pallas_call | solution.py:441
  17.0 0.1 collective-permute-start.4
  17.1 1.2 %collective-permute-done.4 = f32[128,128]{1,0:T(8,128)S(1)} collective-permute-done((f32[128,128]{1,0:T(8,128)S(1)}, f32[128,128]{1,0:T(8,128)S(1)}, u32[]{:S(2)}, u32[]{:S(2)}) %collective-permute-start.4) | collective-permute-done | bytes 65568 | tf_op jit(solution)/shard_map/ppermute | solution.py:455
  18.3 1.6 %collective-permute-start.5 = (f32[128,128]{1,0:T(8,128)S(1)}, f32[128,128]{1,0:T(8,128)S(1)}, u32[]{:S(2)}, u32[]{:S(2)}) collective-permute-start(f32[128,128]{1,0:T(8,128)S(1)} %add.15), channel_id=1, source_target_pairs={{0,16},{8,24},{16,0},{24,8},{1,17},{9,25},{17,1},{25,9},{2,18},{10... | collective-permute-start | bytes 196616 | tf_op jit(solution)/shard_map/ppermute | solution.py:455
  19.9 2.8 %collective-permute-done.5 = f32[128,128]{1,0:T(8,128)S(1)} collective-permute-done((f32[128,128]{1,0:T(8,128)S(1)}, f32[128,128]{1,0:T(8,128)S(1)}, u32[]{:S(2)}, u32[]{:S(2)}) %collective-permute-start.5) | collective-permute-done | bytes 65568 | tf_op jit(solution)/shard_map/ppermute | solution.py:455
  22.7 0.6 %collective-permute-start.6 = (f32[128,128]{1,0:T(8,128)S(1)}, f32[128,128]{1,0:T(8,128)S(1)}, u32[]{:S(2)}, u32[]{:S(2)}) collective-permute-start(f32[128,128]{1,0:T(8,128)S(1)} %add.16), channel_id=1, source_target_pairs={{0,4},{4,0},{1,5},{5,1},{2,6},{6,2},{3,7},{7,3},{8,12},{12,8},{9,1... | collective-permute-start | bytes 196616 | tf_op jit(solution)/shard_map/ppermute | solution.py:455
  23.2 3.8 %collective-permute-done.6 = f32[128,128]{1,0:T(8,128)S(1)} collective-permute-done((f32[128,128]{1,0:T(8,128)S(1)}, f32[128,128]{1,0:T(8,128)S(1)}, u32[]{:S(2)}, u32[]{:S(2)}) %collective-permute-start.6) | collective-permute-done | bytes 65568 | tf_op jit(solution)/shard_map/ppermute | solution.py:455
  27.0 2.4 %collective-permute-start.7 = (f32[128,128]{1,0:T(8,128)S(1)}, f32[128,128]{1,0:T(8,128)S(1)}, u32[]{:S(2)}, u32[]{:S(2)}) collective-permute-start(f32[128,128]{1,0:T(8,128)S(1)} %add.17), channel_id=1, source_target_pairs={{0,1},{1,0},{2,3},{3,2},{4,5},{5,4},{6,7},{7,6},{8,9},{9,8},{10,11... | collective-permute-start | bytes 196616 | tf_op jit(solution)/shard_map/ppermute | solution.py:455
  29.4 1.3 %collective-permute-start.3 = (bf16[2,128,256]{2,1,0:T(8,128)(2,1)S(1)}, bf16[2,128,256]{2,1,0:T(8,128)(2,1)S(1)}, u32[]{:S(2)}, u32[]{:S(2)}) collective-permute-start(bf16[2,128,256]{2,1,0:T(8,128)(2,1)S(1)} %get-tuple-element.25), channel_id=1, source_target_pairs={{1,0},{2,1},{3,2},{5,4},{6,5},{7,6},{9,8},{10,9},{11,10},{13,12},{... | collective-permute-start | bytes 393224 | tf_op jit(solution)/shard_map/ppermute | solution.py:17
  30.7 0.6 %collective-permute-start.2 = (bf16[512,128]{1,0:T(8,128)(2,1)S(1)}, bf16[512,128]{1,0:T(8,128)(2,1)S(1)}, u32[]{:S(2)}, u32[]{:S(2)}) collective-permute-start(bf16[512,128]{1,0:T(8,128)(2,1)S(1)} %get-tuple-element.23.own_boundary_ref), channel_id=1, source_target_pairs={{0,4},{4,0},{1,5},{5,1},{2,6},{6,2},{3,7},{7,3},{8,12},{12,8},{9,1... | collective-permute-start | bytes 393224 | tf_op jit(solution)/shard_map/ppermute | solution.py:455
  31.3 0.6 %collective-permute-done.7 = f32[128,128]{1,0:T(8,128)S(1)} collective-permute-done((f32[128,128]{1,0:T(8,128)S(1)}, f32[128,128]{1,0:T(8,128)S(1)}, u32[]{:S(2)}, u32[]{:S(2)}) %collective-permute-start.7) | collective-permute-done | bytes 65568 | tf_op jit(solution)/shard_map/ppermute | solution.py:455
  31.9 3.5 %collective-permute-start.8 = (f32[128,128]{1,0:T(8,128)S(1)}, f32[128,128]{1,0:T(8,128)S(1)}, u32[]{:S(2)}, u32[]{:S(2)}) collective-permute-start(f32[128,128]{1,0:T(8,128)S(1)} %add.18), channel_id=1, source_target_pairs={{0,2},{1,3},{2,0},{3,1},{4,6},{5,7},{6,4},{7,5},{8,10},{9,11},{10,... | collective-permute-start | bytes 196616 | tf_op jit(solution)/shard_map/ppermute | solution.py:455
  35.4 2.9 %collective-permute-done.8 = f32[128,128]{1,0:T(8,128)S(1)} collective-permute-done((f32[128,128]{1,0:T(8,128)S(1)}, f32[128,128]{1,0:T(8,128)S(1)}, u32[]{:S(2)}, u32[]{:S(2)}) %collective-permute-start.8) | collective-permute-done | bytes 65568 | tf_op jit(solution)/shard_map/ppermute | solution.py:455
  38.3 0.1 collective-permute-start.9
  38.4 0.0 collective-permute-done.3.border_ref
  38.4 1.0 %input_grad.1 = bf16[8,64,256]{2,1,0:T(8,128)(2,1)} custom-call(bf16[8,64,256]{2,1,0:T(8,128)(2,1)S(1)} %bitcast.13, bf16[8,128,256]{2,1,0:T(8,128)(2,1)S(1)} %get-tuple-element.24.back_ref, bf16[2,128,256]{2,1,0:T(8,128)(2,1)S(1)} %collective-permute-done.3.border_ref, bf16[2,128,64]{2,1,0:T(8,128)(2,1)S(1)} %copy.16.conv_w_ref), custom_call_target="tpu_custom_call" | custom-call | flops 67108864 | bytes 1048576 | tf_op jit(solution)/shard_map/input_grad/pallas_call | solution.py:441
  39.4 0.0 collective-permute-done.2.boundary_ref
  39.4 0.0 copy-start.9
  39.4 0.7 %copy-done.9 = f32[64]{0:T(128)S(1)} copy-done((f32[64]{0:T(128)S(1)}, f32[64]{0:T(128)}, u32[]{:S(2)}) %copy-start.9) | copy-done | bytes 280
  40.1 1.5 %outputs.1 = bf16[8,64,256]{2,1,0:T(8,128)(2,1)} custom-call(bf16[8,64,256]{2,1,0:T(8,128)(2,1)S(1)} %bitcast.15, bf16[512,256]{1,0:T(8,128)(2,1)S(1)} %get-tuple-element.22.hidden_ref, bf16[512,128]{1,0:T(8,128)(2,1)S(1)} %get-tuple-element.23.own_boundary_ref, bf16[512,128]{1,0:T(8,128)(2,1)S(1)} %collective-permute-done.2.boundary_ref, ...), custom_call_target="tpu_custom_call" | custom-call | flops 262144000 | bytes 1048576 | tf_op jit(solution)/shard_map/outputs/pallas_call | solution.py:441
  41.6 0.0 collective-permute-done.9.other_ref
  41.6 0.7 %final.1 = (f32[2,128,64]{2,1,0:T(8,128)S(1)}, f32[1,128]{1,0:T(1,128)}, f32[3,64,64]{2,1,0:T(8,128)}, f32[1,64]{1,0:T(1,128)}) custom-call(f32[128,128]{1,0:T(8,128)S(1)} %add.19.kept_ref, f32[128,128]{1,0:T(8,128)S(1)} %collective-permute-done.9.other_ref), custom_call_target="tpu_custom_call" | custom-call | tf_op jit(solution)/shard_map/final/pallas_call | solution.py:441
  42.3 0.7 %copy.18 = f32[2,128,64]{1,2,0:T(8,128)} copy(f32[2,128,64]{2,1,0:T(8,128)S(1)} %get-tuple-element.34) | data formatting | bytes 131072
  (6 shorter events, 0.1 us)
Async XLA Ops:
  0.6 0.7 %copy-start.6 = (s32[1,2]{1,0:T(1,128)S(1)}, s32[1,2]{1,0:T(1,128)}, u32[]{:S(2)}) copy-start(s32[1,2]{1,0:T(1,128)} %counts_ref.3) | copy-start | bytes 28
  0.6 0.7 %copy-start.5 = (s32[1,2,64]{2,1,0:T(2,128)S(1)}, s32[1,2,64]{2,1,0:T(2,128)}, u32[]{:S(2)}) copy-start(s32[1,2,64]{2,1,0:T(2,128)} %rows_ref.3) | copy-start | bytes 1540
  1.3 0.9 %copy-start = (bf16[1,8,64,256]{3,2,1,0:T(8,128)(2,1)S(1)}, bf16[1,8,64,256]{3,2,1,0:T(8,128)(2,1)}, u32[]{:S(2)}) copy-start(bf16[1,8,64,256]{3,2,1,0:T(8,128)(2,1)} %param.11) | copy-start | bytes 786436
  2.3 1.0 %copy-start.3 = (bf16[2,8,128,128]{3,2,1,0:T(8,128)(2,1)S(1)}, bf16[2,8,128,128]{3,2,1,0:T(8,128)(2,1)}, u32[]{:S(2)}) copy-start(bf16[2,8,128,128]{3,2,1,0:T(8,128)(2,1)} %adj_ref.1) | copy-start | bytes 1572868
  3.3 0.7 %copy-start.7 = (s32[2,8]{1,0:T(2,128)S(1)}, s32[2,8]{1,0:T(2,128)}, u32[]{:S(2)}) copy-start(s32[2,8]{1,0:T(2,128)} %cols_ref.1) | copy-start | bytes 196
  4.0 4.2 %copy-start.2 = (bf16[1,8,64,256]{3,2,1,0:T(8,128)(2,1)S(1)}, bf16[1,8,64,256]{3,2,1,0:T(8,128)(2,1)}, u32[]{:S(2)}) copy-start(bf16[1,8,64,256]{3,2,1,0:T(8,128)(2,1)} %param.10) | copy-start | bytes 786436
  4.0 9.7 %copy-start.1 = (bf16[1,8,64,256]{3,2,1,0:T(8,128)(2,1)S(1)}, bf16[1,8,64,256]{3,2,1,0:T(8,128)(2,1)}, u32[]{:S(2)}) copy-start(bf16[1,8,64,256]{3,2,1,0:T(8,128)(2,1)} %param.11) | copy-start | bytes 786436
  5.2 6.7 %copy-start.10 = (bf16[2,128,64]{1,2,0:T(8,128)(2,1)S(1)}, bf16[2,128,64]{1,2,0:T(8,128)(2,1)}, u32[]{:S(2)}) copy-start(bf16[2,128,64]{1,2,0:T(8,128)(2,1)} %param.12) | copy-start | bytes 98308
  5.2 8.6 %collective-permute-start.1 = (bf16[576,128]{1,0:T(8,128)(2,1)S(1)}, bf16[576,128]{1,0:T(8,128)(2,1)S(1)}, u32[]{:S(2)}, u32[]{:S(2)}) collective-permute-start(bf16[576,128]{1,0:T(8,128)(2,1)S(1)} %get-tuple-element.19.own_packed_ref), channel_id=1, source_target_pairs={{0,4},{4,0},{1,5},{5,1},{2,6},{6,2},{3,7},{7,3},{8,12},{12,8},{9,1... | collective-permute-start | bytes 442376 | tf_op jit(solution)/shard_map/ppermute | solution.py:455
  8.2 5.5 %copy-start.4 = (bf16[3,64,64]{2,1,0:T(8,128)(2,1)S(1)}, bf16[3,64,64]{2,1,0:T(8,128)(2,1)}, u32[]{:S(2)}) copy-start(bf16[3,64,64]{2,1,0:T(8,128)(2,1)} %mix_w_ref.3) | copy-start | bytes 73732
  8.2 5.5 %collective-permute-start = (bf16[2,64,256]{2,1,0:T(8,128)(2,1)S(1)}, bf16[2,64,256]{2,1,0:T(8,128)(2,1)S(1)}, u32[]{:S(2)}, u32[]{:S(2)}) collective-permute-start(bf16[2,64,256]{2,1,0:T(8,128)(2,1)S(1)} %slice_bitcast_fusion), channel_id=1, source_target_pairs={{0,1},{1,2},{2,3},{4,5},{5,6},{6,7},{8,9},{9,10},{10,11},{12,13},{... | collective-permute-start | bytes 196616 | tf_op jit(solution)/shard_map/ppermute | solution.py:17
  13.7 0.7 %copy-start.8 = (f32[128]{0:T(128)S(1)}, f32[128]{0:T(128)}, u32[]{:S(2)}) copy-start(f32[128]{0:T(128)} %param.13) | copy-start | bytes 1540
  17.0 1.3 %collective-permute-start.4 = (f32[128,128]{1,0:T(8,128)S(1)}, f32[128,128]{1,0:T(8,128)S(1)}, u32[]{:S(2)}, u32[]{:S(2)}) collective-permute-start(f32[128,128]{1,0:T(8,128)S(1)} %get-tuple-element.27), channel_id=1, source_target_pairs={{0,8},{8,0},{16,24},{24,16},{1,9},{9,1},{17,25},{25,17},{2,10},{10... | collective-permute-start | bytes 196616 | tf_op jit(solution)/shard_map/ppermute | solution.py:455
  18.3 4.3 %collective-permute-start.5 = (f32[128,128]{1,0:T(8,128)S(1)}, f32[128,128]{1,0:T(8,128)S(1)}, u32[]{:S(2)}, u32[]{:S(2)}) collective-permute-start(f32[128,128]{1,0:T(8,128)S(1)} %add.15), channel_id=1, source_target_pairs={{0,16},{8,24},{16,0},{24,8},{1,17},{9,25},{17,1},{25,9},{2,18},{10... | collective-permute-start | bytes 196616 | tf_op jit(solution)/shard_map/ppermute | solution.py:455
  22.7 4.3 %collective-permute-start.6 = (f32[128,128]{1,0:T(8,128)S(1)}, f32[128,128]{1,0:T(8,128)S(1)}, u32[]{:S(2)}, u32[]{:S(2)}) collective-permute-start(f32[128,128]{1,0:T(8,128)S(1)} %add.16), channel_id=1, source_target_pairs={{0,4},{4,0},{1,5},{5,1},{2,6},{6,2},{3,7},{7,3},{8,12},{12,8},{9,1... | collective-permute-start | bytes 196616 | tf_op jit(solution)/shard_map/ppermute | solution.py:455
  27.0 4.9 %collective-permute-start.7 = (f32[128,128]{1,0:T(8,128)S(1)}, f32[128,128]{1,0:T(8,128)S(1)}, u32[]{:S(2)}, u32[]{:S(2)}) collective-permute-start(f32[128,128]{1,0:T(8,128)S(1)} %add.17), channel_id=1, source_target_pairs={{0,1},{1,0},{2,3},{3,2},{4,5},{5,4},{6,7},{7,6},{8,9},{9,8},{10,11... | collective-permute-start | bytes 196616 | tf_op jit(solution)/shard_map/ppermute | solution.py:455
  29.4 8.9 %collective-permute-start.3 = (bf16[2,128,256]{2,1,0:T(8,128)(2,1)S(1)}, bf16[2,128,256]{2,1,0:T(8,128)(2,1)S(1)}, u32[]{:S(2)}, u32[]{:S(2)}) collective-permute-start(bf16[2,128,256]{2,1,0:T(8,128)(2,1)S(1)} %get-tuple-element.25), channel_id=1, source_target_pairs={{1,0},{2,1},{3,2},{5,4},{6,5},{7,6},{9,8},{10,9},{11,10},{13,12},{... | collective-permute-start | bytes 393224 | tf_op jit(solution)/shard_map/ppermute | solution.py:17
  30.7 8.7 %collective-permute-start.2 = (bf16[512,128]{1,0:T(8,128)(2,1)S(1)}, bf16[512,128]{1,0:T(8,128)(2,1)S(1)}, u32[]{:S(2)}, u32[]{:S(2)}) collective-permute-start(bf16[512,128]{1,0:T(8,128)(2,1)S(1)} %get-tuple-element.23.own_boundary_ref), channel_id=1, source_target_pairs={{0,4},{4,0},{1,5},{5,1},{2,6},{6,2},{3,7},{7,3},{8,12},{12,8},{9,1... | collective-permute-start | bytes 393224 | tf_op jit(solution)/shard_map/ppermute | solution.py:455
  31.9 6.3 %collective-permute-start.8 = (f32[128,128]{1,0:T(8,128)S(1)}, f32[128,128]{1,0:T(8,128)S(1)}, u32[]{:S(2)}, u32[]{:S(2)}) collective-permute-start(f32[128,128]{1,0:T(8,128)S(1)} %add.18), channel_id=1, source_target_pairs={{0,2},{1,3},{2,0},{3,1},{4,6},{5,7},{6,4},{7,5},{8,10},{9,11},{10,... | collective-permute-start | bytes 196616 | tf_op jit(solution)/shard_map/ppermute | solution.py:455
  38.3 3.3 %collective-permute-start.9 = (f32[128,128]{1,0:T(8,128)S(1)}, f32[128,128]{1,0:T(8,128)S(1)}, u32[]{:S(2)}, u32[]{:S(2)}) collective-permute-start(f32[128,128]{1,0:T(8,128)S(1)} %add.19.kept_ref), channel_id=1, source_target_pairs={{0,8},{8,0},{16,24},{24,16},{1,9},{9,1},{17,25},{25,17},{2,10},{10... | collective-permute-start | bytes 196616 | tf_op jit(solution)/shard_map/ppermute | solution.py:455
  39.4 0.7 %copy-start.9 = (f32[64]{0:T(128)S(1)}, f32[64]{0:T(128)}, u32[]{:S(2)}) copy-start(f32[64]{0:T(128)} %param.15) | copy-start | bytes 772

commit v2 on v0

--- a/solution.py
+++ b/solution.py
@@ -1,8 +1,11 @@
+import functools
 import math
 
 import jax
 import jax.numpy as jnp
 from jax import lax
+from jax.experimental import pallas as pl
+from jax.experimental.pallas import tpu as pltpu
 from jax.sharding import PartitionSpec as P
 
 DILATION_SIZE = 2
@@ -85,7 +88,7 @@
     return (grad_mix_w, grad_mix_b)
 
 
-def body(inputs, grad_out, conv_w, conv_b, mix_w, mix_b, adj_tiles, tile_cols, send_rows, counts):
+def general_body(inputs, grad_out, conv_w, conv_b, mix_w, mix_b, adj_tiles, tile_cols, send_rows, counts):
     sample_input = inputs[0]
     sample_grad = grad_out[0]
     timestep_count, chan_count, sensor_count = sample_input.shape
@@ -197,6 +200,608 @@
     )
 
 
+BF16 = jnp.bfloat16
+F32 = jnp.float32
+NT = (((1,), (1,)), ((), ()))
+VMEM_BYTES = 24 * 1024 * 1024
+
+
+def mm(left, right):
+    return jnp.dot(left, right, preferred_element_type=F32)
+
+
+def mm_nt(left, right):
+    return lax.dot_general(left, right, NT, preferred_element_type=F32)
+
+
+def upper_lanes(shape):
+    return lax.broadcasted_iota(jnp.int32, shape, 1) >= shape[1] // 2
+
+
+def halves(matrix):
+    upper = upper_lanes(matrix.shape)
+    zero = jnp.zeros_like(matrix)
+    return jnp.where(upper, zero, matrix), jnp.where(upper, matrix, zero)
+
+
+def fold(first, second):
+    return jnp.where(upper_lanes(first.shape), second, first)
+
+
+def times_halves(left, right):
+    half = left.shape[0] // 2
+    return fold(mm(left[:half], right), mm(left[half:], right))
+
+
+def unfold_nt(folded, right):
+    lower, upper = halves(right)
+    return jnp.concatenate([mm_nt(folded, lower), mm_nt(folded, upper)], 0)
+
+
+def link_matrix(packed):
+    packed = packed.astype(F32)
+    turned = pltpu.roll(packed, packed.shape[1] // 2, 1)
+    low, high = halves(packed)
+    turned_low, turned_high = halves(turned)
+    return jnp.concatenate([low, turned_low, turned_high, high], 0).astype(BF16)
+
+
+def column(row):
+    size = row.shape[1]
+    first = lax.broadcasted_iota(jnp.int32, (size, size), 0)
+    second = lax.broadcasted_iota(jnp.int32, (size, size), 1)
+    return jnp.sum(jnp.where(first == second, row, 0.0), axis=1, keepdims=True)
+
+
+def fetch(pairs, sems):
+    copies = [
+        pltpu.make_async_copy(source, target, sems.at[index])
+        for index, (source, target) in enumerate(pairs)
+    ]
+    for copy in copies:
+        copy.start()
+    return copies
+
+
+def prepare_kernel(
+    cols_hbm,
+    counts_hbm,
+    rows_hbm,
+    adj_hbm,
+    grad_hbm,
+    input_hbm,
+    packed_ref,
+    own_ref,
+    halo_ref,
+    chosen_ref,
+    grad_ref,
+    tail_ref,
+    adj_ref,
+    cols_ref,
+    counts_ref,
+    rows_ref,
+    sems,
+):
+    row_blocks, slots, tile = adj_ref.shape[:3]
+    own_slots = slots // 2
+    steps = input_hbm.shape[0]
+    copies = fetch(
+        [
+            (adj_hbm.at[:, pl.ds(own_slots, own_slots)], adj_ref.at[:, pl.ds(own_slots, own_slots)]),
+            (cols_hbm, cols_ref),
+            (counts_hbm, counts_ref),
+            (rows_hbm, rows_ref),
+            (adj_hbm.at[:, pl.ds(0, own_slots)], adj_ref.at[:, pl.ds(0, own_slots)]),
+            (grad_hbm, grad_ref),
+            (input_hbm.at[pl.ds(steps - DILATION_SIZE, DILATION_SIZE)], tail_ref),
+        ],
+        sems,
+    )
+    other = 1 - lax.axis_index("space")
+    sensors = grad_ref.shape[1]
+    half_rows = grad_ref.shape[0] // 2
+    slot_count = rows_ref.shape[2]
+    upper = upper_lanes((tile, tile)).astype(jnp.int32)
+    copies[0].wait()
+    for r in range(row_blocks):
+        far = adj_ref[r, own_slots].astype(F32)
+        for k in range(own_slots + 1, slots):
+            far = far + adj_ref[r, k].astype(F32)
+        far = jnp.where(upper == other, far, pltpu.roll(far, tile // 2, 1))
+        halo_ref[r * tile : (r + 1) * tile, :] = far.astype(BF16)
+    for copy in copies[1:4]:
+        copy.wait()
+    rows = rows_ref[0, pl.ds(other, 1), :]
+    rows = jnp.concatenate([rows, rows], 1)
+    lanes = lax.broadcasted_iota(jnp.int32, (1, 2 * slot_count), 1)
+    place = lanes - jnp.where(lanes >= slot_count, slot_count, 0)
+    rows = jnp.where(place < counts_ref[0, other], rows, -1)
+    sensor = lax.broadcasted_iota(jnp.int32, (sensors, 2 * slot_count), 0)
+    chosen = jnp.where(sensor == rows, 1.0, 0.0).astype(F32)
+    chosen_ref[...] = chosen.astype(BF16)
+    turned = jnp.transpose(chosen)[:slot_count].astype(BF16)
+    halo = halo_ref[...]
+    packed_ref[2 * half_rows :, :] = times_halves(turned, halo).astype(BF16)
+    copies[4].wait()
+    for r in range(row_blocks):
+        sums = [jnp.zeros((tile, tile), F32), jnp.zeros((tile, tile), F32)]
+        for k in range(own_slots):
+            item = adj_ref[r, k].astype(F32)
+            for block in range(2):
+                share = jnp.where(cols_ref[r, k] == block, 1.0, 0.0).astype(F32)
+                sums[block] = sums[block] + item * share
+        own_ref[r * tile : (r + 1) * tile, :] = jnp.concatenate(sums, 1).astype(BF16)
+    copies[5].wait()
+    grad = grad_ref[...]
+    packed_ref[:half_rows, :] = times_halves(grad, halo).astype(BF16)
+    first = mm(grad, own_ref[...]).astype(BF16)
+    packed_ref[half_rows : 2 * half_rows, :] = times_halves(first, halo).astype(BF16)
+    copies[6].wait()
+
+
+def gate_step(t, earlier, input_ref, preact, hidden_ref, slopes_ref, right_ref):
+    steps, chans, sensors = input_ref.shape
+    at = slice(t * chans, (t + 1) * chans)
+    span = slice(t * sensors, (t + 1) * sensors)
+    filtered = jnp.tanh(preact[:chans])
+    gating = 0.5 * jnp.tanh(0.5 * preact[chans:]) + 0.5
+    product = filtered * gating
+    hidden = product.astype(BF16)
+    hidden_ref[at, :] = hidden
+    slopes_ref[t, :chans] = (1.0 - filtered * filtered) * gating
+    slopes_ref[t, chans:] = product * (1.0 - gating)
+    right_ref[:chans, span] = earlier
+    right_ref[chans : 2 * chans, span] = input_ref[t]
+    right_ref[2 * chans : 2 * chans + 16, span] = jnp.ones((16, sensors), BF16)
+    right_ref[2 * chans + 16 : 3 * chans + 16, span] = hidden
+    right_ref[3 * chans + 16 :, span] = hidden
+
+
+def forward_kernel(
+    input_hbm,
+    conv_w_hbm,
+    conv_b_hbm,
+    mix_w_hbm,
+    mix_b_hbm,
+    grad_ref,
+    own_ref,
+    hidden_ref,
+    slopes_ref,
+    right_ref,
+    near_ref,
+    input_ref,
+    taps_ref,
+    turned_taps_ref,
+    bias_ref,
+    mix_ref,
+    mixing_ref,
+    mix_bias_ref,
+    sems,
+):
+    copies = fetch(
+        [
+            (input_hbm, input_ref),
+            (conv_w_hbm, taps_ref),
+            (conv_b_hbm, bias_ref),
+            (mix_w_hbm, mix_ref),
+            (mix_b_hbm, mix_bias_ref),
+        ],
+        sems,
+    )
+    steps, chans, sensors = input_ref.shape
+    near_ref[...] = mm(grad_ref[...], own_ref[...])
+    for copy in copies:
+        copy.wait()
+    mixing = jnp.transpose(mix_ref[...].reshape(3 * chans, chans).astype(F32))
+    mixing_ref[...] = mixing.astype(BF16)
+    taps = taps_ref[...].reshape(2 * chans, 2 * chans).astype(F32)
+    taps = jnp.transpose(taps).astype(BF16)
+    turned_taps_ref[...] = taps
+    bias = column(bias_ref[...])
+    for t in range(DILATION_SIZE, steps):
+        earlier = input_ref[t - DILATION_SIZE]
+        preact = mm(taps, jnp.concatenate([earlier, input_ref[t]], 0)) + bias
+        gate_step(t, earlier, input_ref, preact, hidden_ref, slopes_ref, right_ref)
+
+
+def backward_kernel(
+    grad_ref,
+    own_packed_ref,
+    packed_ref,
+    border_ref,
+    own_ref,
+    chosen_ref,
+    near_ref,
+    input_ref,
+    taps_ref,
+    turned_taps_ref,
+    bias_ref,
+    mixing_ref,
+    hidden_old_ref,
+    slopes_old_ref,
+    right_old_ref,
+    kept_ref,
+    given_ref,
+    back_ref,
+    early_ref,
+    hidden_ref,
+    left_scr,
+    one_scr,
+    two_scr,
+    slopes_ref,
+    right_ref,
+):
+    steps, wide, sensors = back_ref.shape
+    chans = wide // 2
+    rows = steps * chans
+    half_rows = rows // 2
+    border_rows = DILATION_SIZE * chans
+    border_span = DILATION_SIZE * sensors
+    core = lax.axis_index("dp") % 2
+    own = own_ref[...]
+    chosen = chosen_ref[...]
+    link = link_matrix(packed_ref[rows:, :])
+    one = (near_ref[...] + unfold_nt(packed_ref[:half_rows, :], chosen)).astype(BF16)
+    second = packed_ref[half_rows:rows, :].astype(F32) + mm(own_packed_ref[:half_rows, :], link)
+    two = (mm(one, own) + unfold_nt(second.astype(BF16), chosen)).astype(BF16)
+    one_scr[...] = one
+    two_scr[...] = two
+    bias = column(bias_ref[...])
+    has_earlier = lax.axis_index("tm") > 0
+    hidden_ref[border_rows:, :] = hidden_old_ref[border_rows:, :]
+    for t in range(DILATION_SIZE):
+        earlier = border_ref[t]
+        earlier = jnp.where(has_earlier, earlier, jnp.zeros_like(earlier))
+        window = jnp.concatenate([earlier, input_ref[t]], 0)
+        preact = mm(turned_taps_ref[...], window) + bias
+        gate_step(t, earlier, input_ref, preact, hidden_ref, slopes_ref, right_ref)
+    mixing = mixing_ref[...]
+    for t in range(steps):
+        at = slice(t * chans, (t + 1) * chans)
+        span = slice(t * sensors, (t + 1) * sensors)
+        fields = jnp.concatenate([grad_ref[at, :], one_scr[at, :], two_scr[at, :]], 0)
+        back_hidden = mm(mixing, fields)
+        back_hidden = jnp.concatenate([back_hidden, back_hidden], 0)
+        slopes = slopes_ref[t] if t < DILATION_SIZE else slopes_old_ref[t]
+        back_pre = (back_hidden * slopes).astype(BF16)
+        back_ref[t] = back_pre
+        left_scr[:wide, span] = back_pre
+        left_scr[wide:, span] = fields
+        if t < DILATION_SIZE:
+            early_ref[t] = mm(taps_ref[0], back_pre).astype(BF16)
+    ones = wide + 16
+    conv = mm_nt(right_old_ref[:ones, border_span:], left_scr[: wide + chans, border_span:])
+    conv = conv + mm_nt(right_ref[:ones, :], left_scr[: wide + chans, :border_span])
+    mixes = mm_nt(left_scr[wide:, border_span:], right_old_ref[ones:, border_span:])
+    mixes = mixes + mm_nt(left_scr[wide:, :border_span], right_ref[ones:, :])
+    sums = conv[wide : wide + 8]
+    conv = conv[:wide, :wide]
+    zero, first, second = [mixes[k * chans : (k + 1) * chans] for k in range(3)]
+    tail = jnp.concatenate([sums[:, wide:], jnp.zeros((8, chans), F32)], 1)
+    biases = jnp.concatenate(
+        [
+            pltpu.roll(tail, chans, 1),
+            pltpu.roll(sums[:, :wide], chans, 1),
+            sums[:, :wide],
+            jnp.zeros((chans - 24, wide), F32),
+        ],
+        0,
+    )
+    mixes = jnp.concatenate([fold(zero, first), fold(second, biases)], 0)
+    kept_ref[...] = jnp.where(core == 0, conv, mixes)
+    given_ref[...] = jnp.where(core == 0, mixes, conv)
+
+
+def boundary_kernel(hidden_ref, own_ref, chosen_ref, boundary_ref):
+    hidden = hidden_ref[...]
+    chosen = chosen_ref[...]
+    hop = mm_nt(hidden, own_ref[...]).astype(BF16)
+    half_rows = hidden.shape[0] // 2
+    boundary_ref[:half_rows, :] = times_halves(hidden, chosen).astype(BF16)
+    boundary_ref[half_rows:, :] = times_halves(hop, chosen).astype(BF16)
+
+
+def outputs_kernel(
+    input_ref,
+    hidden_ref,
+    own_boundary_ref,
+    boundary_ref,
+    packed_ref,
+    own_ref,
+    halo_ref,
+    mix_ref,
+    bias_ref,
+    out_ref,
+):
+    steps, chans, sensors = input_ref.shape
+    rows = steps * chans
+    half_rows = rows // 2
+    own = own_ref[...]
+    halo = halo_ref[...]
+    link = link_matrix(packed_ref[rows:, :])
+    hidden = hidden_ref[...]
+    one = (mm_nt(hidden, own) + unfold_nt(boundary_ref[:half_rows, :], halo)).astype(BF16)
+    far = boundary_ref[half_rows:, :].astype(F32) + mm_nt(own_boundary_ref[:half_rows, :], link)
+    two = (mm_nt(one, own) + unfold_nt(far.astype(BF16), halo)).astype(BF16)
+    bias = column(bias_ref[...])
+    for t in range(steps):
+        at = slice(t * chans, (t + 1) * chans)
+        mixed = mm(mix_ref[0], hidden[at]) + mm(mix_ref[1], one[at]) + mm(mix_ref[2], two[at])
+        out_ref[t] = (mixed + bias + input_ref[t].astype(F32)).astype(BF16)
+
+
+def input_grad_kernel(grad_ref, back_ref, early_ref, taps_ref, out_ref):
+    steps, chans, sensors = out_ref.shape
+    has_later = lax.axis_index("tm") < lax.axis_size("tm") - 1
+    taps = jnp.concatenate([taps_ref[0], taps_ref[1]], 1)
+    for t in range(steps):
+        at = slice(t * chans, (t + 1) * chans)
+        later = t + DILATION_SIZE
+        total = grad_ref[at, :].astype(F32)
+        if later < steps:
+            total = total + mm(taps, jnp.concatenate([back_ref[later], back_ref[t]], 0))
+        else:
+            early = early_ref[later - steps].astype(F32)
+            early = jnp.where(has_later, early, jnp.zeros_like(early))
+            total = total + mm(taps_ref[1], back_ref[t]) + early
+        out_ref[t] = total.astype(BF16)
+
+
+def final_kernel(scale, kept_ref, other_ref, conv_w_ref, conv_b_ref, mix_w_ref, mix_b_ref):
+    core = lax.axis_index("dp") % 2
+    kept = kept_ref[...] * scale
+    other = other_ref[...] * scale
+    conv = jnp.where(core == 0, kept, other)
+    mixes = jnp.where(core == 0, other, kept)
+    chans = conv.shape[1] // 2
+    conv_w_ref[0] = conv[:chans]
+    conv_w_ref[1] = conv[chans:]
+    mix_w_ref[0] = mixes[:chans, :chans]
+    mix_w_ref[1] = pltpu.roll(mixes[:chans], chans, 1)[:, :chans]
+    mix_w_ref[2] = mixes[chans:, :chans]
+    biases = mixes[chans : chans + 24]
+    turned = pltpu.roll(biases, chans, 1)
+    mix_b_ref[...] = turned[0:1, :chans]
+    conv_b_ref[...] = fold(turned[8:9], biases[16:17])
+
+
+VMEM = pl.BlockSpec(memory_space=pltpu.VMEM)
+HBM = pl.BlockSpec(memory_space=pltpu.HBM)
+DMA = pltpu.SemaphoreType.DMA
+
+
+def call(kernel, name, in_specs, out_shape, args, scratch=(), micros=1.0):
+    args = [
+        pltpu.with_memory_space_constraint(arg, pltpu.HBM) if spec is HBM else arg
+        for spec, arg in zip(in_specs, args)
+    ]
+    return pl.pallas_call(
+        kernel,
+        out_shape=out_shape,
+        in_specs=in_specs,
+        out_specs=jax.tree.map(lambda _: VMEM, out_shape),
+        scratch_shapes=list(scratch),
+        compiler_params=pltpu.CompilerParams(vmem_limit_bytes=VMEM_BYTES),
+        cost_estimate=pl.CostEstimate(
+            flops=0, bytes_accessed=int(micros * 3_600_000), transcendentals=0
+        ),
+        name=name,
+    )(*args)
+
+
+def swap(value, axis, bit):
+    count = lax.axis_size(axis)
+    return lax.ppermute(value, axis, [(source, source ^ bit) for source in range(count)])
+
+
+def shift(value, axis, steps):
+    count = lax.axis_size(axis)
+    return lax.ppermute(value, axis, [(source, (source + steps) % count) for source in range(count)])
+
+
+def bits(count):
+    return [1 << place for place in range(count.bit_length() - 1)]
+
+
+def after(value, *earlier):
+    return lax.optimization_barrier((value, *earlier))[0]
+
+
+def pair_body(inputs, grad_out, conv_w, conv_b, mix_w, mix_b, adj_tiles, tile_cols, send_rows, counts):
+    sample_input = inputs[0]
+    sample_grad = grad_out[0]
+    steps, chans, sensors = sample_input.shape
+    rows = steps * chans
+    half_rows = rows // 2
+    wide = 2 * chans
+    shape = jax.ShapeDtypeStruct
+    grad_flat = sample_grad.reshape(rows, sensors)
+    taps = jnp.transpose(conv_w, (0, 2, 1))
+    packed, own, halo, chosen, grad, tail = call(
+        prepare_kernel,
+        "prepare",
+        [HBM] * 6,
+        (
+            shape((rows + chans // 2, wide), BF16),
+            shape((sensors, sensors), BF16),
+            shape((sensors, wide), BF16),
+            shape((sensors, wide), BF16),
+            shape((rows, sensors), BF16),
+            shape((DILATION_SIZE, chans, sensors), BF16),
+        ),
+        (tile_cols, counts, send_rows, adj_tiles, grad_flat, sample_input),
+        scratch=(
+            pltpu.VMEM(adj_tiles.shape, BF16),
+            pltpu.SMEM(tile_cols.shape, jnp.int32),
+            pltpu.SMEM(counts.shape, jnp.int32),
+            pltpu.VMEM(send_rows.shape, jnp.int32),
+            DMA((7,)),
+        ),
+        micros=2.0,
+    )
+    packed_far = swap(packed, "space", 1)
+    border = from_behind(tail, "tm", 1)
+    hidden_late, slopes, right, near, kept_input, kept_taps, turned_taps, bias, mix, mixing, mix_bias = call(
+        forward_kernel,
+        "forward",
+        [HBM] * 5 + [VMEM] * 2,
+        (
+            shape((rows, sensors), BF16),
+            shape((steps, wide, sensors), F32),
+            shape((2 * wide + 16, steps * sensors), BF16),
+            shape((rows, sensors), F32),
+            shape(sample_input.shape, BF16),
+            shape(taps.shape, BF16),
+            shape((wide, wide), BF16),
+            shape((1, wide), F32),
+            shape(mix_w.shape, BF16),
+            shape((chans, 3 * chans), BF16),
+            shape((1, chans), F32),
+        ),
+        (
+            sample_input,
+            taps,
+            conv_b.reshape(1, wide),
+            mix_w,
+            mix_b.reshape(1, chans),
+            grad,
+            own,
+        ),
+        scratch=(DMA((5,)),),
+        micros=1.5,
+    )
+    border_span = DILATION_SIZE * sensors
+    kept, given, back, early, hidden = call(
+        backward_kernel,
+        "backward",
+        [VMEM] * 15,
+        (
+            shape((wide, wide), F32),
+            shape((wide, wide), F32),
+            shape((steps, wide, sensors), BF16),
+            shape((DILATION_SIZE, chans, sensors), BF16),
+            shape((rows, sensors), BF16),
+        ),
+        (
+            grad,
+            packed,
+            packed_far,
+            border,
+            own,
+            chosen,
+            near,
+            kept_input,
+            kept_taps,
+            turned_taps,
+            bias,
+            mixing,
+            hidden_late,
+            slopes,
+            right,
+        ),
+        scratch=(
+            pltpu.VMEM((wide + 3 * chans, steps * sensors), BF16),
+            pltpu.VMEM((rows, sensors), BF16),
+            pltpu.VMEM((rows, sensors), BF16),
+            pltpu.VMEM((DILATION_SIZE, wide, sensors), F32),
+            pltpu.VMEM((2 * wide + 16, border_span), BF16),
+        ),
+        micros=2.0,
+    )
+    total = kept + swap(given, "dp", 1)
+    rounds = (
+        [("dp", bit) for bit in bits(lax.axis_size("dp"))[1:]]
+        + [("space", bit) for bit in bits(lax.axis_size("space"))]
+        + [("tm", bit) for bit in bits(lax.axis_size("tm"))]
+    )
+    early_far = shift(early, "tm", -1)
+    for index, (axis, bit) in enumerate(rounds):
+        if index == 2:
+            boundary = call(
+                boundary_kernel,
+                "boundary",
+                [VMEM] * 3,
+                shape((rows, wide), BF16),
+                (after(hidden, total), own, chosen),
+                micros=0.4,
+            )
+            boundary_far = swap(boundary, "space", 1)
+        arrived = swap(total, axis, bit)
+        if index == 2:
+            grad_inputs = call(
+                input_grad_kernel,
+                "input_grad",
+                [VMEM] * 4,
+                shape(sample_grad.shape, BF16),
+                (grad, back, early_far, kept_taps),
+                micros=1.2,
+            )
+            arrived = after(arrived, grad_inputs)
+        if index == 3:
+            outputs = call(
+                outputs_kernel,
+                "outputs",
+                [VMEM] * 9,
+                shape(sample_input.shape, BF16),
+                (kept_input, hidden, boundary, boundary_far, packed_far, own, halo, mix, mix_bias),
+                micros=2.0,
+            )
+            arrived = after(arrived, outputs)
+        total = total + arrived
+    total_far = swap(total, "dp", 1)
+    cell_count = (
+        inputs.shape[0]
+        * steps
+        * sensors
+        * lax.axis_size("dp")
+        * lax.axis_size("space")
+        * lax.axis_size("tm")
+    )
+    scale = 1.0 / math.sqrt(cell_count)
+    grad_taps, grad_conv_b, grad_mix_w, grad_mix_b = call(
+        functools.partial(final_kernel, scale),
+        "final",
+        [VMEM] * 2,
+        (
+            shape((2, chans, wide), F32),
+            shape((1, wide), F32),
+            shape((3, chans, chans), F32),
+            shape((1, chans), F32),
+        ),
+        (total, total_far),
+    )
+    return (
+        outputs[None],
+        grad_inputs[None],
+        jnp.transpose(grad_taps, (0, 2, 1)),
+        grad_conv_b.reshape(wide),
+        grad_mix_w,
+        grad_mix_b.reshape(chans),
+    )
+
+
+def power_of_two(count):
+    return count & (count - 1) == 0
+
+
+def body(inputs, grad_out, conv_w, conv_b, mix_w, mix_b, adj_tiles, tile_cols, send_rows, counts):
+    tile = adj_tiles.shape[2]
+    axes = [lax.axis_size(axis) for axis in ("dp", "space", "tm")]
+    fits = (
+        axes[1] == 2
+        and axes[0] % 2 == 0
+        and all(power_of_two(count) for count in axes)
+        and inputs.shape[0] == 1
+        and inputs.shape[3] == 2 * tile
+        and inputs.shape[2] * 2 == tile
+        and send_rows.shape[2] * 2 == tile
+    )
+    chosen = pair_body if fits else general_body
+    return chosen(
+        inputs, grad_out, conv_w, conv_b, mix_w, mix_b, adj_tiles, tile_cols, send_rows, counts
+    )
+
+
 def solution(mesh):
     in_specs = (
         P("dp", "tm", None, "space"),

time: 259 us -> 35.3 us (0.14)
  waiting for transfers between devices: 113 us -> 6.85 us
  blocking collectives: 41.5 us -> 0 us
  other arithmetic: 30.8 us -> 0.05 us
  local copies, waits for them, and re-layouts: 18.8 us -> 0 us
  matrix products: 18.7 us -> 0 us
  between operations: 14.8 us -> 0.71 us
  Pallas kernels: 0 us -> 8.68 us
    psum x1 -> x0, waiting for transfers between devices: 110 us -> none  [body(): lax.psum((grad_conv_w, grad_conv_b, grad_mix_w, grad_mix_b), ('dp', 'spac...]
    psum x1 -> x0, blocking collectives: 41.5 us -> none  [body(): lax.psum((grad_conv_w, grad_conv_b, grad_mix_w, grad_mix_b), ('dp', 'spac...]
    scatter-add x6 -> x0, other arithmetic: 20.1 us -> none  [the longest x2 9.81 us: back_finish(): total.at[:, :, send_rows[0]].add(returned * live_slots.astype(jnp.float32))]
    dot_general x21 -> x0, matrix products: 18.7 us -> none  [the longest x3 3.95 us: body(): jnp.einsum('oc,tcn->ton', mix_w[index], fields[index], preferred_element_...]
    ppermute x0 -> x9, starting transfers between devices: none -> 15.3 us  [the longest x8 10.9 us: swap(): lax.ppermute(value, axis, [(source, source ^ bit) for source in range(cou...]
    all_to_all x4 -> x0, starting transfers between devices: 14.4 us -> none  [the longest x1 4.23 us: body(): lax.all_to_all(back_start(back_two, adj_tiles, tile_cols, send_rows), 'sp...]
    pallas_call x0 -> x7, Pallas kernels: none -> 8.68 us  [call(): pl.pallas_call(kernel, out_shape=out_shape, in_specs=in_specs, out_specs=...]
    unnamed x58 -> x0, local copies, waits for them, and re-layouts: 6.56 us -> none
  transfers between devices with their start and end apart: 7 -> 10, of which waited for: 2 -> 6; matrix products, arithmetic and copies ran while one was open for 18% -> 0% of each run, Pallas kernels for 0% -> 13%
where the time goes in v2:
time: 35.3 us; the launch traced here: 35.1 us
  starting transfers between devices  18.8 us (53%)
  Pallas kernels  8.68 us (25%)
  waiting for transfers between devices  6.85 us (19%)
  between operations  0.71 us (2%)
    ppermute x8, starting transfers between devices, swap(): lax.ppermute(value, axis, [(source, source ^ bit) for source in range(cou...  10.9 us
    pallas_call x7, Pallas kernels, call(): pl.pallas_call(kernel, out_shape=out_shape, in_specs=in_specs, out_specs=...  8.68 us
    ppermute x8, waiting for transfers between devices, swap(): lax.ppermute(value, axis, [(source, source ^ bit) for source in range(cou...  6.41 us
    ppermute x1, starting transfers between devices, shift(): lax.ppermute(value, axis, [(source, (source + steps) % count) for source...  4.39 us
    ppermute x1, starting transfers between devices, from_behind(): lax.ppermute(value, axis, [(source, source + steps) for source in range(l...  3.47 us
  transfers between devices with their start and end apart: 10, of which 6 were waited for; matrix products, arithmetic and copies ran while one was open for 0% of the time, Pallas kernels for 13%

profile of v2, /device:TPU:0, one launch (start us, length us, event | category | flops | bytes accessed | tf_op | source)
XLA Modules:
  0.0 35.1 jit_solution(14786559298267233908)
XLA Ops:
  0.6 2.0 %prepare.1 = (bf16[544,128]{1,0:T(8,128)(2,1)S(1)}, bf16[256,256]{1,0:T(8,128)(2,1)S(1)}, bf16[256,128]{1,0:T(8,128)(2,1)S(1)}, bf16[256,128]{1,0:T(8,128)(2,1)S...) custom-call(s32[2,8]{1,0:T(2,128)} %cols_hbm.1, s32[1,2]{1,0:T(1,128)} %counts_hbm.1, ...), custom_call_target="tpu_custom_call" | custom-call | bytes 7200000 | tf_op jit(solution)/shard_map/prepare/pallas_call | solution.py:578
  2.6 3.0 %collective-permute-start = (bf16[544,128]{1,0:T(8,128)(2,1)S(1)}, bf16[544,128]{1,0:T(8,128)(2,1)S(1)}, u32[]{:S(2)}, u32[]{:S(2)}) collective-permute-start(bf16[544,128]{1,0:T(8,128)(2,1)S(1)} %get-tuple-element.38.own_packed_ref), channel_id=1, source_target_pairs={{0,4},{4,0},{1,5},{5,1},{2,6},{6,2},{3,7},{7,3},{8,12},{12,8},{9,1... | collective-permute-start | bytes 417800 | tf_op jit(solution)/shard_map/ppermute | solution.py:594
  5.7 3.5 %collective-permute-start.1 = (bf16[2,64,256]{2,1,0:T(8,128)(2,1)S(1)}, bf16[2,64,256]{2,1,0:T(8,128)(2,1)S(1)}, u32[]{:S(2)}, u32[]{:S(2)}) collective-permute-start(bf16[2,64,256]{2,1,0:T(8,128)(2,1)S(1)} %get-tuple-element.39), channel_id=1, source_target_pairs={{0,1},{1,2},{2,3},{4,5},{5,6},{6,7},{8,9},{9,10},{10,11},{12,13},{... | collective-permute-start | bytes 196616 | tf_op jit(solution)/shard_map/ppermute | solution.py:17
  9.1 1.4 %forward.1 = (bf16[512,256]{1,0:T(8,128)(2,1)S(1)}, f32[8,128,256]{2,1,0:T(8,128)S(1)}, bf16[272,2048]{1,0:T(8,128)(2,1)S(1)}, f32[512,256]{1,0:T(8,128)S(1)}, b...) custom-call(bf16[8,64,256]{2,1,0:T(8,128)(2,1)} %bitcast.11, ...), custom_call_target="tpu_custom_call" | custom-call | bytes 5400000 | tf_op jit(solution)/shard_map/forward/pallas_call | solution.py:578
  10.6 0.4 %collective-permute-done.1.border_ref = bf16[2,64,256]{2,1,0:T(8,128)(2,1)S(1)} collective-permute-done((bf16[2,64,256]{2,1,0:T(8,128)(2,1)S(1)}, bf16[2,64,256]{2,1,0:T(8,128)(2,1)S(1)}, u32[]{:S(2)}, u32[]{:S(2)}) %collective-permute-start.1) | collective-permute-done | bytes 65568 | tf_op jit(solution)/shard_map/ppermute | solution.py:17
  11.0 0.0 collective-permute-done.packed_ref
  11.0 1.5 %backward.1 = (f32[128,128]{1,0:T(8,128)S(1)}, f32[128,128]{1,0:T(8,128)S(1)}, bf16[8,128,256]{2,1,0:T(8,128)(2,1)S(1)}, bf16[2,64,256]{2,1,0:T(8,128)(2,1)S(1)}, bf16[512,256]{1,0:T(8,128)(2,1)S(1)}) custom-call(bf16[512,256]{1,0:T(8,128)(2,1)S(1)} %get-tuple-element.35.grad_ref, bf16[544,128]{1,0:T(8,128)(2,1)S(1)} %get-tuple-element.38.own_packed_ref, ...), custom_call_target="tpu_custom_call" | custom-call | bytes 7200000 | tf_op jit(solution)/shard_map/backward/pallas_call | solution.py:578
  12.5 0.0 collective-permute-start.2
  12.6 1.2 %collective-permute-done.2 = f32[128,128]{1,0:T(8,128)S(1)} collective-permute-done((f32[128,128]{1,0:T(8,128)S(1)}, f32[128,128]{1,0:T(8,128)S(1)}, u32[]{:S(2)}, u32[]{:S(2)}) %collective-permute-start.2) | collective-permute-done | bytes 65568 | tf_op jit(solution)/shard_map/ppermute | solution.py:594
  13.8 1.6 %collective-permute-start.3 = (f32[128,128]{1,0:T(8,128)S(1)}, f32[128,128]{1,0:T(8,128)S(1)}, u32[]{:S(2)}, u32[]{:S(2)}) collective-permute-start(f32[128,128]{1,0:T(8,128)S(1)} %add.15), channel_id=1, source_target_pairs={{0,16},{8,24},{16,0},{24,8},{1,17},{9,25},{17,1},{25,9},{2,18},{10... | collective-permute-start | bytes 196616 | tf_op jit(solution)/shard_map/ppermute | solution.py:594
  15.4 2.8 %collective-permute-done.3 = f32[128,128]{1,0:T(8,128)S(1)} collective-permute-done((f32[128,128]{1,0:T(8,128)S(1)}, f32[128,128]{1,0:T(8,128)S(1)}, u32[]{:S(2)}, u32[]{:S(2)}) %collective-permute-start.3) | collective-permute-done | bytes 65568 | tf_op jit(solution)/shard_map/ppermute | solution.py:594
  18.1 0.6 %collective-permute-start.4 = (f32[128,128]{1,0:T(8,128)S(1)}, f32[128,128]{1,0:T(8,128)S(1)}, u32[]{:S(2)}, u32[]{:S(2)}) collective-permute-start(f32[128,128]{1,0:T(8,128)S(1)} %add.16), channel_id=1, source_target_pairs={{0,4},{4,0},{1,5},{5,1},{2,6},{6,2},{3,7},{7,3},{8,12},{12,8},{9,1... | collective-permute-start | bytes 196616 | tf_op jit(solution)/shard_map/ppermute | solution.py:594
  18.7 4.4 %collective-permute-start.6 = (bf16[2,64,256]{2,1,0:T(8,128)(2,1)S(1)}, bf16[2,64,256]{2,1,0:T(8,128)(2,1)S(1)}, u32[]{:S(2)}, u32[]{:S(2)}) collective-permute-start(bf16[2,64,256]{2,1,0:T(8,128)(2,1)S(1)} %get-tuple-element.57), channel_id=1, source_target_pairs={{0,3},{1,0},{2,1},{3,2},{4,7},{5,4},{6,5},{7,6},{8,11},{9,8},{10,9... | collective-permute-start | bytes 196616 | tf_op jit(solution)/shard_map/ppermute | solution.py:599
  23.1 0.0 collective-permute-done.4
  23.1 1.8 %collective-permute-start.7 = (f32[128,128]{1,0:T(8,128)S(1)}, f32[128,128]{1,0:T(8,128)S(1)}, u32[]{:S(2)}, u32[]{:S(2)}) collective-permute-start(f32[128,128]{1,0:T(8,128)S(1)} %add.17), channel_id=1, source_target_pairs={{0,1},{1,0},{2,3},{3,2},{4,5},{5,4},{6,7},{7,6},{8,9},{9,8},{10,11... | collective-permute-start | bytes 196616 | tf_op jit(solution)/shard_map/ppermute | solution.py:594
  24.9 0.4 %boundary.1.own_boundary_ref = bf16[512,128]{1,0:T(8,128)(2,1)S(1)} custom-call(bf16[512,256]{1,0:T(8,128)(2,1)S(1)} %get-tuple-element.52.hidden_ref, bf16[256,256]{1,0:T(8,128)(2,1)S(1)} %get-tuple-element.36.own_ref, bf16[256,128]{1,0:T(8,128)(2,1)S(1)} %get-tuple-element.40.chosen_ref), custom_call_target="tpu_custom_call" | custom-call | bytes 1440000 | tf_op jit(solution)/shard_map/boundary/pallas_call | solution.py:578
  25.4 0.6 %collective-permute-start.5 = (bf16[512,128]{1,0:T(8,128)(2,1)S(1)}, bf16[512,128]{1,0:T(8,128)(2,1)S(1)}, u32[]{:S(2)}, u32[]{:S(2)}) collective-permute-start(bf16[512,128]{1,0:T(8,128)(2,1)S(1)} %boundary.1.own_boundary_ref), channel_id=1, source_target_pairs={{0,4},{4,0},{1,5},{5,1},{2,6},{6,2},{3,7},{7,3},{8,12},{12,8},{9,1... | collective-permute-start | bytes 393224 | tf_op jit(solution)/shard_map/ppermute | solution.py:594
  26.0 0.0 collective-permute-done.6.early_ref
  26.0 1.0 %input_grad.1 = bf16[8,64,256]{2,1,0:T(8,128)(2,1)} custom-call(bf16[512,256]{1,0:T(8,128)(2,1)S(1)} %get-tuple-element.35.grad_ref, bf16[8,128,256]{2,1,0:T(8,128)(2,1)S(1)} %get-tuple-element.56.back_ref, bf16[2,64,256]{2,1,0:T(8,128)(2,1)S(1)} %collective-permute-done.6.early_ref, bf16[2,64,128]{2,1,0:T(8,128)(2,1)S(1)} %get-tuple-element.42.taps_ref), custom_call_target="tpu_custom_call" | custom-call | bytes 4320000 | tf_op jit(solution)/shard_map/input_grad/pallas_call | solution.py:578
  27.0 0.5 %collective-permute-done.7 = f32[128,128]{1,0:T(8,128)S(1)} collective-permute-done((f32[128,128]{1,0:T(8,128)S(1)}, f32[128,128]{1,0:T(8,128)S(1)}, u32[]{:S(2)}, u32[]{:S(2)}) %collective-permute-start.7) | collective-permute-done | bytes 65568 | tf_op jit(solution)/shard_map/ppermute | solution.py:594
  27.5 3.3 %collective-permute-start.8 = (f32[128,128]{1,0:T(8,128)S(1)}, f32[128,128]{1,0:T(8,128)S(1)}, u32[]{:S(2)}, u32[]{:S(2)}) collective-permute-start(f32[128,128]{1,0:T(8,128)S(1)} %add.18), channel_id=1, source_target_pairs={{0,2},{1,3},{2,0},{3,1},{4,6},{5,7},{6,4},{7,5},{8,10},{9,11},{10,... | collective-permute-start | bytes 196616 | tf_op jit(solution)/shard_map/ppermute | solution.py:594
  30.8 0.0 collective-permute-done.5.boundary_ref
  30.8 1.6 %outputs.1 = bf16[8,64,256]{2,1,0:T(8,128)(2,1)} custom-call(bf16[8,64,256]{2,1,0:T(8,128)(2,1)S(1)} %get-tuple-element.37.input_ref, bf16[512,256]{1,0:T(8,128)(2,1)S(1)} %get-tuple-element.52.hidden_ref, bf16[512,128]{1,0:T(8,128)(2,1)S(1)} %boundary.1.own_boundary_ref, bf16[512,128]{1,0:T(8,128)(2,1)S(1)} %collective-permute-done.5.boundary_ref, ...), custom_call_target="tpu_custom_call" | custom-call | bytes 7200000 | tf_op jit(solution)/shard_map/outputs/pallas_call | solution.py:578
  32.4 0.6 %collective-permute-done.8 = f32[128,128]{1,0:T(8,128)S(1)} collective-permute-done((f32[128,128]{1,0:T(8,128)S(1)}, f32[128,128]{1,0:T(8,128)S(1)}, u32[]{:S(2)}, u32[]{:S(2)}) %collective-permute-start.8) | collective-permute-done | bytes 65568 | tf_op jit(solution)/shard_map/ppermute | solution.py:594
  33.0 0.1 collective-permute-start.9
  33.1 1.2 %collective-permute-done.9.other_ref = f32[128,128]{1,0:T(8,128)S(1)} collective-permute-done((f32[128,128]{1,0:T(8,128)S(1)}, f32[128,128]{1,0:T(8,128)S(1)}, u32[]{:S(2)}, u32[]{:S(2)}) %collective-permute-start.9) | collective-permute-done | bytes 65568 | tf_op jit(solution)/shard_map/ppermute | solution.py:594
  34.4 0.7 %final.1 = (f32[2,64,128]{2,1,0:T(8,128)}, f32[1,128]{1,0:T(1,128)}, f32[3,64,64]{2,1,0:T(8,128)}, f32[1,64]{1,0:T(1,128)}) custom-call(f32[128,128]{1,0:T(8,128)S(1)} %add.19.kept_ref, f32[128,128]{1,0:T(8,128)S(1)} %collective-permute-done.9.other_ref), custom_call_target="tpu_custom_call" | custom-call | bytes 3600000 | tf_op jit(solution)/shard_map/final/pallas_call | solution.py:578
  (5 shorter events, 0.0 us)
Async XLA Ops:
  2.6 8.4 %collective-permute-start = (bf16[544,128]{1,0:T(8,128)(2,1)S(1)}, bf16[544,128]{1,0:T(8,128)(2,1)S(1)}, u32[]{:S(2)}, u32[]{:S(2)}) collective-permute-start(bf16[544,128]{1,0:T(8,128)(2,1)S(1)} %get-tuple-element.38.own_packed_ref), channel_id=1, source_target_pairs={{0,4},{4,0},{1,5},{5,1},{2,6},{6,2},{3,7},{7,3},{8,12},{12,8},{9,1... | collective-permute-start | bytes 417800 | tf_op jit(solution)/shard_map/ppermute | solution.py:594
  5.7 5.4 %collective-permute-start.1 = (bf16[2,64,256]{2,1,0:T(8,128)(2,1)S(1)}, bf16[2,64,256]{2,1,0:T(8,128)(2,1)S(1)}, u32[]{:S(2)}, u32[]{:S(2)}) collective-permute-start(bf16[2,64,256]{2,1,0:T(8,128)(2,1)S(1)} %get-tuple-element.39), channel_id=1, source_target_pairs={{0,1},{1,2},{2,3},{4,5},{5,6},{6,7},{8,9},{9,10},{10,11},{12,13},{... | collective-permute-start | bytes 196616 | tf_op jit(solution)/shard_map/ppermute | solution.py:17
  12.5 1.3 %collective-permute-start.2 = (f32[128,128]{1,0:T(8,128)S(1)}, f32[128,128]{1,0:T(8,128)S(1)}, u32[]{:S(2)}, u32[]{:S(2)}) collective-permute-start(f32[128,128]{1,0:T(8,128)S(1)} %get-tuple-element.51), channel_id=1, source_target_pairs={{0,8},{8,0},{16,24},{24,16},{1,9},{9,1},{17,25},{25,17},{2,10},{10... | collective-permute-start | bytes 196616 | tf_op jit(solution)/shard_map/ppermute | solution.py:594
  13.8 4.3 %collective-permute-start.3 = (f32[128,128]{1,0:T(8,128)S(1)}, f32[128,128]{1,0:T(8,128)S(1)}, u32[]{:S(2)}, u32[]{:S(2)}) collective-permute-start(f32[128,128]{1,0:T(8,128)S(1)} %add.15), channel_id=1, source_target_pairs={{0,16},{8,24},{16,0},{24,8},{1,17},{9,25},{17,1},{25,9},{2,18},{10... | collective-permute-start | bytes 196616 | tf_op jit(solution)/shard_map/ppermute | solution.py:594
  18.1 5.0 %collective-permute-start.4 = (f32[128,128]{1,0:T(8,128)S(1)}, f32[128,128]{1,0:T(8,128)S(1)}, u32[]{:S(2)}, u32[]{:S(2)}) collective-permute-start(f32[128,128]{1,0:T(8,128)S(1)} %add.16), channel_id=1, source_target_pairs={{0,4},{4,0},{1,5},{5,1},{2,6},{6,2},{3,7},{7,3},{8,12},{12,8},{9,1... | collective-permute-start | bytes 196616 | tf_op jit(solution)/shard_map/ppermute | solution.py:594
  18.7 7.2 %collective-permute-start.6 = (bf16[2,64,256]{2,1,0:T(8,128)(2,1)S(1)}, bf16[2,64,256]{2,1,0:T(8,128)(2,1)S(1)}, u32[]{:S(2)}, u32[]{:S(2)}) collective-permute-start(bf16[2,64,256]{2,1,0:T(8,128)(2,1)S(1)} %get-tuple-element.57), channel_id=1, source_target_pairs={{0,3},{1,0},{2,1},{3,2},{4,7},{5,4},{6,5},{7,6},{8,11},{9,8},{10,9... | collective-permute-start | bytes 196616 | tf_op jit(solution)/shard_map/ppermute | solution.py:599
  23.1 4.3 %collective-permute-start.7 = (f32[128,128]{1,0:T(8,128)S(1)}, f32[128,128]{1,0:T(8,128)S(1)}, u32[]{:S(2)}, u32[]{:S(2)}) collective-permute-start(f32[128,128]{1,0:T(8,128)S(1)} %add.17), channel_id=1, source_target_pairs={{0,1},{1,0},{2,3},{3,2},{4,5},{5,4},{6,7},{7,6},{8,9},{9,8},{10,11... | collective-permute-start | bytes 196616 | tf_op jit(solution)/shard_map/ppermute | solution.py:594
  25.4 5.4 %collective-permute-start.5 = (bf16[512,128]{1,0:T(8,128)(2,1)S(1)}, bf16[512,128]{1,0:T(8,128)(2,1)S(1)}, u32[]{:S(2)}, u32[]{:S(2)}) collective-permute-start(bf16[512,128]{1,0:T(8,128)(2,1)S(1)} %boundary.1.own_boundary_ref), channel_id=1, source_target_pairs={{0,4},{4,0},{1,5},{5,1},{2,6},{6,2},{3,7},{7,3},{8,12},{12,8},{9,1... | collective-permute-start | bytes 393224 | tf_op jit(solution)/shard_map/ppermute | solution.py:594
  27.5 5.5 %collective-permute-start.8 = (f32[128,128]{1,0:T(8,128)S(1)}, f32[128,128]{1,0:T(8,128)S(1)}, u32[]{:S(2)}, u32[]{:S(2)}) collective-permute-start(f32[128,128]{1,0:T(8,128)S(1)} %add.18), channel_id=1, source_target_pairs={{0,2},{1,3},{2,0},{3,1},{4,6},{5,7},{6,4},{7,5},{8,10},{9,11},{10,... | collective-permute-start | bytes 196616 | tf_op jit(solution)/shard_map/ppermute | solution.py:594
  33.0 1.3 %collective-permute-start.9 = (f32[128,128]{1,0:T(8,128)S(1)}, f32[128,128]{1,0:T(8,128)S(1)}, u32[]{:S(2)}, u32[]{:S(2)}) collective-permute-start(f32[128,128]{1,0:T(8,128)S(1)} %add.19.kept_ref), channel_id=1, source_target_pairs={{0,8},{8,0},{16,24},{24,16},{1,9},{9,1},{17,25},{25,17},{2,10},{10... | collective-permute-start | bytes 196616 | tf_op jit(solution)/shard_map/ppermute | solution.py:594

commit v3 on v2

--- a/solution.py
+++ b/solution.py
@@ -1,4 +1,5 @@
 import functools
+import itertools
 import math
 
 import jax
@@ -201,6 +202,7 @@
 
 
 BF16 = jnp.bfloat16
+AXES = ("dp", "space", "tm")
 F32 = jnp.float32
 NT = (((1,), (1,)), ((), ()))
 VMEM_BYTES = 24 * 1024 * 1024
@@ -233,17 +235,18 @@
     return fold(mm(left[:half], right), mm(left[half:], right))
 
 
-def unfold_nt(folded, right):
-    lower, upper = halves(right)
-    return jnp.concatenate([mm_nt(folded, lower), mm_nt(folded, upper)], 0)
-
-
 def link_matrix(packed):
     packed = packed.astype(F32)
     turned = pltpu.roll(packed, packed.shape[1] // 2, 1)
-    low, high = halves(packed)
-    turned_low, turned_high = halves(turned)
-    return jnp.concatenate([low, turned_low, turned_high, high], 0).astype(BF16)
+    blank = jnp.zeros_like(packed)
+    return jnp.concatenate([halves(turned)[1], halves(packed)[1], blank, blank], 0).astype(BF16)
+
+
+def turned_link_matrix(packed):
+    packed = packed.astype(F32)
+    turned = pltpu.roll(packed, packed.shape[1] // 2, 1)
+    blank = jnp.zeros_like(packed)
+    return jnp.concatenate([blank, blank, halves(packed)[0], halves(turned)[0]], 0).astype(BF16)
 
 
 def column(row):
@@ -299,7 +302,7 @@
     )
     other = 1 - lax.axis_index("space")
     sensors = grad_ref.shape[1]
-    half_rows = grad_ref.shape[0] // 2
+    rows_count = grad_ref.shape[0]
     slot_count = rows_ref.shape[2]
     upper = upper_lanes((tile, tile)).astype(jnp.int32)
     copies[0].wait()
@@ -321,7 +324,7 @@
     chosen_ref[...] = chosen.astype(BF16)
     turned = jnp.transpose(chosen)[:slot_count].astype(BF16)
     halo = halo_ref[...]
-    packed_ref[2 * half_rows :, :] = times_halves(turned, halo).astype(BF16)
+    packed_ref[rows_count:, :] = times_halves(turned, halo).astype(BF16)
     copies[4].wait()
     for r in range(row_blocks):
         sums = [jnp.zeros((tile, tile), F32), jnp.zeros((tile, tile), F32)]
@@ -331,11 +334,9 @@
                 share = jnp.where(cols_ref[r, k] == block, 1.0, 0.0).astype(F32)
                 sums[block] = sums[block] + item * share
         own_ref[r * tile : (r + 1) * tile, :] = jnp.concatenate(sums, 1).astype(BF16)
+    both = fold(halo, mm(own_ref[...], halo).astype(BF16))
     copies[5].wait()
-    grad = grad_ref[...]
-    packed_ref[:half_rows, :] = times_halves(grad, halo).astype(BF16)
-    first = mm(grad, own_ref[...]).astype(BF16)
-    packed_ref[half_rows : 2 * half_rows, :] = times_halves(first, halo).astype(BF16)
+    packed_ref[:rows_count, :] = mm(grad_ref[...], both).astype(BF16)
     copies[6].wait()
 
 
@@ -434,24 +435,24 @@
     steps, wide, sensors = back_ref.shape
     chans = wide // 2
     rows = steps * chans
-    half_rows = rows // 2
     border_rows = DILATION_SIZE * chans
     border_span = DILATION_SIZE * sensors
     core = lax.axis_index("dp") % 2
     own = own_ref[...]
     chosen = chosen_ref[...]
-    link = link_matrix(packed_ref[rows:, :])
-    one = (near_ref[...] + unfold_nt(packed_ref[:half_rows, :], chosen)).astype(BF16)
-    second = packed_ref[half_rows:rows, :].astype(F32) + mm(own_packed_ref[:half_rows, :], link)
-    two = (mm(one, own) + unfold_nt(second.astype(BF16), chosen)).astype(BF16)
+    chosen_low, chosen_high = halves(chosen)
+    packed = packed_ref[:rows, :]
+    one = (near_ref[...] + mm_nt(packed, chosen_low)).astype(BF16)
+    second = packed.astype(F32) + mm(own_packed_ref[:rows, :], link_matrix(packed_ref[rows:, :]))
+    two = (mm(one, own) + mm_nt(second.astype(BF16), chosen_high)).astype(BF16)
     one_scr[...] = one
     two_scr[...] = two
     bias = column(bias_ref[...])
-    has_earlier = lax.axis_index("tm") > 0
+    place = lax.axis_index("tm")
     hidden_ref[border_rows:, :] = hidden_old_ref[border_rows:, :]
     for t in range(DILATION_SIZE):
         earlier = border_ref[t]
-        earlier = jnp.where(has_earlier, earlier, jnp.zeros_like(earlier))
+        earlier = jnp.where(place > 0, earlier, jnp.zeros_like(earlier))
         window = jnp.concatenate([earlier, input_ref[t]], 0)
         preact = mm(turned_taps_ref[...], window) + bias
         gate_step(t, earlier, input_ref, preact, hidden_ref, slopes_ref, right_ref)
@@ -477,28 +478,24 @@
     sums = conv[wide : wide + 8]
     conv = conv[:wide, :wide]
     zero, first, second = [mixes[k * chans : (k + 1) * chans] for k in range(3)]
-    tail = jnp.concatenate([sums[:, wide:], jnp.zeros((8, chans), F32)], 1)
-    biases = jnp.concatenate(
-        [
-            pltpu.roll(tail, chans, 1),
-            pltpu.roll(sums[:, :wide], chans, 1),
-            sums[:, :wide],
-            jnp.zeros((chans - 24, wide), F32),
-        ],
-        0,
-    )
-    mixes = jnp.concatenate([fold(zero, first), fold(second, biases)], 0)
+    blank = jnp.zeros((chans, wide), F32)
+    mixes = jnp.concatenate([fold(zero, first), fold(second, blank)], 0)
+    mix_sums = jnp.concatenate([sums[:, wide:], blank[:8, :chans]], 1)
+    conv = jnp.concatenate([conv, sums[:, :wide], blank[:8]], 0)
+    mixes = jnp.concatenate([mixes, mix_sums, blank[:8]], 0)
     kept_ref[...] = jnp.where(core == 0, conv, mixes)
     given_ref[...] = jnp.where(core == 0, mixes, conv)
 
 
+def boundary_rows(hidden, own, chosen):
+    chosen_low, chosen_high = halves(chosen)
+    hop = mm_nt(hidden, own).astype(BF16)
+    return (mm(hidden, chosen_low) + mm(hop, chosen_high)).astype(BF16)
+
+
 def boundary_kernel(hidden_ref, own_ref, chosen_ref, boundary_ref):
-    hidden = hidden_ref[...]
-    chosen = chosen_ref[...]
-    hop = mm_nt(hidden, own_ref[...]).astype(BF16)
-    half_rows = hidden.shape[0] // 2
-    boundary_ref[:half_rows, :] = times_halves(hidden, chosen).astype(BF16)
-    boundary_ref[half_rows:, :] = times_halves(hop, chosen).astype(BF16)
+    hidden = hidden_ref[: boundary_ref.shape[0], :]
+    boundary_ref[...] = boundary_rows(hidden, own_ref[...], chosen_ref[...])
 
 
 def outputs_kernel(
@@ -515,14 +512,16 @@
 ):
     steps, chans, sensors = input_ref.shape
     rows = steps * chans
-    half_rows = rows // 2
     own = own_ref[...]
     halo = halo_ref[...]
-    link = link_matrix(packed_ref[rows:, :])
+    halo_low, halo_high = halves(halo)
+    link = turned_link_matrix(packed_ref[rows:, :])
     hidden = hidden_ref[...]
-    one = (mm_nt(hidden, own) + unfold_nt(boundary_ref[:half_rows, :], halo)).astype(BF16)
-    far = boundary_ref[half_rows:, :].astype(F32) + mm_nt(own_boundary_ref[:half_rows, :], link)
-    two = (mm_nt(one, own) + unfold_nt(far.astype(BF16), halo)).astype(BF16)
+    own_boundary = own_boundary_ref[...]
+    boundary = boundary_ref[...]
+    one = (mm_nt(hidden, own) + mm_nt(boundary, halo_low)).astype(BF16)
+    far = (boundary.astype(F32) + mm_nt(own_boundary, link)).astype(BF16)
+    two = (mm_nt(one, own) + mm_nt(far, halo_high)).astype(BF16)
     bias = column(bias_ref[...])
     for t in range(steps):
         at = slice(t * chans, (t + 1) * chans)
@@ -554,15 +553,14 @@
     conv = jnp.where(core == 0, kept, other)
     mixes = jnp.where(core == 0, other, kept)
     chans = conv.shape[1] // 2
+    wide = 2 * chans
     conv_w_ref[0] = conv[:chans]
-    conv_w_ref[1] = conv[chans:]
+    conv_w_ref[1] = conv[chans:wide]
     mix_w_ref[0] = mixes[:chans, :chans]
     mix_w_ref[1] = pltpu.roll(mixes[:chans], chans, 1)[:, :chans]
-    mix_w_ref[2] = mixes[chans:, :chans]
-    biases = mixes[chans : chans + 24]
-    turned = pltpu.roll(biases, chans, 1)
-    mix_b_ref[...] = turned[0:1, :chans]
-    conv_b_ref[...] = fold(turned[8:9], biases[16:17])
+    mix_w_ref[2] = mixes[chans:wide, :chans]
+    conv_b_ref[...] = (conv[wide : wide + 8] + conv[wide + 8 :])[:1]
+    mix_b_ref[...] = (mixes[wide : wide + 8] + mixes[wide + 8 :])[:1, :chans]
 
 
 VMEM = pl.BlockSpec(memory_space=pltpu.VMEM)
@@ -599,8 +597,45 @@
     return lax.ppermute(value, axis, [(source, (source + steps) % count) for source in range(count)])
 
 
+def flip(value, mask):
+    sizes = [lax.axis_size(axis) for axis in AXES]
+    places = list(itertools.product(*[range(size) for size in sizes]))
+    index = {place: number for number, place in enumerate(places)}
+    pairs = [
+        (index[place], index[tuple(part ^ bit for part, bit in zip(place, mask))])
+        for place in places
+    ]
+    return lax.ppermute(value, AXES, pairs)
+
+
+def groups():
+    dp, space, tm = [bits(lax.axis_size(axis)) for axis in AXES]
+    first = [(bit, 0, 0) for bit in dp[1:]]
+    second = [(0, bit, 0) for bit in space]
+    third = [(0, 0, bit) for bit in tm]
+    return [closure(masks) for masks in (first + third[:1], second + third[1:]) if masks]
+
+
+def closure(masks):
+    found = [(0, 0, 0)]
+    for mask in masks:
+        found = found + [tuple(left ^ right for left, right in zip(item, mask)) for item in found]
+    return found[1:]
+
+
 def bits(count):
     return [1 << place for place in range(count.bit_length() - 1)]
+
+
+def to_bf16(value):
+    return lax.reduce_precision(value, exponent_bits=8, mantissa_bits=7)
+
+
+def round_sums(sums):
+    end = sums.shape[0]
+    high = sums[end - 16 : end - 8]
+    rest = jnp.pad(high - to_bf16(high), ((end - 8, 0), (0, 0)))
+    return to_bf16(sums + rest)
 
 
 def after(value, *earlier):
@@ -615,6 +650,7 @@
     half_rows = rows // 2
     wide = 2 * chans
     shape = jax.ShapeDtypeStruct
+    border_rows = DILATION_SIZE * chans
     grad_flat = sample_grad.reshape(rows, sensors)
     taps = jnp.transpose(conv_w, (0, 2, 1))
     packed, own, halo, chosen, grad, tail = call(
@@ -640,7 +676,7 @@
         micros=2.0,
     )
     packed_far = swap(packed, "space", 1)
-    border = from_behind(tail, "tm", 1)
+    border = shift(tail, "tm", 1)
     hidden_late, slopes, right, near, kept_input, kept_taps, turned_taps, bias, mix, mixing, mix_bias = call(
         forward_kernel,
         "forward",
@@ -676,8 +712,8 @@
         "backward",
         [VMEM] * 15,
         (
-            shape((wide, wide), F32),
-            shape((wide, wide), F32),
+            shape((wide + 16, wide), F32),
+            shape((wide + 16, wide), F32),
             shape((steps, wide, sensors), BF16),
             shape((DILATION_SIZE, chans, sensors), BF16),
             shape((rows, sensors), BF16),
@@ -709,45 +745,52 @@
         micros=2.0,
     )
     total = kept + swap(given, "dp", 1)
-    rounds = (
-        [("dp", bit) for bit in bits(lax.axis_size("dp"))[1:]]
-        + [("space", bit) for bit in bits(lax.axis_size("space"))]
-        + [("tm", bit) for bit in bits(lax.axis_size("tm"))]
-    )
+    rounds = groups()
     early_far = shift(early, "tm", -1)
-    for index, (axis, bit) in enumerate(rounds):
-        if index == 2:
-            boundary = call(
-                boundary_kernel,
-                "boundary",
-                [VMEM] * 3,
-                shape((rows, wide), BF16),
-                (after(hidden, total), own, chosen),
-                micros=0.4,
-            )
-            boundary_far = swap(boundary, "space", 1)
-        arrived = swap(total, axis, bit)
-        if index == 2:
-            grad_inputs = call(
-                input_grad_kernel,
-                "input_grad",
-                [VMEM] * 4,
-                shape(sample_grad.shape, BF16),
-                (grad, back, early_far, kept_taps),
-                micros=1.2,
-            )
-            arrived = after(arrived, grad_inputs)
-        if index == 3:
-            outputs = call(
-                outputs_kernel,
-                "outputs",
-                [VMEM] * 9,
-                shape(sample_input.shape, BF16),
-                (kept_input, hidden, boundary, boundary_far, packed_far, own, halo, mix, mix_bias),
-                micros=2.0,
-            )
-            arrived = after(arrived, outputs)
-        total = total + arrived
+    boundary_first = call(
+        boundary_kernel,
+        "boundary",
+        [VMEM] * 3,
+        shape((rows, wide), BF16),
+        (hidden, own, chosen),
+        micros=0.3,
+    )
+    first_far = swap(boundary_first, "space", 1)
+    outputs = call(
+        outputs_kernel,
+        "outputs",
+        [VMEM] * 9,
+        shape(sample_input.shape, BF16),
+        (
+            kept_input,
+            hidden,
+            boundary_first,
+            first_far,
+            packed_far,
+            own,
+            halo,
+            mix,
+            mix_bias,
+        ),
+        micros=2.0,
+    )
+    grad_inputs = call(
+        input_grad_kernel,
+        "input_grad",
+        [VMEM] * 4,
+        shape(sample_grad.shape, BF16),
+        (grad, back, early_far, kept_taps),
+        micros=1.2,
+    )
+    ready = {-2: (first_far,), -1: (outputs, grad_inputs)}
+    for index, group in enumerate(rounds):
+        rounded = round_sums(total)
+        sent = rounded.astype(BF16)
+        parts = [rounded] + [flip(sent, mask).astype(F32) for mask in group]
+        parts[1] = after(parts[1], *ready.get(index - len(rounds), ()))
+        while len(parts) > 1:
+            parts = [left + right for left, right in zip(parts[::2], parts[1::2])]
+        total = parts[0]
     total_far = swap(total, "dp", 1)
     cell_count = (
         inputs.shape[0]

time: 35.3 us -> 31.6 us (0.90)
  starting transfers between devices: 18.8 us -> 15.4 us
    ppermute x8 -> x4, starting transfers between devices: 10.9 us -> 3.53 us  [swap(): lax.ppermute(value, axis, [(source, source ^ bit) for source in range(cou...]
    ppermute x8 -> x4, waiting for transfers between devices: 6.41 us -> 1.58 us  [swap(): lax.ppermute(value, axis, [(source, source ^ bit) for source in range(cou...]
    ppermute x1 -> x6, starting transfers between devices: 3.47 us -> 8.01 us  [flip(): return lax.ppermute(value, AXES, pairs)]
    ppermute x1 -> x2, waiting for transfers between devices: 0.01 us -> 3.06 us  [shift(): lax.ppermute(value, axis, [(source, (source + steps) % count) for source...]
    ppermute x1 -> x6, waiting for transfers between devices: 0.45 us -> 1.89 us  [flip(): return lax.ppermute(value, AXES, pairs)]
    ppermute x1 -> x2, starting transfers between devices: 4.39 us -> 3.91 us  [shift(): lax.ppermute(value, axis, [(source, (source + steps) % count) for source...]
  transfers between devices with their start and end apart: 10 -> 12, of which waited for: 6 -> 6; matrix products, arithmetic and copies ran while one was open for 0% -> 0% of each run, Pallas kernels for 13% -> 14%
where the time goes in v3:
time: 31.6 us; the launch traced here: 31.4 us
  starting transfers between devices  15.4 us (49%)
  Pallas kernels  8.61 us (27%)
  waiting for transfers between devices  6.53 us (21%)
  between operations  0.74 us (2%)
    pallas_call x7, Pallas kernels, call(): pl.pallas_call(kernel, out_shape=out_shape, in_specs=in_specs, out_specs=...  8.61 us
    ppermute x6, starting transfers between devices, flip(): return lax.ppermute(value, AXES, pairs)  8.01 us
    ppermute x2, starting transfers between devices, shift(): lax.ppermute(value, axis, [(source, (source + steps) % count) for source...  3.91 us
    ppermute x4, starting transfers between devices, swap(): lax.ppermute(value, axis, [(source, source ^ bit) for source in range(cou...  3.53 us
    ppermute x2, waiting for transfers between devices, shift(): lax.ppermute(value, axis, [(source, (source + steps) % count) for source...  3.06 us
    ppermute x6, waiting for transfers between devices, flip(): return lax.ppermute(value, AXES, pairs)  1.89 us
    ppermute x4, waiting for transfers between devices, swap(): lax.ppermute(value, axis, [(source, source ^ bit) for source in range(cou...  1.58 us
  transfers between devices with their start and end apart: 12, of which 6 were waited for; matrix products, arithmetic and copies ran while one was open for 0% of the time, Pallas kernels for 14%

profile of v3, /device:TPU:0, one launch (start us, length us, event | category | flops | bytes accessed | tf_op | source)
XLA Modules:
  0.0 31.4 jit_solution(2288236350706866260)
XLA Ops:
  0.6 1.9 %prepare.1 = (bf16[544,128]{1,0:T(8,128)(2,1)S(1)}, bf16[256,256]{1,0:T(8,128)(2,1)S(1)}, bf16[256,128]{1,0:T(8,128)(2,1)S(1)}, bf16[256,128]{1,0:T(8,128)(2,1)S...) custom-call(s32[2,8]{1,0:T(2,128)} %cols_hbm.1, s32[1,2]{1,0:T(1,128)} %counts_hbm.1, ...), custom_call_target="tpu_custom_call" | custom-call | bytes 7200000 | tf_op jit(solution)/shard_map/prepare/pallas_call | solution.py:576
  2.5 3.0 %collective-permute-start = (bf16[544,128]{1,0:T(8,128)(2,1)S(1)}, bf16[544,128]{1,0:T(8,128)(2,1)S(1)}, u32[]{:S(2)}, u32[]{:S(2)}) collective-permute-start(bf16[544,128]{1,0:T(8,128)(2,1)S(1)} %get-tuple-element.37.own_packed_ref), channel_id=1, source_target_pairs={{0,4},{4,0},{1,5},{5,1},{2,6},{6,2},{3,7},{7,3},{8,12},{12,8},{9,1... | collective-permute-start | bytes 417800 | tf_op jit(solution)/shard_map/ppermute | solution.py:592
  5.6 1.6 %collective-permute-start.1 = (bf16[2,64,256]{2,1,0:T(8,128)(2,1)S(1)}, bf16[2,64,256]{2,1,0:T(8,128)(2,1)S(1)}, u32[]{:S(2)}, u32[]{:S(2)}) collective-permute-start(bf16[2,64,256]{2,1,0:T(8,128)(2,1)S(1)} %get-tuple-element.38), channel_id=1, source_target_pairs={{0,1},{1,2},{2,3},{3,0},{4,5},{5,6},{6,7},{7,4},{8,9},{9,10},{10,1... | collective-permute-start | bytes 196616 | tf_op jit(solution)/shard_map/ppermute | solution.py:597
  7.1 1.4 %forward.1 = (bf16[512,256]{1,0:T(8,128)(2,1)S(1)}, f32[8,128,256]{2,1,0:T(8,128)S(1)}, bf16[272,2048]{1,0:T(8,128)(2,1)S(1)}, f32[512,256]{1,0:T(8,128)S(1)}, b...) custom-call(bf16[8,64,256]{2,1,0:T(8,128)(2,1)} %bitcast.11, ...), custom_call_target="tpu_custom_call" | custom-call | bytes 5400000 | tf_op jit(solution)/shard_map/forward/pallas_call | solution.py:576
  8.6 3.1 %collective-permute-done.1.border_ref = bf16[2,64,256]{2,1,0:T(8,128)(2,1)S(1)} collective-permute-done((bf16[2,64,256]{2,1,0:T(8,128)(2,1)S(1)}, bf16[2,64,256]{2,1,0:T(8,128)(2,1)S(1)}, u32[]{:S(2)}, u32[]{:S(2)}) %collective-permute-start.1) | collective-permute-done | bytes 65568 | tf_op jit(solution)/shard_map/ppermute | solution.py:597
  11.6 0.0 collective-permute-done.packed_ref
  11.6 1.5 %backward.1 = (f32[144,128]{1,0:T(8,128)S(1)}, f32[144,128]{1,0:T(8,128)S(1)}, bf16[8,128,256]{2,1,0:T(8,128)(2,1)S(1)}, bf16[2,64,256]{2,1,0:T(8,128)(2,1)S(1)}, bf16[512,256]{1,0:T(8,128)(2,1)S(1)}) custom-call(bf16[512,256]{1,0:T(8,128)(2,1)S(1)} %get-tuple-element.34.grad_ref, bf16[544,128]{1,0:T(8,128)(2,1)S(1)} %get-tuple-element.37.own_packed_ref, ...), custom_call_target="tpu_custom_call" | custom-call | bytes 7200000 | tf_op jit(solution)/shard_map/backward/pallas_call | solution.py:576
  13.1 0.1 collective-permute-start.4
  13.2 0.6 %boundary.1.own_boundary_ref = bf16[512,128]{1,0:T(8,128)(2,1)S(1)} custom-call(bf16[512,256]{1,0:T(8,128)(2,1)S(1)} %get-tuple-element.48.hidden_ref, bf16[256,256]{1,0:T(8,128)(2,1)S(1)} %get-tuple-element.35.own_ref, bf16[256,128]{1,0:T(8,128)(2,1)S(1)} %get-tuple-element.39.chosen_ref), custom_call_target="tpu_custom_call" | custom-call | bytes 1080000 | tf_op jit(solution)/shard_map/boundary/pallas_call | solution.py:576
  13.8 0.4 %collective-permute-start.2 = (bf16[512,128]{1,0:T(8,128)(2,1)S(1)}, bf16[512,128]{1,0:T(8,128)(2,1)S(1)}, u32[]{:S(2)}, u32[]{:S(2)}) collective-permute-start(bf16[512,128]{1,0:T(8,128)(2,1)S(1)} %boundary.1.own_boundary_ref), channel_id=1, source_target_pairs={{0,4},{4,0},{1,5},{5,1},{2,6},{6,2},{3,7},{7,3},{8,12},{12,8},{9,1... | collective-permute-start | bytes 393224 | tf_op jit(solution)/shard_map/ppermute | solution.py:592
  14.1 0.3 %collective-permute-done.4 = f32[144,128]{1,0:T(8,128)S(1)} collective-permute-done((f32[144,128]{1,0:T(8,128)S(1)}, f32[144,128]{1,0:T(8,128)S(1)}, u32[]{:S(2)}, u32[]{:S(2)}) %collective-permute-start.4) | collective-permute-done | bytes 73760 | tf_op jit(solution)/shard_map/ppermute | solution.py:592
  14.5 1.6 %collective-permute-start.5 = (bf16[144,128]{1,0:T(8,128)(2,1)S(1)}, bf16[144,128]{1,0:T(8,128)(2,1)S(1)}, u32[]{:S(2)}, u32[]{:S(2)}) collective-permute-start(bf16[144,128]{1,0:T(8,128)(2,1)S(1)} %fusion), channel_id=1, source_target_pairs={{0,16},{1,17},{2,18},{3,19},{4,20},{5,21},{6,22},{7,23},{8,24},{9,... | collective-permute-start | bytes 110600 | tf_op jit(solution)/shard_map/ppermute | solution.py:608
  16.1 0.3 collective-permute-start.7
  16.3 1.7 %collective-permute-start.6 = (bf16[144,128]{1,0:T(8,128)(2,1)S(1)}, bf16[144,128]{1,0:T(8,128)(2,1)S(1)}, u32[]{:S(2)}, u32[]{:S(2)}) collective-permute-start(bf16[144,128]{1,0:T(8,128)(2,1)S(1)} %fusion), channel_id=1, source_target_pairs={{0,1},{1,0},{2,3},{3,2},{4,5},{5,4},{6,7},{7,6},{8,9},{9,8},{10,11... | collective-permute-start | bytes 110600 | tf_op jit(solution)/shard_map/ppermute | solution.py:608
  18.1 2.3 %collective-permute-start.3 = (bf16[2,64,256]{2,1,0:T(8,128)(2,1)S(1)}, bf16[2,64,256]{2,1,0:T(8,128)(2,1)S(1)}, u32[]{:S(2)}, u32[]{:S(2)}) collective-permute-start(bf16[2,64,256]{2,1,0:T(8,128)(2,1)S(1)} %get-tuple-element.53), channel_id=1, source_target_pairs={{0,3},{1,0},{2,1},{3,2},{4,7},{5,4},{6,5},{7,6},{8,11},{9,8},{10,9... | collective-permute-start | bytes 196616 | tf_op jit(solution)/shard_map/ppermute | solution.py:597
  20.4 0.0 collective-permute-done.5
  20.4 0.0 collective-permute-done.2.boundary_ref
  20.4 0.6 %collective-permute-done.7 = bf16[144,128]{1,0:T(8,128)(2,1)S(1)} collective-permute-done((bf16[144,128]{1,0:T(8,128)(2,1)S(1)}, bf16[144,128]{1,0:T(8,128)(2,1)S(1)}, u32[]{:S(2)}, u32[]{:S(2)}) %collective-permute-start.7) | collective-permute-done | bytes 36896 | tf_op jit(solution)/shard_map/ppermute | solution.py:608
  21.0 0.0 collective-permute-done.6
  21.1 1.4 %collective-permute-start.8 = (bf16[144,128]{1,0:T(8,128)(2,1)S(1)}, bf16[144,128]{1,0:T(8,128)(2,1)S(1)}, u32[]{:S(2)}, u32[]{:S(2)}) collective-permute-start(bf16[144,128]{1,0:T(8,128)(2,1)S(1)} %fusion.1), channel_id=1, source_target_pairs={{0,4},{1,5},{2,6},{3,7},{4,0},{5,1},{6,2},{7,3},{8,12},{9,13},{10,... | collective-permute-start | bytes 110600 | tf_op jit(solution)/shard_map/ppermute | solution.py:608
  22.5 2.0 %collective-permute-start.10 = (bf16[144,128]{1,0:T(8,128)(2,1)S(1)}, bf16[144,128]{1,0:T(8,128)(2,1)S(1)}, u32[]{:S(2)}, u32[]{:S(2)}) collective-permute-start(bf16[144,128]{1,0:T(8,128)(2,1)S(1)} %fusion.1), channel_id=1, source_target_pairs={{0,6},{1,7},{2,4},{3,5},{4,2},{5,3},{6,0},{7,1},{8,14},{9,15},{10,... | collective-permute-start | bytes 110600 | tf_op jit(solution)/shard_map/ppermute | solution.py:608
  24.5 1.1 %collective-permute-start.9 = (bf16[144,128]{1,0:T(8,128)(2,1)S(1)}, bf16[144,128]{1,0:T(8,128)(2,1)S(1)}, u32[]{:S(2)}, u32[]{:S(2)}) collective-permute-start(bf16[144,128]{1,0:T(8,128)(2,1)S(1)} %fusion.1), channel_id=1, source_target_pairs={{0,2},{1,3},{2,0},{3,1},{4,6},{5,7},{6,4},{7,5},{8,10},{9,11},{10,... | collective-permute-start | bytes 110600 | tf_op jit(solution)/shard_map/ppermute | solution.py:608
  25.5 0.0 collective-permute-done.3.early_ref
  25.5 1.0 %input_grad.1 = bf16[8,64,256]{2,1,0:T(8,128)(2,1)} custom-call(bf16[512,256]{1,0:T(8,128)(2,1)S(1)} %get-tuple-element.34.grad_ref, bf16[8,128,256]{2,1,0:T(8,128)(2,1)S(1)} %get-tuple-element.52.back_ref, bf16[2,64,256]{2,1,0:T(8,128)(2,1)S(1)} %collective-permute-done.3.early_ref, bf16[2,64,128]{2,1,0:T(8,128)(2,1)S(1)} %get-tuple-element.41.taps_ref), custom_call_target="tpu_custom_call" | custom-call | bytes 4320000 | tf_op jit(solution)/shard_map/input_grad/pallas_call | solution.py:576
  26.5 1.5 %outputs.1 = bf16[8,64,256]{2,1,0:T(8,128)(2,1)} custom-call(bf16[8,64,256]{2,1,0:T(8,128)(2,1)S(1)} %get-tuple-element.36.input_ref, bf16[512,256]{1,0:T(8,128)(2,1)S(1)} %get-tuple-element.48.hidden_ref, bf16[512,128]{1,0:T(8,128)(2,1)S(1)} %boundary.1.own_boundary_ref, bf16[512,128]{1,0:T(8,128)(2,1)S(1)} %collective-permute-done.2.boundary_ref, ...), custom_call_target="tpu_custom_call" | custom-call | bytes 7200000 | tf_op jit(solution)/shard_map/outputs/pallas_call | solution.py:576
  28.1 0.0 collective-permute-done.8
  28.1 0.2 collective-permute-done.10
  28.2 1.1 %collective-permute-done.9 = bf16[144,128]{1,0:T(8,128)(2,1)S(1)} collective-permute-done((bf16[144,128]{1,0:T(8,128)(2,1)S(1)}, bf16[144,128]{1,0:T(8,128)(2,1)S(1)}, u32[]{:S(2)}, u32[]{:S(2)}) %collective-permute-start.9) | collective-permute-done | bytes 36896 | tf_op jit(solution)/shard_map/ppermute | solution.py:608
  29.4 0.1 collective-permute-start.11
  29.4 1.3 %collective-permute-done.11.other_ref = f32[144,128]{1,0:T(8,128)S(1)} collective-permute-done((f32[144,128]{1,0:T(8,128)S(1)}, f32[144,128]{1,0:T(8,128)S(1)}, u32[]{:S(2)}, u32[]{:S(2)}) %collective-permute-start.11) | collective-permute-done | bytes 73760 | tf_op jit(solution)/shard_map/ppermute | solution.py:592
  30.7 0.7 %final.1 = (f32[2,64,128]{2,1,0:T(8,128)}, f32[1,128]{1,0:T(1,128)}, f32[3,64,64]{2,1,0:T(8,128)}, f32[1,64]{1,0:T(1,128)}) custom-call(f32[144,128]{1,0:T(8,128)S(1)} %add_add_fusion.kept_ref, f32[144,128]{1,0:T(8,128)S(1)} %collective-permute-done.11.other_ref), custom_call_target="tpu_custom_call" | custom-call | bytes 3600000 | tf_op jit(solution)/shard_map/final/pallas_call | solution.py:576
  (9 shorter events, 0.1 us)
Async XLA Ops:
  2.5 9.1 %collective-permute-start = (bf16[544,128]{1,0:T(8,128)(2,1)S(1)}, bf16[544,128]{1,0:T(8,128)(2,1)S(1)}, u32[]{:S(2)}, u32[]{:S(2)}) collective-permute-start(bf16[544,128]{1,0:T(8,128)(2,1)S(1)} %get-tuple-element.37.own_packed_ref), channel_id=1, source_target_pairs={{0,4},{4,0},{1,5},{5,1},{2,6},{6,2},{3,7},{7,3},{8,12},{12,8},{9,1... | collective-permute-start | bytes 417800 | tf_op jit(solution)/shard_map/ppermute | solution.py:592
  5.6 6.1 %collective-permute-start.1 = (bf16[2,64,256]{2,1,0:T(8,128)(2,1)S(1)}, bf16[2,64,256]{2,1,0:T(8,128)(2,1)S(1)}, u32[]{:S(2)}, u32[]{:S(2)}) collective-permute-start(bf16[2,64,256]{2,1,0:T(8,128)(2,1)S(1)} %get-tuple-element.38), channel_id=1, source_target_pairs={{0,1},{1,2},{2,3},{3,0},{4,5},{5,6},{6,7},{7,4},{8,9},{9,10},{10,1... | collective-permute-start | bytes 196616 | tf_op jit(solution)/shard_map/ppermute | solution.py:597
  13.1 1.3 %collective-permute-start.4 = (f32[144,128]{1,0:T(8,128)S(1)}, f32[144,128]{1,0:T(8,128)S(1)}, u32[]{:S(2)}, u32[]{:S(2)}) collective-permute-start(f32[144,128]{1,0:T(8,128)S(1)} %get-tuple-element.55), channel_id=1, source_target_pairs={{0,8},{8,0},{16,24},{24,16},{1,9},{9,1},{17,25},{25,17},{2,10},{10... | collective-permute-start | bytes 221192 | tf_op jit(solution)/shard_map/ppermute | solution.py:592
  13.8 6.6 %collective-permute-start.2 = (bf16[512,128]{1,0:T(8,128)(2,1)S(1)}, bf16[512,128]{1,0:T(8,128)(2,1)S(1)}, u32[]{:S(2)}, u32[]{:S(2)}) collective-permute-start(bf16[512,128]{1,0:T(8,128)(2,1)S(1)} %boundary.1.own_boundary_ref), channel_id=1, source_target_pairs={{0,4},{4,0},{1,5},{5,1},{2,6},{6,2},{3,7},{7,3},{8,12},{12,8},{9,1... | collective-permute-start | bytes 393224 | tf_op jit(solution)/shard_map/ppermute | solution.py:592
  14.5 5.9 %collective-permute-start.5 = (bf16[144,128]{1,0:T(8,128)(2,1)S(1)}, bf16[144,128]{1,0:T(8,128)(2,1)S(1)}, u32[]{:S(2)}, u32[]{:S(2)}) collective-permute-start(bf16[144,128]{1,0:T(8,128)(2,1)S(1)} %fusion), channel_id=1, source_target_pairs={{0,16},{1,17},{2,18},{3,19},{4,20},{5,21},{6,22},{7,23},{8,24},{9,... | collective-permute-start | bytes 110600 | tf_op jit(solution)/shard_map/ppermute | solution.py:608
  16.1 5.0 %collective-permute-start.7 = (bf16[144,128]{1,0:T(8,128)(2,1)S(1)}, bf16[144,128]{1,0:T(8,128)(2,1)S(1)}, u32[]{:S(2)}, u32[]{:S(2)}) collective-permute-start(bf16[144,128]{1,0:T(8,128)(2,1)S(1)} %fusion), channel_id=1, source_target_pairs={{0,17},{1,16},{2,19},{3,18},{4,21},{5,20},{6,23},{7,22},{8,25},{9,... | collective-permute-start | bytes 110600 | tf_op jit(solution)/shard_map/ppermute | solution.py:608
  16.3 4.7 %collective-permute-start.6 = (bf16[144,128]{1,0:T(8,128)(2,1)S(1)}, bf16[144,128]{1,0:T(8,128)(2,1)S(1)}, u32[]{:S(2)}, u32[]{:S(2)}) collective-permute-start(bf16[144,128]{1,0:T(8,128)(2,1)S(1)} %fusion), channel_id=1, source_target_pairs={{0,1},{1,0},{2,3},{3,2},{4,5},{5,4},{6,7},{7,6},{8,9},{9,8},{10,11... | collective-permute-start | bytes 110600 | tf_op jit(solution)/shard_map/ppermute | solution.py:608
  18.1 7.5 %collective-permute-start.3 = (bf16[2,64,256]{2,1,0:T(8,128)(2,1)S(1)}, bf16[2,64,256]{2,1,0:T(8,128)(2,1)S(1)}, u32[]{:S(2)}, u32[]{:S(2)}) collective-permute-start(bf16[2,64,256]{2,1,0:T(8,128)(2,1)S(1)} %get-tuple-element.53), channel_id=1, source_target_pairs={{0,3},{1,0},{2,1},{3,2},{4,7},{5,4},{6,5},{7,6},{8,11},{9,8},{10,9... | collective-permute-start | bytes 196616 | tf_op jit(solution)/shard_map/ppermute | solution.py:597
  21.1 7.0 %collective-permute-start.8 = (bf16[144,128]{1,0:T(8,128)(2,1)S(1)}, bf16[144,128]{1,0:T(8,128)(2,1)S(1)}, u32[]{:S(2)}, u32[]{:S(2)}) collective-permute-start(bf16[144,128]{1,0:T(8,128)(2,1)S(1)} %fusion.1), channel_id=1, source_target_pairs={{0,4},{1,5},{2,6},{3,7},{4,0},{5,1},{6,2},{7,3},{8,12},{9,13},{10,... | collective-permute-start | bytes 110600 | tf_op jit(solution)/shard_map/ppermute | solution.py:608
  22.5 5.8 %collective-permute-start.10 = (bf16[144,128]{1,0:T(8,128)(2,1)S(1)}, bf16[144,128]{1,0:T(8,128)(2,1)S(1)}, u32[]{:S(2)}, u32[]{:S(2)}) collective-permute-start(bf16[144,128]{1,0:T(8,128)(2,1)S(1)} %fusion.1), channel_id=1, source_target_pairs={{0,6},{1,7},{2,4},{3,5},{4,2},{5,3},{6,0},{7,1},{8,14},{9,15},{10,... | collective-permute-start | bytes 110600 | tf_op jit(solution)/shard_map/ppermute | solution.py:608
  24.5 4.9 %collective-permute-start.9 = (bf16[144,128]{1,0:T(8,128)(2,1)S(1)}, bf16[144,128]{1,0:T(8,128)(2,1)S(1)}, u32[]{:S(2)}, u32[]{:S(2)}) collective-permute-start(bf16[144,128]{1,0:T(8,128)(2,1)S(1)} %fusion.1), channel_id=1, source_target_pairs={{0,2},{1,3},{2,0},{3,1},{4,6},{5,7},{6,4},{7,5},{8,10},{9,11},{10,... | collective-permute-start | bytes 110600 | tf_op jit(solution)/shard_map/ppermute | solution.py:608
  29.4 1.3 %collective-permute-start.11 = (f32[144,128]{1,0:T(8,128)S(1)}, f32[144,128]{1,0:T(8,128)S(1)}, u32[]{:S(2)}, u32[]{:S(2)}) collective-permute-start(f32[144,128]{1,0:T(8,128)S(1)} %add_add_fusion.kept_ref), channel_id=1, source_target_pairs={{0,8},{8,0},{16,24},{24,16},{1,9},{9,1},{17,25},{25,17},{2,10},{10... | collective-permute-start | bytes 221192 | tf_op jit(solution)/shard_map/ppermute | solution.py:592

commit v4 on v3

--- a/solution.py
+++ b/solution.py
@@ -235,11 +235,10 @@
     return fold(mm(left[:half], right), mm(left[half:], right))
 
 
-def link_matrix(packed):
+def link_rows(packed):
     packed = packed.astype(F32)
     turned = pltpu.roll(packed, packed.shape[1] // 2, 1)
-    blank = jnp.zeros_like(packed)
-    return jnp.concatenate([halves(turned)[1], halves(packed)[1], blank, blank], 0).astype(BF16)
+    return jnp.concatenate([halves(packed)[0], halves(turned)[0]], 0).astype(BF16)
 
 
 def turned_link_matrix(packed):
@@ -305,15 +304,14 @@
     rows_count = grad_ref.shape[0]
     slot_count = rows_ref.shape[2]
     upper = upper_lanes((tile, tile)).astype(jnp.int32)
-    copies[0].wait()
+    for copy in copies[:5]:
+        copy.wait()
     for r in range(row_blocks):
         far = adj_ref[r, own_slots].astype(F32)
         for k in range(own_slots + 1, slots):
             far = far + adj_ref[r, k].astype(F32)
         far = jnp.where(upper == other, far, pltpu.roll(far, tile // 2, 1))
         halo_ref[r * tile : (r + 1) * tile, :] = far.astype(BF16)
-    for copy in copies[1:4]:
-        copy.wait()
     rows = rows_ref[0, pl.ds(other, 1), :]
     rows = jnp.concatenate([rows, rows], 1)
     lanes = lax.broadcasted_iota(jnp.int32, (1, 2 * slot_count), 1)
@@ -325,7 +323,6 @@
     turned = jnp.transpose(chosen)[:slot_count].astype(BF16)
     halo = halo_ref[...]
     packed_ref[rows_count:, :] = times_halves(turned, halo).astype(BF16)
-    copies[4].wait()
     for r in range(row_blocks):
         sums = [jnp.zeros((tile, tile), F32), jnp.zeros((tile, tile), F32)]
         for k in range(own_slots):
@@ -366,10 +363,12 @@
     mix_b_hbm,
     grad_ref,
     own_ref,
+    chosen_ref,
     hidden_ref,
     slopes_ref,
     right_ref,
     near_ref,
+    spread_ref,
     input_ref,
     taps_ref,
     turned_taps_ref,
@@ -390,7 +389,19 @@
         sems,
     )
     steps, chans, sensors = input_ref.shape
-    near_ref[...] = mm(grad_ref[...], own_ref[...])
+    own = own_ref[...]
+    near = mm(grad_ref[...], own)
+    near_ref[:, :sensors] = near
+    near_ref[:, sensors:] = mm(near.astype(BF16), own)
+    turned = jnp.transpose(chosen_ref[...].astype(F32)).astype(BF16)
+    slot_count = turned.shape[0] // 2
+    spread_ref[:, :sensors] = jnp.where(
+        lax.broadcasted_iota(jnp.int32, turned.shape, 0) < slot_count,
+        turned,
+        jnp.zeros_like(turned),
+    )
+    spread_ref[:slot_count, sensors:] = mm(turned[:slot_count], own).astype(BF16)
+    spread_ref[slot_count:, sensors:] = turned[slot_count:]
     for copy in copies:
         copy.wait()
     mixing = jnp.transpose(mix_ref[...].reshape(3 * chans, chans).astype(F32))
@@ -410,11 +421,9 @@
     own_packed_ref,
     packed_ref,
     border_ref,
-    own_ref,
-    chosen_ref,
     near_ref,
+    spread_ref,
     input_ref,
-    taps_ref,
     turned_taps_ref,
     bias_ref,
     mixing_ref,
@@ -424,11 +433,9 @@
     kept_ref,
     given_ref,
     back_ref,
-    early_ref,
     hidden_ref,
     left_scr,
-    one_scr,
-    two_scr,
+    both_scr,
     slopes_ref,
     right_ref,
 ):
@@ -438,15 +445,12 @@
     border_rows = DILATION_SIZE * chans
     border_span = DILATION_SIZE * sensors
     core = lax.axis_index("dp") % 2
-    own = own_ref[...]
-    chosen = chosen_ref[...]
-    chosen_low, chosen_high = halves(chosen)
-    packed = packed_ref[:rows, :]
-    one = (near_ref[...] + mm_nt(packed, chosen_low)).astype(BF16)
-    second = packed.astype(F32) + mm(own_packed_ref[:rows, :], link_matrix(packed_ref[rows:, :]))
-    two = (mm(one, own) + mm_nt(second.astype(BF16), chosen_high)).astype(BF16)
-    one_scr[...] = one
-    two_scr[...] = two
+    linked = mm(link_rows(packed_ref[rows:, :]), spread_ref[:, :sensors]).astype(BF16)
+    blank = jnp.zeros_like(linked)
+    linked = jnp.concatenate([blank, linked], 1)
+    spread = jnp.concatenate([spread_ref[...], linked, jnp.zeros_like(linked)], 0)
+    packed = jnp.concatenate([packed_ref[:rows, :], own_packed_ref[:rows, :]], 1)
+    both_scr[...] = (near_ref[...] + mm(packed, spread)).astype(BF16)
     bias = column(bias_ref[...])
     place = lax.axis_index("tm")
     hidden_ref[border_rows:, :] = hidden_old_ref[border_rows:, :]
@@ -460,7 +464,9 @@
     for t in range(steps):
         at = slice(t * chans, (t + 1) * chans)
         span = slice(t * sensors, (t + 1) * sensors)
-        fields = jnp.concatenate([grad_ref[at, :], one_scr[at, :], two_scr[at, :]], 0)
+        fields = jnp.concatenate(
+            [grad_ref[at, :], both_scr[at, :sensors], both_scr[at, sensors:]], 0
+        )
         back_hidden = mm(mixing, fields)
         back_hidden = jnp.concatenate([back_hidden, back_hidden], 0)
         slopes = slopes_ref[t] if t < DILATION_SIZE else slopes_old_ref[t]
@@ -468,8 +474,6 @@
         back_ref[t] = back_pre
         left_scr[:wide, span] = back_pre
         left_scr[wide:, span] = fields
-        if t < DILATION_SIZE:
-            early_ref[t] = mm(taps_ref[0], back_pre).astype(BF16)
     ones = wide + 16
     conv = mm_nt(right_old_ref[:ones, border_span:], left_scr[: wide + chans, border_span:])
     conv = conv + mm_nt(right_ref[:ones, :], left_scr[: wide + chans, :border_span])
@@ -491,6 +495,11 @@
     chosen_low, chosen_high = halves(chosen)
     hop = mm_nt(hidden, own).astype(BF16)
     return (mm(hidden, chosen_low) + mm(hop, chosen_high)).astype(BF16)
+
+
+def early_kernel(back_ref, taps_ref, early_ref):
+    for t in range(DILATION_SIZE):
+        early_ref[t] = mm(taps_ref[0], back_ref[t]).astype(BF16)
 
 
 def boundary_kernel(hidden_ref, own_ref, chosen_ref, boundary_ref):
@@ -613,7 +622,7 @@
     first = [(bit, 0, 0) for bit in dp[1:]]
     second = [(0, bit, 0) for bit in space]
     third = [(0, 0, bit) for bit in tm]
-    return [closure(masks) for masks in (first + third[:1], second + third[1:]) if masks]
+    return [closure(masks) for masks in (first + second, third) if masks]
 
 
 def closure(masks):
@@ -677,15 +686,16 @@
     )
     packed_far = swap(packed, "space", 1)
     border = shift(tail, "tm", 1)
-    hidden_late, slopes, right, near, kept_input, kept_taps, turned_taps, bias, mix, mixing, mix_bias = call(
+    hidden_late, slopes, right, near, spread, kept_input, kept_taps, turned_taps, bias, mix, mixing, mix_bias = call(
         forward_kernel,
         "forward",
-        [HBM] * 5 + [VMEM] * 2,
+        [HBM] * 5 + [VMEM] * 3,
         (
             shape((rows, sensors), BF16),
             shape((steps, wide, sensors), F32),
             shape((2 * wide + 16, steps * sensors), BF16),
-            shape((rows, sensors), F32),
+            shape((rows, 2 * sensors), F32),
+            shape((wide, 2 * sensors), BF16),
             shape(sample_input.shape, BF16),
             shape(taps.shape, BF16),
             shape((wide, wide), BF16),
@@ -702,20 +712,20 @@
             mix_b.reshape(1, chans),
             grad,
             own,
+            chosen,
         ),
         scratch=(DMA((5,)),),
         micros=1.5,
     )
     border_span = DILATION_SIZE * sensors
-    kept, given, back, early, hidden = call(
+    kept, given, back, hidden = call(
         backward_kernel,
         "backward",
-        [VMEM] * 15,
+        [VMEM] * 13,
         (
             shape((wide + 16, wide), F32),
             shape((wide + 16, wide), F32),
             shape((steps, wide, sensors), BF16),
-            shape((DILATION_SIZE, chans, sensors), BF16),
             shape((rows, sensors), BF16),
         ),
         (
@@ -723,11 +733,9 @@
             packed,
             packed_far,
             border,
-            own,
-            chosen,
             near,
+            spread,
             kept_input,
-            kept_taps,
             turned_taps,
             bias,
             mixing,
@@ -737,8 +745,7 @@
         ),
         scratch=(
             pltpu.VMEM((wide + 3 * chans, steps * sensors), BF16),
-            pltpu.VMEM((rows, sensors), BF16),
-            pltpu.VMEM((rows, sensors), BF16),
+            pltpu.VMEM((rows, 2 * sensors), BF16),
             pltpu.VMEM((DILATION_SIZE, wide, sensors), F32),
             pltpu.VMEM((2 * wide + 16, border_span), BF16),
         ),
@@ -746,6 +753,14 @@
     )
     total = kept + swap(given, "dp", 1)
     rounds = groups()
+    early = call(
+        early_kernel,
+        "early",
+        [VMEM] * 2,
+        shape((DILATION_SIZE, chans, sensors), BF16),
+        (back, kept_taps),
+        micros=0.3,
+    )
     early_far = shift(early, "tm", -1)
     boundary_first = call(
         boundary_kernel,

time: 31.6 us -> 31.1 us (0.984)
  starting transfers between devices: 15.4 us -> 14.6 us
  waiting for transfers between devices: 6.53 us -> 7.15 us
    ppermute x6, starting transfers between devices: 8.01 us -> 7.11 us  [flip(): return lax.ppermute(value, AXES, pairs)]
    ppermute x6, waiting for transfers between devices: 1.89 us -> 2.66 us  [flip(): return lax.ppermute(value, AXES, pairs)]
    pallas_call x7 -> x8, Pallas kernels: 8.61 us -> 8.37 us  [call(): pl.pallas_call(kernel, out_shape=out_shape, in_specs=in_specs, out_specs=...]
  transfers between devices with their start and end apart: 12 -> 12, of which waited for: 6 -> 6; matrix products, arithmetic and copies ran while one was open for 0% -> 0% of each run, Pallas kernels for 14% -> 16%
where the time goes in v4:
time: 31.1 us; the launch traced here: 31 us
  starting transfers between devices  14.6 us (47%)
  Pallas kernels  8.37 us (27%)
  waiting for transfers between devices  7.15 us (23%)
  between operations  0.75 us (2%)
    pallas_call x8, Pallas kernels, call(): pl.pallas_call(kernel, out_shape=out_shape, in_specs=in_specs, out_specs=...  8.37 us
    ppermute x6, starting transfers between devices, flip(): return lax.ppermute(value, AXES, pairs)  7.11 us
    ppermute x2, starting transfers between devices, shift(): lax.ppermute(value, axis, [(source, (source + steps) % count) for source...  3.96 us
    ppermute x4, starting transfers between devices, swap(): lax.ppermute(value, axis, [(source, source ^ bit) for source in range(cou...  3.52 us
    ppermute x2, waiting for transfers between devices, shift(): lax.ppermute(value, axis, [(source, (source + steps) % count) for source...  2.9 us
    ppermute x6, waiting for transfers between devices, flip(): return lax.ppermute(value, AXES, pairs)  2.66 us
    ppermute x4, waiting for transfers between devices, swap(): lax.ppermute(value, axis, [(source, source ^ bit) for source in range(cou...  1.59 us
  transfers between devices with their start and end apart: 12, of which 6 were waited for; matrix products, arithmetic and copies ran while one was open for 0% of the time, Pallas kernels for 16%

profile of v4, /device:TPU:0, one launch (start us, length us, event | category | flops | bytes accessed | tf_op | source)
XLA Modules:
  0.0 31.0 jit_solution(2837678286015335599)
XLA Ops:
  0.6 1.7 %prepare.1 = (bf16[544,128]{1,0:T(8,128)(2,1)S(1)}, bf16[256,256]{1,0:T(8,128)(2,1)S(1)}, bf16[256,128]{1,0:T(8,128)(2,1)S(1)}, bf16[256,128]{1,0:T(8,128)(2,1)S...) custom-call(s32[2,8]{1,0:T(2,128)} %cols_hbm.1, s32[1,2]{1,0:T(1,128)} %counts_hbm.1, ...), custom_call_target="tpu_custom_call" | custom-call | bytes 7200000 | tf_op jit(solution)/shard_map/prepare/pallas_call | solution.py:585
  2.4 3.0 %collective-permute-start = (bf16[544,128]{1,0:T(8,128)(2,1)S(1)}, bf16[544,128]{1,0:T(8,128)(2,1)S(1)}, u32[]{:S(2)}, u32[]{:S(2)}) collective-permute-start(bf16[544,128]{1,0:T(8,128)(2,1)S(1)} %get-tuple-element.38.own_packed_ref), channel_id=1, source_target_pairs={{0,4},{4,0},{1,5},{5,1},{2,6},{6,2},{3,7},{7,3},{8,12},{12,8},{9,1... | collective-permute-start | bytes 417800 | tf_op jit(solution)/shard_map/ppermute | solution.py:601
  5.4 1.6 %collective-permute-start.1 = (bf16[2,64,256]{2,1,0:T(8,128)(2,1)S(1)}, bf16[2,64,256]{2,1,0:T(8,128)(2,1)S(1)}, u32[]{:S(2)}, u32[]{:S(2)}) collective-permute-start(bf16[2,64,256]{2,1,0:T(8,128)(2,1)S(1)} %get-tuple-element.39), channel_id=1, source_target_pairs={{0,1},{1,2},{2,3},{3,0},{4,5},{5,6},{6,7},{7,4},{8,9},{9,10},{10,1... | collective-permute-start | bytes 196616 | tf_op jit(solution)/shard_map/ppermute | solution.py:606
  7.0 1.6 %forward.1 = (bf16[512,256]{1,0:T(8,128)(2,1)S(1)}, f32[8,128,256]{2,1,0:T(8,128)S(1)}, bf16[272,2048]{1,0:T(8,128)(2,1)S(1)}, f32[512,512]{1,0:T(8,128)S(1)}, b...) custom-call(bf16[8,64,256]{2,1,0:T(8,128)(2,1)} %bitcast.11, ...), custom_call_target="tpu_custom_call" | custom-call | bytes 5400000 | tf_op jit(solution)/shard_map/forward/pallas_call | solution.py:585
  8.6 2.9 %collective-permute-done.1.border_ref = bf16[2,64,256]{2,1,0:T(8,128)(2,1)S(1)} collective-permute-done((bf16[2,64,256]{2,1,0:T(8,128)(2,1)S(1)}, bf16[2,64,256]{2,1,0:T(8,128)(2,1)S(1)}, u32[]{:S(2)}, u32[]{:S(2)}) %collective-permute-start.1) | collective-permute-done | bytes 65568 | tf_op jit(solution)/shard_map/ppermute | solution.py:606
  11.5 0.0 collective-permute-done.packed_ref
  11.5 1.1 %backward.1 = (f32[144,128]{1,0:T(8,128)S(1)}, f32[144,128]{1,0:T(8,128)S(1)}, bf16[8,128,256]{2,1,0:T(8,128)(2,1)S(1)}, bf16[512,256]{1,0:T(8,128)(2,1)S(1)}) custom-call(bf16[512,256]{1,0:T(8,128)(2,1)S(1)} %get-tuple-element.34.grad_ref, bf16[544,128]{1,0:T(8,128)(2,1)S(1)} %get-tuple-element.38.own_packed_ref, ...), custom_call_target="tpu_custom_call" | custom-call | bytes 7200000 | tf_op jit(solution)/shard_map/backward/pallas_call | solution.py:585
  12.6 0.1 collective-permute-start.4
  12.7 0.6 %boundary.1.own_boundary_ref = bf16[512,128]{1,0:T(8,128)(2,1)S(1)} custom-call(bf16[512,256]{1,0:T(8,128)(2,1)S(1)} %get-tuple-element.48.hidden_ref, bf16[256,256]{1,0:T(8,128)(2,1)S(1)} %get-tuple-element.35.own_ref, bf16[256,128]{1,0:T(8,128)(2,1)S(1)} %get-tuple-element.36.chosen_ref), custom_call_target="tpu_custom_call" | custom-call | bytes 1080000 | tf_op jit(solution)/shard_map/boundary/pallas_call | solution.py:585
  13.2 0.3 %collective-permute-start.2 = (bf16[512,128]{1,0:T(8,128)(2,1)S(1)}, bf16[512,128]{1,0:T(8,128)(2,1)S(1)}, u32[]{:S(2)}, u32[]{:S(2)}) collective-permute-start(bf16[512,128]{1,0:T(8,128)(2,1)S(1)} %boundary.1.own_boundary_ref), channel_id=1, source_target_pairs={{0,4},{4,0},{1,5},{5,1},{2,6},{6,2},{3,7},{7,3},{8,12},{12,8},{9,1... | collective-permute-start | bytes 393224 | tf_op jit(solution)/shard_map/ppermute | solution.py:601
  13.6 0.3 %collective-permute-done.4 = f32[144,128]{1,0:T(8,128)S(1)} collective-permute-done((f32[144,128]{1,0:T(8,128)S(1)}, f32[144,128]{1,0:T(8,128)S(1)}, u32[]{:S(2)}, u32[]{:S(2)}) %collective-permute-start.4) | collective-permute-done | bytes 73760 | tf_op jit(solution)/shard_map/ppermute | solution.py:601
  14.0 1.6 %collective-permute-start.5 = (bf16[144,128]{1,0:T(8,128)(2,1)S(1)}, bf16[144,128]{1,0:T(8,128)(2,1)S(1)}, u32[]{:S(2)}, u32[]{:S(2)}) collective-permute-start(bf16[144,128]{1,0:T(8,128)(2,1)S(1)} %fusion), channel_id=1, source_target_pairs={{0,16},{1,17},{2,18},{3,19},{4,20},{5,21},{6,22},{7,23},{8,24},{9,... | collective-permute-start | bytes 110600 | tf_op jit(solution)/shard_map/ppermute | solution.py:617
  15.5 1.4 %collective-permute-start.7 = (bf16[144,128]{1,0:T(8,128)(2,1)S(1)}, bf16[144,128]{1,0:T(8,128)(2,1)S(1)}, u32[]{:S(2)}, u32[]{:S(2)}) collective-permute-start(bf16[144,128]{1,0:T(8,128)(2,1)S(1)} %fusion), channel_id=1, source_target_pairs={{0,20},{1,21},{2,22},{3,23},{4,16},{5,17},{6,18},{7,19},{8,28},{9,... | collective-permute-start | bytes 110600 | tf_op jit(solution)/shard_map/ppermute | solution.py:617
  16.9 0.6 %collective-permute-start.6 = (bf16[144,128]{1,0:T(8,128)(2,1)S(1)}, bf16[144,128]{1,0:T(8,128)(2,1)S(1)}, u32[]{:S(2)}, u32[]{:S(2)}) collective-permute-start(bf16[144,128]{1,0:T(8,128)(2,1)S(1)} %fusion), channel_id=1, source_target_pairs={{0,4},{1,5},{2,6},{3,7},{4,0},{5,1},{6,2},{7,3},{8,12},{9,13},{10,... | collective-permute-start | bytes 110600 | tf_op jit(solution)/shard_map/ppermute | solution.py:617
  17.5 0.2 early.1
  17.7 2.4 %collective-permute-start.3 = (bf16[2,64,256]{2,1,0:T(8,128)(2,1)S(1)}, bf16[2,64,256]{2,1,0:T(8,128)(2,1)S(1)}, u32[]{:S(2)}, u32[]{:S(2)}) collective-permute-start(bf16[2,64,256]{2,1,0:T(8,128)(2,1)S(1)} %early.1), channel_id=1, source_target_pairs={{0,3},{1,0},{2,1},{3,2},{4,7},{5,4},{6,5},{7,6},{8,11},{9,8},{10,9... | collective-permute-start | bytes 196616 | tf_op jit(solution)/shard_map/ppermute | solution.py:606
  20.1 0.0 collective-permute-done.5
  20.1 0.0 collective-permute-done.2.boundary_ref
  20.1 0.3 collective-permute-done.7
  20.4 0.5 %collective-permute-done.6 = bf16[144,128]{1,0:T(8,128)(2,1)S(1)} collective-permute-done((bf16[144,128]{1,0:T(8,128)(2,1)S(1)}, bf16[144,128]{1,0:T(8,128)(2,1)S(1)}, u32[]{:S(2)}, u32[]{:S(2)}) %collective-permute-start.6) | collective-permute-done | bytes 36896 | tf_op jit(solution)/shard_map/ppermute | solution.py:617
  20.9 0.2 collective-permute-start.8
  21.1 2.5 %collective-permute-start.10 = (bf16[144,128]{1,0:T(8,128)(2,1)S(1)}, bf16[144,128]{1,0:T(8,128)(2,1)S(1)}, u32[]{:S(2)}, u32[]{:S(2)}) collective-permute-start(bf16[144,128]{1,0:T(8,128)(2,1)S(1)} %fusion.1), channel_id=1, source_target_pairs={{0,3},{1,2},{2,1},{3,0},{4,7},{5,6},{6,5},{7,4},{8,11},{9,10},{10,... | collective-permute-start | bytes 110600 | tf_op jit(solution)/shard_map/ppermute | solution.py:617
  23.6 0.8 %collective-permute-start.9 = (bf16[144,128]{1,0:T(8,128)(2,1)S(1)}, bf16[144,128]{1,0:T(8,128)(2,1)S(1)}, u32[]{:S(2)}, u32[]{:S(2)}) collective-permute-start(bf16[144,128]{1,0:T(8,128)(2,1)S(1)} %fusion.1), channel_id=1, source_target_pairs={{0,2},{1,3},{2,0},{3,1},{4,6},{5,7},{6,4},{7,5},{8,10},{9,11},{10,... | collective-permute-start | bytes 110600 | tf_op jit(solution)/shard_map/ppermute | solution.py:617
  24.5 0.0 collective-permute-done.3.early_ref
  24.5 1.0 %input_grad.1 = bf16[8,64,256]{2,1,0:T(8,128)(2,1)} custom-call(bf16[512,256]{1,0:T(8,128)(2,1)S(1)} %get-tuple-element.34.grad_ref, bf16[8,128,256]{2,1,0:T(8,128)(2,1)S(1)} %get-tuple-element.52.back_ref, bf16[2,64,256]{2,1,0:T(8,128)(2,1)S(1)} %collective-permute-done.3.early_ref, bf16[2,64,128]{2,1,0:T(8,128)(2,1)S(1)} %get-tuple-element.53.taps_ref), custom_call_target="tpu_custom_call" | custom-call | bytes 4320000 | tf_op jit(solution)/shard_map/input_grad/pallas_call | solution.py:585
  25.5 1.5 %outputs.1 = bf16[8,64,256]{2,1,0:T(8,128)(2,1)} custom-call(bf16[8,64,256]{2,1,0:T(8,128)(2,1)S(1)} %get-tuple-element.37.input_ref, bf16[512,256]{1,0:T(8,128)(2,1)S(1)} %get-tuple-element.48.hidden_ref, bf16[512,128]{1,0:T(8,128)(2,1)S(1)} %boundary.1.own_boundary_ref, bf16[512,128]{1,0:T(8,128)(2,1)S(1)} %collective-permute-done.2.boundary_ref, ...), custom_call_target="tpu_custom_call" | custom-call | bytes 7200000 | tf_op jit(solution)/shard_map/outputs/pallas_call | solution.py:585
  27.0 0.0 collective-permute-done.8
  27.0 0.0 collective-permute-done.10
  27.0 1.9 %collective-permute-done.9 = bf16[144,128]{1,0:T(8,128)(2,1)S(1)} collective-permute-done((bf16[144,128]{1,0:T(8,128)(2,1)S(1)}, bf16[144,128]{1,0:T(8,128)(2,1)S(1)}, u32[]{:S(2)}, u32[]{:S(2)}) %collective-permute-start.9) | collective-permute-done | bytes 36896 | tf_op jit(solution)/shard_map/ppermute | solution.py:617
  28.9 0.1 collective-permute-start.11
  29.0 1.3 %collective-permute-done.11.other_ref = f32[144,128]{1,0:T(8,128)S(1)} collective-permute-done((f32[144,128]{1,0:T(8,128)S(1)}, f32[144,128]{1,0:T(8,128)S(1)}, u32[]{:S(2)}, u32[]{:S(2)}) %collective-permute-start.11) | collective-permute-done | bytes 73760 | tf_op jit(solution)/shard_map/ppermute | solution.py:601
  30.2 0.7 %final.1 = (f32[2,64,128]{2,1,0:T(8,128)}, f32[1,128]{1,0:T(1,128)}, f32[3,64,64]{2,1,0:T(8,128)}, f32[1,64]{1,0:T(1,128)}) custom-call(f32[144,128]{1,0:T(8,128)S(1)} %add_add_fusion.kept_ref, f32[144,128]{1,0:T(8,128)S(1)} %collective-permute-done.11.other_ref), custom_call_target="tpu_custom_call" | custom-call | bytes 3600000 | tf_op jit(solution)/shard_map/final/pallas_call | solution.py:585
  (9 shorter events, 0.1 us)
Async XLA Ops:
  2.4 9.1 %collective-permute-start = (bf16[544,128]{1,0:T(8,128)(2,1)S(1)}, bf16[544,128]{1,0:T(8,128)(2,1)S(1)}, u32[]{:S(2)}, u32[]{:S(2)}) collective-permute-start(bf16[544,128]{1,0:T(8,128)(2,1)S(1)} %get-tuple-element.38.own_packed_ref), channel_id=1, source_target_pairs={{0,4},{4,0},{1,5},{5,1},{2,6},{6,2},{3,7},{7,3},{8,12},{12,8},{9,1... | collective-permute-start | bytes 417800 | tf_op jit(solution)/shard_map/ppermute | solution.py:601
  5.4 6.1 %collective-permute-start.1 = (bf16[2,64,256]{2,1,0:T(8,128)(2,1)S(1)}, bf16[2,64,256]{2,1,0:T(8,128)(2,1)S(1)}, u32[]{:S(2)}, u32[]{:S(2)}) collective-permute-start(bf16[2,64,256]{2,1,0:T(8,128)(2,1)S(1)} %get-tuple-element.39), channel_id=1, source_target_pairs={{0,1},{1,2},{2,3},{3,0},{4,5},{5,6},{6,7},{7,4},{8,9},{9,10},{10,1... | collective-permute-start | bytes 196616 | tf_op jit(solution)/shard_map/ppermute | solution.py:606
  12.6 1.3 %collective-permute-start.4 = (f32[144,128]{1,0:T(8,128)S(1)}, f32[144,128]{1,0:T(8,128)S(1)}, u32[]{:S(2)}, u32[]{:S(2)}) collective-permute-start(f32[144,128]{1,0:T(8,128)S(1)} %get-tuple-element.55), channel_id=1, source_target_pairs={{0,8},{8,0},{16,24},{24,16},{1,9},{9,1},{17,25},{25,17},{2,10},{10... | collective-permute-start | bytes 221192 | tf_op jit(solution)/shard_map/ppermute | solution.py:601
  13.2 6.8 %collective-permute-start.2 = (bf16[512,128]{1,0:T(8,128)(2,1)S(1)}, bf16[512,128]{1,0:T(8,128)(2,1)S(1)}, u32[]{:S(2)}, u32[]{:S(2)}) collective-permute-start(bf16[512,128]{1,0:T(8,128)(2,1)S(1)} %boundary.1.own_boundary_ref), channel_id=1, source_target_pairs={{0,4},{4,0},{1,5},{5,1},{2,6},{6,2},{3,7},{7,3},{8,12},{12,8},{9,1... | collective-permute-start | bytes 393224 | tf_op jit(solution)/shard_map/ppermute | solution.py:601
  14.0 6.1 %collective-permute-start.5 = (bf16[144,128]{1,0:T(8,128)(2,1)S(1)}, bf16[144,128]{1,0:T(8,128)(2,1)S(1)}, u32[]{:S(2)}, u32[]{:S(2)}) collective-permute-start(bf16[144,128]{1,0:T(8,128)(2,1)S(1)} %fusion), channel_id=1, source_target_pairs={{0,16},{1,17},{2,18},{3,19},{4,20},{5,21},{6,22},{7,23},{8,24},{9,... | collective-permute-start | bytes 110600 | tf_op jit(solution)/shard_map/ppermute | solution.py:617
  15.5 4.9 %collective-permute-start.7 = (bf16[144,128]{1,0:T(8,128)(2,1)S(1)}, bf16[144,128]{1,0:T(8,128)(2,1)S(1)}, u32[]{:S(2)}, u32[]{:S(2)}) collective-permute-start(bf16[144,128]{1,0:T(8,128)(2,1)S(1)} %fusion), channel_id=1, source_target_pairs={{0,20},{1,21},{2,22},{3,23},{4,16},{5,17},{6,18},{7,19},{8,28},{9,... | collective-permute-start | bytes 110600 | tf_op jit(solution)/shard_map/ppermute | solution.py:617
  16.9 4.0 %collective-permute-start.6 = (bf16[144,128]{1,0:T(8,128)(2,1)S(1)}, bf16[144,128]{1,0:T(8,128)(2,1)S(1)}, u32[]{:S(2)}, u32[]{:S(2)}) collective-permute-start(bf16[144,128]{1,0:T(8,128)(2,1)S(1)} %fusion), channel_id=1, source_target_pairs={{0,4},{1,5},{2,6},{3,7},{4,0},{5,1},{6,2},{7,3},{8,12},{9,13},{10,... | collective-permute-start | bytes 110600 | tf_op jit(solution)/shard_map/ppermute | solution.py:617
  17.7 6.8 %collective-permute-start.3 = (bf16[2,64,256]{2,1,0:T(8,128)(2,1)S(1)}, bf16[2,64,256]{2,1,0:T(8,128)(2,1)S(1)}, u32[]{:S(2)}, u32[]{:S(2)}) collective-permute-start(bf16[2,64,256]{2,1,0:T(8,128)(2,1)S(1)} %early.1), channel_id=1, source_target_pairs={{0,3},{1,0},{2,1},{3,2},{4,7},{5,4},{6,5},{7,6},{8,11},{9,8},{10,9... | collective-permute-start | bytes 196616 | tf_op jit(solution)/shard_map/ppermute | solution.py:606
  20.9 6.1 %collective-permute-start.8 = (bf16[144,128]{1,0:T(8,128)(2,1)S(1)}, bf16[144,128]{1,0:T(8,128)(2,1)S(1)}, u32[]{:S(2)}, u32[]{:S(2)}) collective-permute-start(bf16[144,128]{1,0:T(8,128)(2,1)S(1)} %fusion.1), channel_id=1, source_target_pairs={{0,1},{1,0},{2,3},{3,2},{4,5},{5,4},{6,7},{7,6},{8,9},{9,8},{10,11... | collective-permute-start | bytes 110600 | tf_op jit(solution)/shard_map/ppermute | solution.py:617
  21.1 5.8 %collective-permute-start.10 = (bf16[144,128]{1,0:T(8,128)(2,1)S(1)}, bf16[144,128]{1,0:T(8,128)(2,1)S(1)}, u32[]{:S(2)}, u32[]{:S(2)}) collective-permute-start(bf16[144,128]{1,0:T(8,128)(2,1)S(1)} %fusion.1), channel_id=1, source_target_pairs={{0,3},{1,2},{2,1},{3,0},{4,7},{5,6},{6,5},{7,4},{8,11},{9,10},{10,... | collective-permute-start | bytes 110600 | tf_op jit(solution)/shard_map/ppermute | solution.py:617
  23.6 5.3 %collective-permute-start.9 = (bf16[144,128]{1,0:T(8,128)(2,1)S(1)}, bf16[144,128]{1,0:T(8,128)(2,1)S(1)}, u32[]{:S(2)}, u32[]{:S(2)}) collective-permute-start(bf16[144,128]{1,0:T(8,128)(2,1)S(1)} %fusion.1), channel_id=1, source_target_pairs={{0,2},{1,3},{2,0},{3,1},{4,6},{5,7},{6,4},{7,5},{8,10},{9,11},{10,... | collective-permute-start | bytes 110600 | tf_op jit(solution)/shard_map/ppermute | solution.py:617
  28.9 1.3 %collective-permute-start.11 = (f32[144,128]{1,0:T(8,128)S(1)}, f32[144,128]{1,0:T(8,128)S(1)}, u32[]{:S(2)}, u32[]{:S(2)}) collective-permute-start(f32[144,128]{1,0:T(8,128)S(1)} %add_add_fusion.kept_ref), channel_id=1, source_target_pairs={{0,8},{8,0},{16,24},{24,16},{1,9},{9,1},{17,25},{25,17},{2,10},{10... | collective-permute-start | bytes 221192 | tf_op jit(solution)/shard_map/ppermute | solution.py:601

commit v5 on v4

--- a/solution.py
+++ b/solution.py
@@ -622,14 +622,16 @@
     first = [(bit, 0, 0) for bit in dp[1:]]
     second = [(0, bit, 0) for bit in space]
     third = [(0, 0, bit) for bit in tm]
-    return [closure(masks) for masks in (first + second, third) if masks]
-
-
-def closure(masks):
+    orders = ((2, 1, 0), (1, 0, 2))
+    return [closure(masks, order) for masks, order in zip((first + second, third), orders) if masks]
+
+
+def closure(masks, order):
     found = [(0, 0, 0)]
     for mask in masks:
         found = found + [tuple(left ^ right for left, right in zip(item, mask)) for item in found]
-    return found[1:]
+    found = found[1:]
+    return [found[place] for place in order] if len(found) == len(order) else found
 
 
 def bits(count):

time: 31.1 us -> 29.8 us (0.958)
  waiting for transfers between devices: 7.15 us -> 5.81 us
    ppermute x6, waiting for transfers between devices: 2.66 us -> 1.01 us  [flip(): return lax.ppermute(value, AXES, pairs)]
    ppermute x4, waiting for transfers between devices: 1.59 us -> 1.9 us  [swap(): lax.ppermute(value, axis, [(source, source ^ bit) for source in range(cou...]
where the time goes in v5:
time: 29.8 us; the launch traced here: 29.6 us
  starting transfers between devices  14.6 us (49%)
  Pallas kernels  8.37 us (28%)
  waiting for transfers between devices  5.81 us (19%)
  between operations  0.73 us (2%)
    pallas_call x8, Pallas kernels, call(): pl.pallas_call(kernel, out_shape=out_shape, in_specs=in_specs, out_specs=...  8.37 us
    ppermute x6, starting transfers between devices, flip(): return lax.ppermute(value, AXES, pairs)  7.11 us
    ppermute x2, starting transfers between devices, shift(): lax.ppermute(value, axis, [(source, (source + steps) % count) for source...  3.96 us
    ppermute x4, starting transfers between devices, swap(): lax.ppermute(value, axis, [(source, source ^ bit) for source in range(cou...  3.52 us
    ppermute x2, waiting for transfers between devices, shift(): lax.ppermute(value, axis, [(source, (source + steps) % count) for source...  2.9 us
    ppermute x4, waiting for transfers between devices, swap(): lax.ppermute(value, axis, [(source, source ^ bit) for source in range(cou...  1.9 us
    ppermute x6, waiting for transfers between devices, flip(): return lax.ppermute(value, AXES, pairs)  1.01 us
  transfers between devices with their start and end apart: 12, of which 6 were waited for; matrix products, arithmetic and copies ran while one was open for 0% of the time, Pallas kernels for 16%

profile of v5, /device:TPU:0, one launch (start us, length us, event | category | flops | bytes accessed | tf_op | source)
XLA Modules:
  0.0 29.6 jit_solution(7278270452769144860)
XLA Ops:
  0.6 1.7 %prepare.1 = (bf16[544,128]{1,0:T(8,128)(2,1)S(1)}, bf16[256,256]{1,0:T(8,128)(2,1)S(1)}, bf16[256,128]{1,0:T(8,128)(2,1)S(1)}, bf16[256,128]{1,0:T(8,128)(2,1)S...) custom-call(s32[2,8]{1,0:T(2,128)} %cols_hbm.1, s32[1,2]{1,0:T(1,128)} %counts_hbm.1, ...), custom_call_target="tpu_custom_call" | custom-call | bytes 7200000 | tf_op jit(solution)/shard_map/prepare/pallas_call | solution.py:585
  2.4 3.0 %collective-permute-start = (bf16[544,128]{1,0:T(8,128)(2,1)S(1)}, bf16[544,128]{1,0:T(8,128)(2,1)S(1)}, u32[]{:S(2)}, u32[]{:S(2)}) collective-permute-start(bf16[544,128]{1,0:T(8,128)(2,1)S(1)} %get-tuple-element.38.own_packed_ref), channel_id=1, source_target_pairs={{0,4},{4,0},{1,5},{5,1},{2,6},{6,2},{3,7},{7,3},{8,12},{12,8},{9,1... | collective-permute-start | bytes 417800 | tf_op jit(solution)/shard_map/ppermute | solution.py:601
  5.4 1.6 %collective-permute-start.1 = (bf16[2,64,256]{2,1,0:T(8,128)(2,1)S(1)}, bf16[2,64,256]{2,1,0:T(8,128)(2,1)S(1)}, u32[]{:S(2)}, u32[]{:S(2)}) collective-permute-start(bf16[2,64,256]{2,1,0:T(8,128)(2,1)S(1)} %get-tuple-element.39), channel_id=1, source_target_pairs={{0,1},{1,2},{2,3},{3,0},{4,5},{5,6},{6,7},{7,4},{8,9},{9,10},{10,1... | collective-permute-start | bytes 196616 | tf_op jit(solution)/shard_map/ppermute | solution.py:606
  7.0 1.6 %forward.1 = (bf16[512,256]{1,0:T(8,128)(2,1)S(1)}, f32[8,128,256]{2,1,0:T(8,128)S(1)}, bf16[272,2048]{1,0:T(8,128)(2,1)S(1)}, f32[512,512]{1,0:T(8,128)S(1)}, b...) custom-call(bf16[8,64,256]{2,1,0:T(8,128)(2,1)} %bitcast.11, ...), custom_call_target="tpu_custom_call" | custom-call | bytes 5400000 | tf_op jit(solution)/shard_map/forward/pallas_call | solution.py:585
  8.6 2.9 %collective-permute-done.1.border_ref = bf16[2,64,256]{2,1,0:T(8,128)(2,1)S(1)} collective-permute-done((bf16[2,64,256]{2,1,0:T(8,128)(2,1)S(1)}, bf16[2,64,256]{2,1,0:T(8,128)(2,1)S(1)}, u32[]{:S(2)}, u32[]{:S(2)}) %collective-permute-start.1) | collective-permute-done | bytes 65568 | tf_op jit(solution)/shard_map/ppermute | solution.py:606
  11.5 0.0 collective-permute-done.packed_ref
  11.5 1.1 %backward.1 = (f32[144,128]{1,0:T(8,128)S(1)}, f32[144,128]{1,0:T(8,128)S(1)}, bf16[8,128,256]{2,1,0:T(8,128)(2,1)S(1)}, bf16[512,256]{1,0:T(8,128)(2,1)S(1)}) custom-call(bf16[512,256]{1,0:T(8,128)(2,1)S(1)} %get-tuple-element.34.grad_ref, bf16[544,128]{1,0:T(8,128)(2,1)S(1)} %get-tuple-element.38.own_packed_ref, ...), custom_call_target="tpu_custom_call" | custom-call | bytes 7200000 | tf_op jit(solution)/shard_map/backward/pallas_call | solution.py:585
  12.6 0.1 collective-permute-start.4
  12.7 0.6 %boundary.1.own_boundary_ref = bf16[512,128]{1,0:T(8,128)(2,1)S(1)} custom-call(bf16[512,256]{1,0:T(8,128)(2,1)S(1)} %get-tuple-element.48.hidden_ref, bf16[256,256]{1,0:T(8,128)(2,1)S(1)} %get-tuple-element.35.own_ref, bf16[256,128]{1,0:T(8,128)(2,1)S(1)} %get-tuple-element.36.chosen_ref), custom_call_target="tpu_custom_call" | custom-call | bytes 1080000 | tf_op jit(solution)/shard_map/boundary/pallas_call | solution.py:585
  13.2 0.3 %collective-permute-start.2 = (bf16[512,128]{1,0:T(8,128)(2,1)S(1)}, bf16[512,128]{1,0:T(8,128)(2,1)S(1)}, u32[]{:S(2)}, u32[]{:S(2)}) collective-permute-start(bf16[512,128]{1,0:T(8,128)(2,1)S(1)} %boundary.1.own_boundary_ref), channel_id=1, source_target_pairs={{0,4},{4,0},{1,5},{5,1},{2,6},{6,2},{3,7},{7,3},{8,12},{12,8},{9,1... | collective-permute-start | bytes 393224 | tf_op jit(solution)/shard_map/ppermute | solution.py:601
  13.6 0.3 %collective-permute-done.4 = f32[144,128]{1,0:T(8,128)S(1)} collective-permute-done((f32[144,128]{1,0:T(8,128)S(1)}, f32[144,128]{1,0:T(8,128)S(1)}, u32[]{:S(2)}, u32[]{:S(2)}) %collective-permute-start.4) | collective-permute-done | bytes 73760 | tf_op jit(solution)/shard_map/ppermute | solution.py:601
  14.0 2.4 %collective-permute-start.5 = (bf16[144,128]{1,0:T(8,128)(2,1)S(1)}, bf16[144,128]{1,0:T(8,128)(2,1)S(1)}, u32[]{:S(2)}, u32[]{:S(2)}) collective-permute-start(bf16[144,128]{1,0:T(8,128)(2,1)S(1)} %fusion), channel_id=1, source_target_pairs={{0,20},{1,21},{2,22},{3,23},{4,16},{5,17},{6,18},{7,19},{8,28},{9,... | collective-permute-start | bytes 110600 | tf_op jit(solution)/shard_map/ppermute | solution.py:617
  16.4 0.5 %collective-permute-start.7 = (bf16[144,128]{1,0:T(8,128)(2,1)S(1)}, bf16[144,128]{1,0:T(8,128)(2,1)S(1)}, u32[]{:S(2)}, u32[]{:S(2)}) collective-permute-start(bf16[144,128]{1,0:T(8,128)(2,1)S(1)} %fusion), channel_id=1, source_target_pairs={{0,16},{1,17},{2,18},{3,19},{4,20},{5,21},{6,22},{7,23},{8,24},{9,... | collective-permute-start | bytes 110600 | tf_op jit(solution)/shard_map/ppermute | solution.py:617
  16.9 0.6 %collective-permute-start.6 = (bf16[144,128]{1,0:T(8,128)(2,1)S(1)}, bf16[144,128]{1,0:T(8,128)(2,1)S(1)}, u32[]{:S(2)}, u32[]{:S(2)}) collective-permute-start(bf16[144,128]{1,0:T(8,128)(2,1)S(1)} %fusion), channel_id=1, source_target_pairs={{0,4},{1,5},{2,6},{3,7},{4,0},{5,1},{6,2},{7,3},{8,12},{9,13},{10,... | collective-permute-start | bytes 110600 | tf_op jit(solution)/shard_map/ppermute | solution.py:617
  17.5 0.2 early.1
  17.7 2.4 %collective-permute-start.3 = (bf16[2,64,256]{2,1,0:T(8,128)(2,1)S(1)}, bf16[2,64,256]{2,1,0:T(8,128)(2,1)S(1)}, u32[]{:S(2)}, u32[]{:S(2)}) collective-permute-start(bf16[2,64,256]{2,1,0:T(8,128)(2,1)S(1)} %early.1), channel_id=1, source_target_pairs={{0,3},{1,0},{2,1},{3,2},{4,7},{5,4},{6,5},{7,6},{8,11},{9,8},{10,9... | collective-permute-start | bytes 196616 | tf_op jit(solution)/shard_map/ppermute | solution.py:606
  20.1 0.0 collective-permute-done.5
  20.1 0.3 %collective-permute-done.2.boundary_ref = bf16[512,128]{1,0:T(8,128)(2,1)S(1)} collective-permute-done((bf16[512,128]{1,0:T(8,128)(2,1)S(1)}, bf16[512,128]{1,0:T(8,128)(2,1)S(1)}, u32[]{:S(2)}, u32[]{:S(2)}) %collective-permute-start.2) | collective-permute-done | bytes 131104 | tf_op jit(solution)/shard_map/ppermute | solution.py:601
  20.4 0.0 collective-permute-done.7
  20.4 0.5 %collective-permute-done.6 = bf16[144,128]{1,0:T(8,128)(2,1)S(1)} collective-permute-done((bf16[144,128]{1,0:T(8,128)(2,1)S(1)}, bf16[144,128]{1,0:T(8,128)(2,1)S(1)}, u32[]{:S(2)}, u32[]{:S(2)}) %collective-permute-start.6) | collective-permute-done | bytes 36896 | tf_op jit(solution)/shard_map/ppermute | solution.py:617
  20.9 0.8 %collective-permute-start.8 = (bf16[144,128]{1,0:T(8,128)(2,1)S(1)}, bf16[144,128]{1,0:T(8,128)(2,1)S(1)}, u32[]{:S(2)}, u32[]{:S(2)}) collective-permute-start(bf16[144,128]{1,0:T(8,128)(2,1)S(1)} %fusion.1), channel_id=1, source_target_pairs={{0,2},{1,3},{2,0},{3,1},{4,6},{5,7},{6,4},{7,5},{8,10},{9,11},{10,... | collective-permute-start | bytes 110600 | tf_op jit(solution)/shard_map/ppermute | solution.py:617
  21.8 1.3 %collective-permute-start.10 = (bf16[144,128]{1,0:T(8,128)(2,1)S(1)}, bf16[144,128]{1,0:T(8,128)(2,1)S(1)}, u32[]{:S(2)}, u32[]{:S(2)}) collective-permute-start(bf16[144,128]{1,0:T(8,128)(2,1)S(1)} %fusion.1), channel_id=1, source_target_pairs={{0,3},{1,2},{2,1},{3,0},{4,7},{5,6},{6,5},{7,4},{8,11},{9,10},{10,... | collective-permute-start | bytes 110600 | tf_op jit(solution)/shard_map/ppermute | solution.py:617
  23.1 1.4 %collective-permute-start.9 = (bf16[144,128]{1,0:T(8,128)(2,1)S(1)}, bf16[144,128]{1,0:T(8,128)(2,1)S(1)}, u32[]{:S(2)}, u32[]{:S(2)}) collective-permute-start(bf16[144,128]{1,0:T(8,128)(2,1)S(1)} %fusion.1), channel_id=1, source_target_pairs={{0,1},{1,0},{2,3},{3,2},{4,5},{5,4},{6,7},{7,6},{8,9},{9,8},{10,11... | collective-permute-start | bytes 110600 | tf_op jit(solution)/shard_map/ppermute | solution.py:617
  24.5 0.0 collective-permute-done.3.early_ref
  24.5 1.0 %input_grad.1 = bf16[8,64,256]{2,1,0:T(8,128)(2,1)} custom-call(bf16[512,256]{1,0:T(8,128)(2,1)S(1)} %get-tuple-element.34.grad_ref, bf16[8,128,256]{2,1,0:T(8,128)(2,1)S(1)} %get-tuple-element.52.back_ref, bf16[2,64,256]{2,1,0:T(8,128)(2,1)S(1)} %collective-permute-done.3.early_ref, bf16[2,64,128]{2,1,0:T(8,128)(2,1)S(1)} %get-tuple-element.53.taps_ref), custom_call_target="tpu_custom_call" | custom-call | bytes 4320000 | tf_op jit(solution)/shard_map/input_grad/pallas_call | solution.py:585
  25.5 1.5 %outputs.1 = bf16[8,64,256]{2,1,0:T(8,128)(2,1)} custom-call(bf16[8,64,256]{2,1,0:T(8,128)(2,1)S(1)} %get-tuple-element.37.input_ref, bf16[512,256]{1,0:T(8,128)(2,1)S(1)} %get-tuple-element.48.hidden_ref, bf16[512,128]{1,0:T(8,128)(2,1)S(1)} %boundary.1.own_boundary_ref, bf16[512,128]{1,0:T(8,128)(2,1)S(1)} %collective-permute-done.2.boundary_ref, ...), custom_call_target="tpu_custom_call" | custom-call | bytes 7200000 | tf_op jit(solution)/shard_map/outputs/pallas_call | solution.py:585
  27.0 0.0 collective-permute-done.8
  27.0 0.5 %collective-permute-done.10 = bf16[144,128]{1,0:T(8,128)(2,1)S(1)} collective-permute-done((bf16[144,128]{1,0:T(8,128)(2,1)S(1)}, bf16[144,128]{1,0:T(8,128)(2,1)S(1)}, u32[]{:S(2)}, u32[]{:S(2)}) %collective-permute-start.10) | collective-permute-done | bytes 36896 | tf_op jit(solution)/shard_map/ppermute | solution.py:617
  27.5 0.0 collective-permute-done.9
  27.5 0.1 collective-permute-start.11
  27.6 1.3 %collective-permute-done.11.other_ref = f32[144,128]{1,0:T(8,128)S(1)} collective-permute-done((f32[144,128]{1,0:T(8,128)S(1)}, f32[144,128]{1,0:T(8,128)S(1)}, u32[]{:S(2)}, u32[]{:S(2)}) %collective-permute-start.11) | collective-permute-done | bytes 73760 | tf_op jit(solution)/shard_map/ppermute | solution.py:601
  28.9 0.7 %final.1 = (f32[2,64,128]{2,1,0:T(8,128)}, f32[1,128]{1,0:T(1,128)}, f32[3,64,64]{2,1,0:T(8,128)}, f32[1,64]{1,0:T(1,128)}) custom-call(f32[144,128]{1,0:T(8,128)S(1)} %add_add_fusion.kept_ref, f32[144,128]{1,0:T(8,128)S(1)} %collective-permute-done.11.other_ref), custom_call_target="tpu_custom_call" | custom-call | bytes 3600000 | tf_op jit(solution)/shard_map/final/pallas_call | solution.py:585
  (9 shorter events, 0.1 us)
Async XLA Ops:
  2.4 9.1 %collective-permute-start = (bf16[544,128]{1,0:T(8,128)(2,1)S(1)}, bf16[544,128]{1,0:T(8,128)(2,1)S(1)}, u32[]{:S(2)}, u32[]{:S(2)}) collective-permute-start(bf16[544,128]{1,0:T(8,128)(2,1)S(1)} %get-tuple-element.38.own_packed_ref), channel_id=1, source_target_pairs={{0,4},{4,0},{1,5},{5,1},{2,6},{6,2},{3,7},{7,3},{8,12},{12,8},{9,1... | collective-permute-start | bytes 417800 | tf_op jit(solution)/shard_map/ppermute | solution.py:601
  5.4 6.1 %collective-permute-start.1 = (bf16[2,64,256]{2,1,0:T(8,128)(2,1)S(1)}, bf16[2,64,256]{2,1,0:T(8,128)(2,1)S(1)}, u32[]{:S(2)}, u32[]{:S(2)}) collective-permute-start(bf16[2,64,256]{2,1,0:T(8,128)(2,1)S(1)} %get-tuple-element.39), channel_id=1, source_target_pairs={{0,1},{1,2},{2,3},{3,0},{4,5},{5,6},{6,7},{7,4},{8,9},{9,10},{10,1... | collective-permute-start | bytes 196616 | tf_op jit(solution)/shard_map/ppermute | solution.py:606
  12.6 1.3 %collective-permute-start.4 = (f32[144,128]{1,0:T(8,128)S(1)}, f32[144,128]{1,0:T(8,128)S(1)}, u32[]{:S(2)}, u32[]{:S(2)}) collective-permute-start(f32[144,128]{1,0:T(8,128)S(1)} %get-tuple-element.55), channel_id=1, source_target_pairs={{0,8},{8,0},{16,24},{24,16},{1,9},{9,1},{17,25},{25,17},{2,10},{10... | collective-permute-start | bytes 221192 | tf_op jit(solution)/shard_map/ppermute | solution.py:601
  13.2 7.1 %collective-permute-start.2 = (bf16[512,128]{1,0:T(8,128)(2,1)S(1)}, bf16[512,128]{1,0:T(8,128)(2,1)S(1)}, u32[]{:S(2)}, u32[]{:S(2)}) collective-permute-start(bf16[512,128]{1,0:T(8,128)(2,1)S(1)} %boundary.1.own_boundary_ref), channel_id=1, source_target_pairs={{0,4},{4,0},{1,5},{5,1},{2,6},{6,2},{3,7},{7,3},{8,12},{12,8},{9,1... | collective-permute-start | bytes 393224 | tf_op jit(solution)/shard_map/ppermute | solution.py:601
  14.0 6.1 %collective-permute-start.5 = (bf16[144,128]{1,0:T(8,128)(2,1)S(1)}, bf16[144,128]{1,0:T(8,128)(2,1)S(1)}, u32[]{:S(2)}, u32[]{:S(2)}) collective-permute-start(bf16[144,128]{1,0:T(8,128)(2,1)S(1)} %fusion), channel_id=1, source_target_pairs={{0,20},{1,21},{2,22},{3,23},{4,16},{5,17},{6,18},{7,19},{8,28},{9,... | collective-permute-start | bytes 110600 | tf_op jit(solution)/shard_map/ppermute | solution.py:617
  16.4 4.0 %collective-permute-start.7 = (bf16[144,128]{1,0:T(8,128)(2,1)S(1)}, bf16[144,128]{1,0:T(8,128)(2,1)S(1)}, u32[]{:S(2)}, u32[]{:S(2)}) collective-permute-start(bf16[144,128]{1,0:T(8,128)(2,1)S(1)} %fusion), channel_id=1, source_target_pairs={{0,16},{1,17},{2,18},{3,19},{4,20},{5,21},{6,22},{7,23},{8,24},{9,... | collective-permute-start | bytes 110600 | tf_op jit(solution)/shard_map/ppermute | solution.py:617
  16.9 4.0 %collective-permute-start.6 = (bf16[144,128]{1,0:T(8,128)(2,1)S(1)}, bf16[144,128]{1,0:T(8,128)(2,1)S(1)}, u32[]{:S(2)}, u32[]{:S(2)}) collective-permute-start(bf16[144,128]{1,0:T(8,128)(2,1)S(1)} %fusion), channel_id=1, source_target_pairs={{0,4},{1,5},{2,6},{3,7},{4,0},{5,1},{6,2},{7,3},{8,12},{9,13},{10,... | collective-permute-start | bytes 110600 | tf_op jit(solution)/shard_map/ppermute | solution.py:617
  17.7 6.8 %collective-permute-start.3 = (bf16[2,64,256]{2,1,0:T(8,128)(2,1)S(1)}, bf16[2,64,256]{2,1,0:T(8,128)(2,1)S(1)}, u32[]{:S(2)}, u32[]{:S(2)}) collective-permute-start(bf16[2,64,256]{2,1,0:T(8,128)(2,1)S(1)} %early.1), channel_id=1, source_target_pairs={{0,3},{1,0},{2,1},{3,2},{4,7},{5,4},{6,5},{7,6},{8,11},{9,8},{10,9... | collective-permute-start | bytes 196616 | tf_op jit(solution)/shard_map/ppermute | solution.py:606
  20.9 6.1 %collective-permute-start.8 = (bf16[144,128]{1,0:T(8,128)(2,1)S(1)}, bf16[144,128]{1,0:T(8,128)(2,1)S(1)}, u32[]{:S(2)}, u32[]{:S(2)}) collective-permute-start(bf16[144,128]{1,0:T(8,128)(2,1)S(1)} %fusion.1), channel_id=1, source_target_pairs={{0,2},{1,3},{2,0},{3,1},{4,6},{5,7},{6,4},{7,5},{8,10},{9,11},{10,... | collective-permute-start | bytes 110600 | tf_op jit(solution)/shard_map/ppermute | solution.py:617
  21.8 5.8 %collective-permute-start.10 = (bf16[144,128]{1,0:T(8,128)(2,1)S(1)}, bf16[144,128]{1,0:T(8,128)(2,1)S(1)}, u32[]{:S(2)}, u32[]{:S(2)}) collective-permute-start(bf16[144,128]{1,0:T(8,128)(2,1)S(1)} %fusion.1), channel_id=1, source_target_pairs={{0,3},{1,2},{2,1},{3,0},{4,7},{5,6},{6,5},{7,4},{8,11},{9,10},{10,... | collective-permute-start | bytes 110600 | tf_op jit(solution)/shard_map/ppermute | solution.py:617
  23.1 4.4 %collective-permute-start.9 = (bf16[144,128]{1,0:T(8,128)(2,1)S(1)}, bf16[144,128]{1,0:T(8,128)(2,1)S(1)}, u32[]{:S(2)}, u32[]{:S(2)}) collective-permute-start(bf16[144,128]{1,0:T(8,128)(2,1)S(1)} %fusion.1), channel_id=1, source_target_pairs={{0,1},{1,0},{2,3},{3,2},{4,5},{5,4},{6,7},{7,6},{8,9},{9,8},{10,11... | collective-permute-start | bytes 110600 | tf_op jit(solution)/shard_map/ppermute | solution.py:617
  27.5 1.3 %collective-permute-start.11 = (f32[144,128]{1,0:T(8,128)S(1)}, f32[144,128]{1,0:T(8,128)S(1)}, u32[]{:S(2)}, u32[]{:S(2)}) collective-permute-start(f32[144,128]{1,0:T(8,128)S(1)} %add_add_fusion.kept_ref), channel_id=1, source_target_pairs={{0,8},{8,0},{16,24},{24,16},{1,9},{9,1},{17,25},{25,17},{2,10},{10... | collective-permute-start | bytes 221192 | tf_op jit(solution)/shard_map/ppermute | solution.py:601

commit v6 on v5

--- a/solution.py
+++ b/solution.py
@@ -239,13 +239,6 @@
     packed = packed.astype(F32)
     turned = pltpu.roll(packed, packed.shape[1] // 2, 1)
     return jnp.concatenate([halves(packed)[0], halves(turned)[0]], 0).astype(BF16)
-
-
-def turned_link_matrix(packed):
-    packed = packed.astype(F32)
-    turned = pltpu.roll(packed, packed.shape[1] // 2, 1)
-    blank = jnp.zeros_like(packed)
-    return jnp.concatenate([blank, blank, halves(packed)[0], halves(turned)[0]], 0).astype(BF16)
 
 
 def column(row):
@@ -376,6 +369,7 @@
     mix_ref,
     mixing_ref,
     mix_bias_ref,
+    mix_wide_ref,
     sems,
 ):
     copies = fetch(
@@ -406,6 +400,7 @@
         copy.wait()
     mixing = jnp.transpose(mix_ref[...].reshape(3 * chans, chans).astype(F32))
     mixing_ref[...] = mixing.astype(BF16)
+    mix_wide_ref[...] = jnp.concatenate([mix_ref[0], mix_ref[1], mix_ref[2]], 1)
     taps = taps_ref[...].reshape(2 * chans, 2 * chans).astype(F32)
     taps = jnp.transpose(taps).astype(BF16)
     turned_taps_ref[...] = taps
@@ -482,13 +477,17 @@
     sums = conv[wide : wide + 8]
     conv = conv[:wide, :wide]
     zero, first, second = [mixes[k * chans : (k + 1) * chans] for k in range(3)]
-    blank = jnp.zeros((chans, wide), F32)
-    mixes = jnp.concatenate([fold(zero, first), fold(second, blank)], 0)
-    mix_sums = jnp.concatenate([sums[:, wide:], blank[:8, :chans]], 1)
-    conv = jnp.concatenate([conv, sums[:, :wide], blank[:8]], 0)
-    mixes = jnp.concatenate([mixes, mix_sums, blank[:8]], 0)
-    kept_ref[...] = jnp.where(core == 0, conv, mixes)
-    given_ref[...] = jnp.where(core == 0, mixes, conv)
+    half = chans // 2
+    blank = jnp.zeros((8, wide), F32)
+    mix_sums = jnp.concatenate([sums[:, wide:], blank[:, :chans]], 1)
+    upper_rows = lax.broadcasted_iota(jnp.int32, blank.shape, 0) >= 4
+    biases = jnp.where(upper_rows, mix_sums, sums[:, :wide])
+    packed = jnp.concatenate(
+        [conv, fold(zero, first), fold(second[:half], second[half:]), biases, blank], 0
+    )
+    cut = packed.shape[0] // 2
+    kept_ref[...] = jnp.where(core == 0, packed[:cut], packed[cut:])
+    given_ref[...] = jnp.where(core == 0, packed[cut:], packed[:cut])
 
 
 def boundary_rows(hidden, own, chosen):
@@ -507,41 +506,60 @@
     boundary_ref[...] = boundary_rows(hidden, own_ref[...], chosen_ref[...])
 
 
-def outputs_kernel(
+def hops_kernel(hidden_ref, packed_ref, own_ref, halo_ref, base_ref, spread_ref):
+    sensors = own_ref.shape[0]
+    slots = halo_ref.shape[1] // 2
+    rows = hidden_ref.shape[0]
+    own = own_ref[...]
+    one = mm_nt(hidden_ref[...], own)
+    base_ref[:, :sensors] = one
+    base_ref[:, sensors:] = mm_nt(one.astype(BF16), own)
+    halo = halo_ref[...]
+    link = link_rows(packed_ref[rows:, :])
+    link = jnp.concatenate([link, jnp.zeros_like(link)], 0)
+    turned = jnp.transpose(jnp.concatenate([halo.astype(F32), mm(halo, link)], 1)).astype(BF16)
+    blank = jnp.zeros((slots, sensors), BF16)
+    first = turned[:slots]
+    spread_ref[:slots, :sensors] = first
+    spread_ref[:slots, sensors:] = mm_nt(first, own).astype(BF16)
+    for block in range(1, 4):
+        at = slice(block * slots, (block + 1) * slots)
+        spread_ref[at, :sensors] = blank
+        spread_ref[at, sensors:] = turned[at] if block < 3 else blank
+
+
+def finish_kernel(
     input_ref,
     hidden_ref,
     own_boundary_ref,
     boundary_ref,
-    packed_ref,
-    own_ref,
-    halo_ref,
+    base_ref,
+    spread_ref,
     mix_ref,
     bias_ref,
-    out_ref,
+    grad_ref,
+    back_ref,
+    early_ref,
+    taps_ref,
+    out_hbm,
+    grad_out_hbm,
+    out_scr,
+    grad_scr,
+    both_scr,
+    sems,
 ):
     steps, chans, sensors = input_ref.shape
-    rows = steps * chans
-    own = own_ref[...]
-    halo = halo_ref[...]
-    halo_low, halo_high = halves(halo)
-    link = turned_link_matrix(packed_ref[rows:, :])
-    hidden = hidden_ref[...]
-    own_boundary = own_boundary_ref[...]
-    boundary = boundary_ref[...]
-    one = (mm_nt(hidden, own) + mm_nt(boundary, halo_low)).astype(BF16)
-    far = (boundary.astype(F32) + mm_nt(own_boundary, link)).astype(BF16)
-    two = (mm_nt(one, own) + mm_nt(far, halo_high)).astype(BF16)
-    bias = column(bias_ref[...])
-    for t in range(steps):
-        at = slice(t * chans, (t + 1) * chans)
-        mixed = mm(mix_ref[0], hidden[at]) + mm(mix_ref[1], one[at]) + mm(mix_ref[2], two[at])
-        out_ref[t] = (mixed + bias + input_ref[t].astype(F32)).astype(BF16)
-
-
-def input_grad_kernel(grad_ref, back_ref, early_ref, taps_ref, out_ref):
-    steps, chans, sensors = out_ref.shape
     has_later = lax.axis_index("tm") < lax.axis_size("tm") - 1
     taps = jnp.concatenate([taps_ref[0], taps_ref[1]], 1)
+    chunk = steps // 2
+    copies = []
+
+    def send(scratch, target, start):
+        span = pl.ds(start, chunk)
+        copy = pltpu.make_async_copy(scratch.at[span], target.at[span], sems.at[len(copies)])
+        copy.start()
+        copies.append(copy)
+
     for t in range(steps):
         at = slice(t * chans, (t + 1) * chans)
         later = t + DILATION_SIZE
@@ -552,24 +570,45 @@
             early = early_ref[later - steps].astype(F32)
             early = jnp.where(has_later, early, jnp.zeros_like(early))
             total = total + mm(taps_ref[1], back_ref[t]) + early
-        out_ref[t] = total.astype(BF16)
+        grad_scr[t] = total.astype(BF16)
+        if (t + 1) % chunk == 0:
+            send(grad_scr, grad_out_hbm, t + 1 - chunk)
+    boundary = jnp.concatenate([boundary_ref[...], own_boundary_ref[...]], 1)
+    both_scr[...] = (base_ref[...] + mm(boundary, spread_ref[...])).astype(BF16)
+    bias = column(bias_ref[...])
+    mix = mix_ref[...]
+    for t in range(steps):
+        at = slice(t * chans, (t + 1) * chans)
+        fields = jnp.concatenate(
+            [hidden_ref[at, :], both_scr[at, :sensors], both_scr[at, sensors:]], 0
+        )
+        out_scr[t] = (mm(mix, fields) + bias + input_ref[t].astype(F32)).astype(BF16)
+        if (t + 1) % chunk == 0:
+            send(out_scr, out_hbm, t + 1 - chunk)
+    for copy in copies:
+        copy.wait()
 
 
 def final_kernel(scale, kept_ref, other_ref, conv_w_ref, conv_b_ref, mix_w_ref, mix_b_ref):
     core = lax.axis_index("dp") % 2
     kept = kept_ref[...] * scale
     other = other_ref[...] * scale
-    conv = jnp.where(core == 0, kept, other)
-    mixes = jnp.where(core == 0, other, kept)
-    chans = conv.shape[1] // 2
-    wide = 2 * chans
-    conv_w_ref[0] = conv[:chans]
-    conv_w_ref[1] = conv[chans:wide]
-    mix_w_ref[0] = mixes[:chans, :chans]
-    mix_w_ref[1] = pltpu.roll(mixes[:chans], chans, 1)[:, :chans]
-    mix_w_ref[2] = mixes[chans:wide, :chans]
-    conv_b_ref[...] = (conv[wide : wide + 8] + conv[wide + 8 :])[:1]
-    mix_b_ref[...] = (mixes[wide : wide + 8] + mixes[wide + 8 :])[:1, :chans]
+    lower = jnp.where(core == 0, kept, other)
+    upper = jnp.where(core == 0, other, kept)
+    chans, wide = conv_w_ref.shape[1:]
+    half = chans // 2
+    start = wide - lower.shape[0]
+    conv_w_ref[0] = lower[:chans]
+    conv_w_ref[1] = jnp.concatenate([lower[chans:], upper[:start]], 0)
+    first = upper[start : start + chans]
+    second = upper[start + chans : start + chans + half]
+    mix_w_ref[0] = first[:, :chans]
+    mix_w_ref[1] = pltpu.roll(first, chans, 1)[:, :chans]
+    mix_w_ref[2] = jnp.concatenate([second, pltpu.roll(second, chans, 1)], 0)[:, :chans]
+    start = start + chans + half
+    biases = upper[start : start + 8] + upper[start + 8 :]
+    conv_b_ref[...] = biases[:1]
+    mix_b_ref[...] = biases[4:5, :chans]
 
 
 VMEM = pl.BlockSpec(memory_space=pltpu.VMEM)
@@ -577,7 +616,7 @@
 DMA = pltpu.SemaphoreType.DMA
 
 
-def call(kernel, name, in_specs, out_shape, args, scratch=(), micros=1.0):
+def call(kernel, name, in_specs, out_shape, args, scratch=(), micros=1.0, space=None):
     args = [
         pltpu.with_memory_space_constraint(arg, pltpu.HBM) if spec is HBM else arg
         for spec, arg in zip(in_specs, args)
@@ -586,7 +625,7 @@
         kernel,
         out_shape=out_shape,
         in_specs=in_specs,
-        out_specs=jax.tree.map(lambda _: VMEM, out_shape),
+        out_specs=jax.tree.map(lambda _: space or VMEM, out_shape),
         scratch_shapes=list(scratch),
         compiler_params=pltpu.CompilerParams(vmem_limit_bytes=VMEM_BYTES),
         cost_estimate=pl.CostEstimate(
@@ -622,7 +661,7 @@
     first = [(bit, 0, 0) for bit in dp[1:]]
     second = [(0, bit, 0) for bit in space]
     third = [(0, 0, bit) for bit in tm]
-    orders = ((2, 1, 0), (1, 0, 2))
+    orders = ((2, 0, 1), (1, 0, 2))
     return [closure(masks, order) for masks, order in zip((first + second, third), orders) if masks]
 
 
@@ -642,10 +681,10 @@
     return lax.reduce_precision(value, exponent_bits=8, mantissa_bits=7)
 
 
-def round_sums(sums):
+def round_sums(sums, has_biases):
     end = sums.shape[0]
     high = sums[end - 16 : end - 8]
-    rest = jnp.pad(high - to_bf16(high), ((end - 8, 0), (0, 0)))
+    rest = jnp.pad((high - to_bf16(high)) * has_biases, ((end - 8, 0), (0, 0)))
     return to_bf16(sums + rest)
 
 
@@ -688,7 +727,7 @@
     )
     packed_far = swap(packed, "space", 1)
     border = shift(tail, "tm", 1)
-    hidden_late, slopes, right, near, spread, kept_input, kept_taps, turned_taps, bias, mix, mixing, mix_bias = call(
+    hidden_late, slopes, right, near, spread, kept_input, kept_taps, turned_taps, bias, mix, mixing, mix_bias, mix_wide = call(
         forward_kernel,
         "forward",
         [HBM] * 5 + [VMEM] * 3,
@@ -705,6 +744,7 @@
             shape(mix_w.shape, BF16),
             shape((chans, 3 * chans), BF16),
             shape((1, chans), F32),
+            shape((chans, 3 * chans), BF16),
         ),
         (
             sample_input,
@@ -720,13 +760,14 @@
         micros=1.5,
     )
     border_span = DILATION_SIZE * sensors
+    sum_rows = (wide + chans + chans // 2 + 16) // 2
     kept, given, back, hidden = call(
         backward_kernel,
         "backward",
         [VMEM] * 13,
         (
-            shape((wide + 16, wide), F32),
-            shape((wide + 16, wide), F32),
+            shape((sum_rows, wide), F32),
+            shape((sum_rows, wide), F32),
             shape((steps, wide, sensors), BF16),
             shape((rows, sensors), BF16),
         ),
@@ -755,6 +796,7 @@
     )
     total = kept + swap(given, "dp", 1)
     rounds = groups()
+    has_biases = (lax.axis_index("dp") % 2).astype(F32)
     early = call(
         early_kernel,
         "early",
@@ -773,35 +815,45 @@
         micros=0.3,
     )
     first_far = swap(boundary_first, "space", 1)
-    outputs = call(
-        outputs_kernel,
-        "outputs",
-        [VMEM] * 9,
-        shape(sample_input.shape, BF16),
+    base, hop_spread = call(
+        hops_kernel,
+        "hops",
+        [VMEM] * 4,
+        (shape((rows, 2 * sensors), F32), shape((2 * wide, 2 * sensors), BF16)),
+        (hidden, packed_far, own, halo),
+        micros=0.5,
+    )
+    outputs, grad_inputs = call(
+        finish_kernel,
+        "finish",
+        [VMEM] * 12,
+        (shape(sample_input.shape, BF16), shape(sample_grad.shape, BF16)),
         (
             kept_input,
             hidden,
             boundary_first,
             first_far,
-            packed_far,
-            own,
-            halo,
-            mix,
+            base,
+            hop_spread,
+            mix_wide,
             mix_bias,
+            grad,
+            back,
+            early_far,
+            kept_taps,
+        ),
+        scratch=(
+            pltpu.VMEM(sample_input.shape, BF16),
+            pltpu.VMEM(sample_grad.shape, BF16),
+            pltpu.VMEM((rows, 2 * sensors), BF16),
+            DMA((4,)),
         ),
         micros=2.0,
-    )
-    grad_inputs = call(
-        input_grad_kernel,
-        "input_grad",
-        [VMEM] * 4,
-        shape(sample_grad.shape, BF16),
-        (grad, back, early_far, kept_taps),
-        micros=1.2,
-    )
-    ready = {-2: (first_far,), -1: (outputs, grad_inputs)}
+        space=HBM,
+    )
+    ready = {-2: (first_far, base), -1: (outputs, grad_inputs)}
     for index, group in enumerate(rounds):
-        rounded = round_sums(total)
+        rounded = round_sums(total, has_biases)
         sent = rounded.astype(BF16)
         parts = [rounded] + [flip(sent, mask).astype(F32) for mask in group]
         parts[1] = after(parts[1], *ready.get(index - len(rounds), ()))

time: 29.8 us -> 29.6 us (level)
  Pallas kernels: 8.37 us -> 7.84 us
  waiting for transfers between devices: 5.81 us -> 6.13 us
    ppermute x6, waiting for transfers between devices: 1.01 us -> 1.92 us  [flip(): return lax.ppermute(value, AXES, pairs)]
    pallas_call x8, Pallas kernels: 8.37 us -> 7.84 us  [call(): pl.pallas_call(kernel, out_shape=out_shape, in_specs=in_specs, out_specs=...]
    ppermute x4, waiting for transfers between devices: 1.9 us -> 1.54 us  [swap(): lax.ppermute(value, axis, [(source, source ^ bit) for source in range(cou...]
  transfers between devices with their start and end apart: 12 -> 12, of which waited for: 6 -> 6; matrix products, arithmetic and copies ran while one was open for 0% -> 0% of each run, Pallas kernels for 16% -> 15%
where the time goes in v6:
time: 29.6 us; the launch traced here: 29.5 us
  starting transfers between devices  14.6 us (49%)
  Pallas kernels  7.84 us (26%)
  waiting for transfers between devices  6.13 us (21%)
  between operations  0.78 us (3%)
    pallas_call x8, Pallas kernels, call(): pl.pallas_call(kernel, out_shape=out_shape, in_specs=in_specs, out_specs=...  7.84 us
    ppermute x6, starting transfers between devices, flip(): return lax.ppermute(value, AXES, pairs)  7.11 us
    ppermute x2, starting transfers between devices, shift(): lax.ppermute(value, axis, [(source, (source + steps) % count) for source...  3.99 us
    ppermute x4, starting transfers between devices, swap(): lax.ppermute(value, axis, [(source, source ^ bit) for source in range(cou...  3.52 us
    ppermute x2, waiting for transfers between devices, shift(): lax.ppermute(value, axis, [(source, (source + steps) % count) for source...  2.67 us
    ppermute x6, waiting for transfers between devices, flip(): return lax.ppermute(value, AXES, pairs)  1.92 us
    ppermute x4, waiting for transfers between devices, swap(): lax.ppermute(value, axis, [(source, source ^ bit) for source in range(cou...  1.54 us
  transfers between devices with their start and end apart: 12, of which 6 were waited for; matrix products, arithmetic and copies ran while one was open for 0% of the time, Pallas kernels for 15%

profile of v6, /device:TPU:0, one launch (start us, length us, event | category | flops | bytes accessed | tf_op | source)
XLA Modules:
  0.0 29.5 jit_solution(2824495564412652413)
XLA Ops:
  0.6 1.7 %prepare.1 = (bf16[544,128]{1,0:T(8,128)(2,1)S(1)}, bf16[256,256]{1,0:T(8,128)(2,1)S(1)}, bf16[256,128]{1,0:T(8,128)(2,1)S(1)}, bf16[256,128]{1,0:T(8,128)(2,1)S...) custom-call(s32[2,8]{1,0:T(2,128)} %cols_hbm.1, s32[1,2]{1,0:T(1,128)} %counts_hbm.1, ...), custom_call_target="tpu_custom_call" | custom-call | bytes 7200000 | tf_op jit(solution)/shard_map/prepare/pallas_call | solution.py:624
  2.4 3.0 %collective-permute-start = (bf16[544,128]{1,0:T(8,128)(2,1)S(1)}, bf16[544,128]{1,0:T(8,128)(2,1)S(1)}, u32[]{:S(2)}, u32[]{:S(2)}) collective-permute-start(bf16[544,128]{1,0:T(8,128)(2,1)S(1)} %get-tuple-element.42.own_packed_ref), channel_id=1, source_target_pairs={{0,4},{4,0},{1,5},{5,1},{2,6},{6,2},{3,7},{7,3},{8,12},{12,8},{9,1... | collective-permute-start | bytes 417800 | tf_op jit(solution)/shard_map/ppermute | solution.py:640
  5.4 1.6 %collective-permute-start.1 = (bf16[2,64,256]{2,1,0:T(8,128)(2,1)S(1)}, bf16[2,64,256]{2,1,0:T(8,128)(2,1)S(1)}, u32[]{:S(2)}, u32[]{:S(2)}) collective-permute-start(bf16[2,64,256]{2,1,0:T(8,128)(2,1)S(1)} %get-tuple-element.43), channel_id=1, source_target_pairs={{0,1},{1,2},{2,3},{3,0},{4,5},{5,6},{6,7},{7,4},{8,9},{9,10},{10,1... | collective-permute-start | bytes 196616 | tf_op jit(solution)/shard_map/ppermute | solution.py:645
  7.0 1.8 %forward.1 = (bf16[512,256]{1,0:T(8,128)(2,1)S(1)}, f32[8,128,256]{2,1,0:T(8,128)S(1)}, bf16[272,2048]{1,0:T(8,128)(2,1)S(1)}, f32[512,512]{1,0:T(8,128)S(1)}, b...) custom-call(bf16[8,64,256]{2,1,0:T(8,128)(2,1)} %bitcast.11, ...), custom_call_target="tpu_custom_call" | custom-call | bytes 5400000 | tf_op jit(solution)/shard_map/forward/pallas_call | solution.py:624
  8.8 2.7 %collective-permute-done.1.border_ref = bf16[2,64,256]{2,1,0:T(8,128)(2,1)S(1)} collective-permute-done((bf16[2,64,256]{2,1,0:T(8,128)(2,1)S(1)}, bf16[2,64,256]{2,1,0:T(8,128)(2,1)S(1)}, u32[]{:S(2)}, u32[]{:S(2)}) %collective-permute-start.1) | collective-permute-done | bytes 65568 | tf_op jit(solution)/shard_map/ppermute | solution.py:645
  11.5 0.0 collective-permute-done.packed_ref
  11.5 1.1 %backward.1 = (f32[120,128]{1,0:T(8,128)S(1)}, f32[120,128]{1,0:T(8,128)S(1)}, bf16[8,128,256]{2,1,0:T(8,128)(2,1)S(1)}, bf16[512,256]{1,0:T(8,128)(2,1)S(1)}) custom-call(bf16[512,256]{1,0:T(8,128)(2,1)S(1)} %get-tuple-element.38.grad_ref, bf16[544,128]{1,0:T(8,128)(2,1)S(1)} %get-tuple-element.42.own_packed_ref, ...), custom_call_target="tpu_custom_call" | custom-call | bytes 7200000 | tf_op jit(solution)/shard_map/backward/pallas_call | solution.py:624
  12.6 0.1 collective-permute-start.4
  12.7 0.6 %boundary.1.own_boundary_ref = bf16[512,128]{1,0:T(8,128)(2,1)S(1)} custom-call(bf16[512,256]{1,0:T(8,128)(2,1)S(1)} %get-tuple-element.52.hidden_ref, bf16[256,256]{1,0:T(8,128)(2,1)S(1)} %get-tuple-element.39.own_ref, bf16[256,128]{1,0:T(8,128)(2,1)S(1)} %get-tuple-element.40.chosen_ref), custom_call_target="tpu_custom_call" | custom-call | bytes 1080000 | tf_op jit(solution)/shard_map/boundary/pallas_call | solution.py:624
  13.2 0.4 %collective-permute-start.2 = (bf16[512,128]{1,0:T(8,128)(2,1)S(1)}, bf16[512,128]{1,0:T(8,128)(2,1)S(1)}, u32[]{:S(2)}, u32[]{:S(2)}) collective-permute-start(bf16[512,128]{1,0:T(8,128)(2,1)S(1)} %boundary.1.own_boundary_ref), channel_id=1, source_target_pairs={{0,4},{4,0},{1,5},{5,1},{2,6},{6,2},{3,7},{7,3},{8,12},{12,8},{9,1... | collective-permute-start | bytes 393224 | tf_op jit(solution)/shard_map/ppermute | solution.py:640
  13.6 0.3 %collective-permute-done.4 = f32[120,128]{1,0:T(8,128)S(1)} collective-permute-done((f32[120,128]{1,0:T(8,128)S(1)}, f32[120,128]{1,0:T(8,128)S(1)}, u32[]{:S(2)}, u32[]{:S(2)}) %collective-permute-start.4) | collective-permute-done | bytes 61472 | tf_op jit(solution)/shard_map/ppermute | solution.py:640
  13.9 2.4 %collective-permute-start.5 = (bf16[120,128]{1,0:T(8,128)(2,1)S(1)}, bf16[120,128]{1,0:T(8,128)(2,1)S(1)}, u32[]{:S(2)}, u32[]{:S(2)}) collective-permute-start(bf16[120,128]{1,0:T(8,128)(2,1)S(1)} %fusion), channel_id=1, source_target_pairs={{0,20},{1,21},{2,22},{3,23},{4,16},{5,17},{6,18},{7,19},{8,28},{9,... | collective-permute-start | bytes 92168 | tf_op jit(solution)/shard_map/ppermute | solution.py:656
  16.4 0.5 %collective-permute-start.6 = (bf16[120,128]{1,0:T(8,128)(2,1)S(1)}, bf16[120,128]{1,0:T(8,128)(2,1)S(1)}, u32[]{:S(2)}, u32[]{:S(2)}) collective-permute-start(bf16[120,128]{1,0:T(8,128)(2,1)S(1)} %fusion), channel_id=1, source_target_pairs={{0,16},{1,17},{2,18},{3,19},{4,20},{5,21},{6,22},{7,23},{8,24},{9,... | collective-permute-start | bytes 92168 | tf_op jit(solution)/shard_map/ppermute | solution.py:656
  16.9 0.6 %collective-permute-start.7 = (bf16[120,128]{1,0:T(8,128)(2,1)S(1)}, bf16[120,128]{1,0:T(8,128)(2,1)S(1)}, u32[]{:S(2)}, u32[]{:S(2)}) collective-permute-start(bf16[120,128]{1,0:T(8,128)(2,1)S(1)} %fusion), channel_id=1, source_target_pairs={{0,4},{1,5},{2,6},{3,7},{4,0},{5,1},{6,2},{7,3},{8,12},{9,13},{10,... | collective-permute-start | bytes 92168 | tf_op jit(solution)/shard_map/ppermute | solution.py:656
  17.5 0.2 early.1
  17.6 2.4 %collective-permute-start.3 = (bf16[2,64,256]{2,1,0:T(8,128)(2,1)S(1)}, bf16[2,64,256]{2,1,0:T(8,128)(2,1)S(1)}, u32[]{:S(2)}, u32[]{:S(2)}) collective-permute-start(bf16[2,64,256]{2,1,0:T(8,128)(2,1)S(1)} %early.1), channel_id=1, source_target_pairs={{0,3},{1,0},{2,1},{3,2},{4,7},{5,4},{6,5},{7,6},{8,11},{9,8},{10,9... | collective-permute-start | bytes 196616 | tf_op jit(solution)/shard_map/ppermute | solution.py:645
  20.1 0.5 %hops.1 = (f32[512,512]{1,0:T(8,128)S(1)}, bf16[256,512]{1,0:T(8,128)(2,1)S(1)}) custom-call(bf16[512,256]{1,0:T(8,128)(2,1)S(1)} %get-tuple-element.52.hidden_ref, bf16[544,128]{1,0:T(8,128)(2,1)S(1)} %collective-permute-done.packed_ref, bf16[256,256]{1,0:T(8,128)(2,1)S(1)} %get-tuple-element.39.own_ref, bf16[256,128]{1,0:T(8,128)(2,1)S(1)} %get-tuple-element.53.halo_ref), custom_call_target="tpu_custom_call" | custom-call | bytes 1800000 | tf_op jit(solution)/shard_map/hops/pallas_call | solution.py:624
  20.5 0.0 collective-permute-done.5
  20.5 0.0 collective-permute-done.2.boundary_ref
  20.6 0.0 collective-permute-done.6
  20.6 0.2 collective-permute-done.7
  20.9 0.9 %collective-permute-start.8 = (bf16[120,128]{1,0:T(8,128)(2,1)S(1)}, bf16[120,128]{1,0:T(8,128)(2,1)S(1)}, u32[]{:S(2)}, u32[]{:S(2)}) collective-permute-start(bf16[120,128]{1,0:T(8,128)(2,1)S(1)} %fusion.1), channel_id=1, source_target_pairs={{0,2},{1,3},{2,0},{3,1},{4,6},{5,7},{6,4},{7,5},{8,10},{9,11},{10,... | collective-permute-start | bytes 92168 | tf_op jit(solution)/shard_map/ppermute | solution.py:656
  21.7 1.4 %collective-permute-start.10 = (bf16[120,128]{1,0:T(8,128)(2,1)S(1)}, bf16[120,128]{1,0:T(8,128)(2,1)S(1)}, u32[]{:S(2)}, u32[]{:S(2)}) collective-permute-start(bf16[120,128]{1,0:T(8,128)(2,1)S(1)} %fusion.1), channel_id=1, source_target_pairs={{0,3},{1,2},{2,1},{3,0},{4,7},{5,6},{6,5},{7,4},{8,11},{9,10},{10,... | collective-permute-start | bytes 92168 | tf_op jit(solution)/shard_map/ppermute | solution.py:656
  23.1 1.4 %collective-permute-start.9 = (bf16[120,128]{1,0:T(8,128)(2,1)S(1)}, bf16[120,128]{1,0:T(8,128)(2,1)S(1)}, u32[]{:S(2)}, u32[]{:S(2)}) collective-permute-start(bf16[120,128]{1,0:T(8,128)(2,1)S(1)} %fusion.1), channel_id=1, source_target_pairs={{0,1},{1,0},{2,3},{3,2},{4,5},{5,4},{6,7},{7,6},{8,9},{9,8},{10,11... | collective-permute-start | bytes 92168 | tf_op jit(solution)/shard_map/ppermute | solution.py:656
  24.4 0.0 collective-permute-done.3.early_ref
  24.4 1.3 %finish.1 = (bf16[8,64,256]{2,1,0:T(8,128)(2,1)}, bf16[8,64,256]{2,1,0:T(8,128)(2,1)}) custom-call(bf16[8,64,256]{2,1,0:T(8,128)(2,1)S(1)} %get-tuple-element.41.input_ref, bf16[512,256]{1,0:T(8,128)(2,1)S(1)} %get-tuple-element.52.hidden_ref, bf16[512,128]{1,0:T(8,128)(2,1)S(1)} %boundary.1.own_boundary_ref, ...), custom_call_target="tpu_custom_call" | custom-call | bytes 7200000 | tf_op jit(solution)/shard_map/finish/pallas_call | solution.py:624
  25.7 0.2 collective-permute-done.8
  25.9 1.5 %collective-permute-done.10 = bf16[120,128]{1,0:T(8,128)(2,1)S(1)} collective-permute-done((bf16[120,128]{1,0:T(8,128)(2,1)S(1)}, bf16[120,128]{1,0:T(8,128)(2,1)S(1)}, u32[]{:S(2)}, u32[]{:S(2)}) %collective-permute-start.10) | collective-permute-done | bytes 30752 | tf_op jit(solution)/shard_map/ppermute | solution.py:656
  27.4 0.0 collective-permute-done.9
  27.4 0.1 collective-permute-start.11
  27.5 1.2 %collective-permute-done.11.other_ref = f32[120,128]{1,0:T(8,128)S(1)} collective-permute-done((f32[120,128]{1,0:T(8,128)S(1)}, f32[120,128]{1,0:T(8,128)S(1)}, u32[]{:S(2)}, u32[]{:S(2)}) %collective-permute-start.11) | collective-permute-done | bytes 61472 | tf_op jit(solution)/shard_map/ppermute | solution.py:640
  28.7 0.7 %final.1 = (f32[2,64,128]{2,1,0:T(8,128)}, f32[1,128]{1,0:T(1,128)}, f32[3,64,64]{2,1,0:T(8,128)}, f32[1,64]{1,0:T(1,128)}) custom-call(f32[120,128]{1,0:T(8,128)S(1)} %add_add_fusion.kept_ref, f32[120,128]{1,0:T(8,128)S(1)} %collective-permute-done.11.other_ref), custom_call_target="tpu_custom_call" | custom-call | bytes 3600000 | tf_op jit(solution)/shard_map/final/pallas_call | solution.py:624
  (9 shorter events, 0.1 us)
Async XLA Ops:
  2.4 9.1 %collective-permute-start = (bf16[544,128]{1,0:T(8,128)(2,1)S(1)}, bf16[544,128]{1,0:T(8,128)(2,1)S(1)}, u32[]{:S(2)}, u32[]{:S(2)}) collective-permute-start(bf16[544,128]{1,0:T(8,128)(2,1)S(1)} %get-tuple-element.42.own_packed_ref), channel_id=1, source_target_pairs={{0,4},{4,0},{1,5},{5,1},{2,6},{6,2},{3,7},{7,3},{8,12},{12,8},{9,1... | collective-permute-start | bytes 417800 | tf_op jit(solution)/shard_map/ppermute | solution.py:640
  5.4 6.1 %collective-permute-start.1 = (bf16[2,64,256]{2,1,0:T(8,128)(2,1)S(1)}, bf16[2,64,256]{2,1,0:T(8,128)(2,1)S(1)}, u32[]{:S(2)}, u32[]{:S(2)}) collective-permute-start(bf16[2,64,256]{2,1,0:T(8,128)(2,1)S(1)} %get-tuple-element.43), channel_id=1, source_target_pairs={{0,1},{1,2},{2,3},{3,0},{4,5},{5,6},{6,7},{7,4},{8,9},{9,10},{10,1... | collective-permute-start | bytes 196616 | tf_op jit(solution)/shard_map/ppermute | solution.py:645
  12.6 1.3 %collective-permute-start.4 = (f32[120,128]{1,0:T(8,128)S(1)}, f32[120,128]{1,0:T(8,128)S(1)}, u32[]{:S(2)}, u32[]{:S(2)}) collective-permute-start(f32[120,128]{1,0:T(8,128)S(1)} %get-tuple-element.63), channel_id=1, source_target_pairs={{0,8},{8,0},{16,24},{24,16},{1,9},{9,1},{17,25},{25,17},{2,10},{10... | collective-permute-start | bytes 184328 | tf_op jit(solution)/shard_map/ppermute | solution.py:640
  13.2 7.3 %collective-permute-start.2 = (bf16[512,128]{1,0:T(8,128)(2,1)S(1)}, bf16[512,128]{1,0:T(8,128)(2,1)S(1)}, u32[]{:S(2)}, u32[]{:S(2)}) collective-permute-start(bf16[512,128]{1,0:T(8,128)(2,1)S(1)} %boundary.1.own_boundary_ref), channel_id=1, source_target_pairs={{0,4},{4,0},{1,5},{5,1},{2,6},{6,2},{3,7},{7,3},{8,12},{12,8},{9,1... | collective-permute-start | bytes 393224 | tf_op jit(solution)/shard_map/ppermute | solution.py:640
  13.9 6.6 %collective-permute-start.5 = (bf16[120,128]{1,0:T(8,128)(2,1)S(1)}, bf16[120,128]{1,0:T(8,128)(2,1)S(1)}, u32[]{:S(2)}, u32[]{:S(2)}) collective-permute-start(bf16[120,128]{1,0:T(8,128)(2,1)S(1)} %fusion), channel_id=1, source_target_pairs={{0,20},{1,21},{2,22},{3,23},{4,16},{5,17},{6,18},{7,19},{8,28},{9,... | collective-permute-start | bytes 92168 | tf_op jit(solution)/shard_map/ppermute | solution.py:656
  16.4 4.2 %collective-permute-start.6 = (bf16[120,128]{1,0:T(8,128)(2,1)S(1)}, bf16[120,128]{1,0:T(8,128)(2,1)S(1)}, u32[]{:S(2)}, u32[]{:S(2)}) collective-permute-start(bf16[120,128]{1,0:T(8,128)(2,1)S(1)} %fusion), channel_id=1, source_target_pairs={{0,16},{1,17},{2,18},{3,19},{4,20},{5,21},{6,22},{7,23},{8,24},{9,... | collective-permute-start | bytes 92168 | tf_op jit(solution)/shard_map/ppermute | solution.py:656
  16.9 3.9 %collective-permute-start.7 = (bf16[120,128]{1,0:T(8,128)(2,1)S(1)}, bf16[120,128]{1,0:T(8,128)(2,1)S(1)}, u32[]{:S(2)}, u32[]{:S(2)}) collective-permute-start(bf16[120,128]{1,0:T(8,128)(2,1)S(1)} %fusion), channel_id=1, source_target_pairs={{0,4},{1,5},{2,6},{3,7},{4,0},{5,1},{6,2},{7,3},{8,12},{9,13},{10,... | collective-permute-start | bytes 92168 | tf_op jit(solution)/shard_map/ppermute | solution.py:656
  17.6 6.8 %collective-permute-start.3 = (bf16[2,64,256]{2,1,0:T(8,128)(2,1)S(1)}, bf16[2,64,256]{2,1,0:T(8,128)(2,1)S(1)}, u32[]{:S(2)}, u32[]{:S(2)}) collective-permute-start(bf16[2,64,256]{2,1,0:T(8,128)(2,1)S(1)} %early.1), channel_id=1, source_target_pairs={{0,3},{1,0},{2,1},{3,2},{4,7},{5,4},{6,5},{7,6},{8,11},{9,8},{10,9... | collective-permute-start | bytes 196616 | tf_op jit(solution)/shard_map/ppermute | solution.py:645
  20.9 5.0 %collective-permute-start.8 = (bf16[120,128]{1,0:T(8,128)(2,1)S(1)}, bf16[120,128]{1,0:T(8,128)(2,1)S(1)}, u32[]{:S(2)}, u32[]{:S(2)}) collective-permute-start(bf16[120,128]{1,0:T(8,128)(2,1)S(1)} %fusion.1), channel_id=1, source_target_pairs={{0,2},{1,3},{2,0},{3,1},{4,6},{5,7},{6,4},{7,5},{8,10},{9,11},{10,... | collective-permute-start | bytes 92168 | tf_op jit(solution)/shard_map/ppermute | solution.py:656
  21.7 5.7 %collective-permute-start.10 = (bf16[120,128]{1,0:T(8,128)(2,1)S(1)}, bf16[120,128]{1,0:T(8,128)(2,1)S(1)}, u32[]{:S(2)}, u32[]{:S(2)}) collective-permute-start(bf16[120,128]{1,0:T(8,128)(2,1)S(1)} %fusion.1), channel_id=1, source_target_pairs={{0,3},{1,2},{2,1},{3,0},{4,7},{5,6},{6,5},{7,4},{8,11},{9,10},{10,... | collective-permute-start | bytes 92168 | tf_op jit(solution)/shard_map/ppermute | solution.py:656
  23.1 4.3 %collective-permute-start.9 = (bf16[120,128]{1,0:T(8,128)(2,1)S(1)}, bf16[120,128]{1,0:T(8,128)(2,1)S(1)}, u32[]{:S(2)}, u32[]{:S(2)}) collective-permute-start(bf16[120,128]{1,0:T(8,128)(2,1)S(1)} %fusion.1), channel_id=1, source_target_pairs={{0,1},{1,0},{2,3},{3,2},{4,5},{5,4},{6,7},{7,6},{8,9},{9,8},{10,11... | collective-permute-start | bytes 92168 | tf_op jit(solution)/shard_map/ppermute | solution.py:656
  27.4 1.3 %collective-permute-start.11 = (f32[120,128]{1,0:T(8,128)S(1)}, f32[120,128]{1,0:T(8,128)S(1)}, u32[]{:S(2)}, u32[]{:S(2)}) collective-permute-start(f32[120,128]{1,0:T(8,128)S(1)} %add_add_fusion.kept_ref), channel_id=1, source_target_pairs={{0,8},{8,0},{16,24},{24,16},{1,9},{9,1},{17,25},{25,17},{2,10},{10... | collective-permute-start | bytes 184328 | tf_op jit(solution)/shard_map/ppermute | solution.py:640

commit v7 on v6

--- a/solution.py
+++ b/solution.py
@@ -370,6 +370,7 @@
     mixing_ref,
     mix_bias_ref,
     mix_wide_ref,
+    boundary_ref,
     sems,
 ):
     copies = fetch(
@@ -409,6 +410,8 @@
         earlier = input_ref[t - DILATION_SIZE]
         preact = mm(taps, jnp.concatenate([earlier, input_ref[t]], 0)) + bias
         gate_step(t, earlier, input_ref, preact, hidden_ref, slopes_ref, right_ref)
+    hidden = hidden_ref[DILATION_SIZE * chans :, :]
+    boundary_ref[...] = boundary_rows(hidden, own, chosen_ref[...])
 
 
 def backward_kernel(
@@ -501,9 +504,11 @@
         early_ref[t] = mm(taps_ref[0], back_ref[t]).astype(BF16)
 
 
-def boundary_kernel(hidden_ref, own_ref, chosen_ref, boundary_ref):
-    hidden = hidden_ref[: boundary_ref.shape[0], :]
-    boundary_ref[...] = boundary_rows(hidden, own_ref[...], chosen_ref[...])
+def boundary_kernel(hidden_ref, late_ref, own_ref, chosen_ref, boundary_ref):
+    early_rows = boundary_ref.shape[0] - late_ref.shape[0]
+    hidden = hidden_ref[:early_rows, :]
+    boundary_ref[:early_rows, :] = boundary_rows(hidden, own_ref[...], chosen_ref[...])
+    boundary_ref[early_rows:, :] = late_ref[...]
 
 
 def hops_kernel(hidden_ref, packed_ref, own_ref, halo_ref, base_ref, spread_ref):
@@ -727,7 +732,7 @@
     )
     packed_far = swap(packed, "space", 1)
     border = shift(tail, "tm", 1)
-    hidden_late, slopes, right, near, spread, kept_input, kept_taps, turned_taps, bias, mix, mixing, mix_bias, mix_wide = call(
+    hidden_late, slopes, right, near, spread, kept_input, kept_taps, turned_taps, bias, mix, mixing, mix_bias, mix_wide, boundary_late = call(
         forward_kernel,
         "forward",
         [HBM] * 5 + [VMEM] * 3,
@@ -745,6 +750,7 @@
             shape((chans, 3 * chans), BF16),
             shape((1, chans), F32),
             shape((chans, 3 * chans), BF16),
+            shape((rows - border_rows, wide), BF16),
         ),
         (
             sample_input,
@@ -809,9 +815,9 @@
     boundary_first = call(
         boundary_kernel,
         "boundary",
-        [VMEM] * 3,
+        [VMEM] * 4,
         shape((rows, wide), BF16),
-        (hidden, own, chosen),
+        (hidden, boundary_late, own, chosen),
         micros=0.3,
     )
     first_far = swap(boundary_first, "space", 1)

time: 29.6 us -> 29.4 us (level)
  transfers between devices with their start and end apart: 12 -> 12, of which waited for: 6 -> 6; matrix products, arithmetic and copies ran while one was open for 0% -> 0% of each run, Pallas kernels for 15% -> 14%
where the time goes in v7:
time: 29.4 us; the launch traced here: 29.3 us
  starting transfers between devices  14.4 us (49%)
  Pallas kernels  7.65 us (26%)
  waiting for transfers between devices  6.32 us (21%)
  between operations  0.78 us (3%)
    pallas_call x8, Pallas kernels, call(): pl.pallas_call(kernel, out_shape=out_shape, in_specs=in_specs, out_specs=...  7.65 us
    ppermute x6, starting transfers between devices, flip(): return lax.ppermute(value, AXES, pairs)  7.11 us
    ppermute x2, starting transfers between devices, shift(): lax.ppermute(value, axis, [(source, (source + steps) % count) for source...  3.79 us
    ppermute x4, starting transfers between devices, swap(): lax.ppermute(value, axis, [(source, source ^ bit) for source in range(cou...  3.52 us
    ppermute x2, waiting for transfers between devices, shift(): lax.ppermute(value, axis, [(source, (source + steps) % count) for source...  2.66 us
    ppermute x6, waiting for transfers between devices, flip(): return lax.ppermute(value, AXES, pairs)  1.92 us
    ppermute x4, waiting for transfers between devices, swap(): lax.ppermute(value, axis, [(source, source ^ bit) for source in range(cou...  1.74 us
  transfers between devices with their start and end apart: 12, of which 6 were waited for; matrix products, arithmetic and copies ran while one was open for 0% of the time, Pallas kernels for 14%

profile of v7, /device:TPU:0, one launch (start us, length us, event | category | flops | bytes accessed | tf_op | source)
XLA Modules:
  0.0 29.3 jit_solution(3383630484280591231)
XLA Ops:
  0.6 1.7 %prepare.1 = (bf16[544,128]{1,0:T(8,128)(2,1)S(1)}, bf16[256,256]{1,0:T(8,128)(2,1)S(1)}, bf16[256,128]{1,0:T(8,128)(2,1)S(1)}, bf16[256,128]{1,0:T(8,128)(2,1)S...) custom-call(s32[2,8]{1,0:T(2,128)} %cols_hbm.1, s32[1,2]{1,0:T(1,128)} %counts_hbm.1, ...), custom_call_target="tpu_custom_call" | custom-call | bytes 7200000 | tf_op jit(solution)/shard_map/prepare/pallas_call | solution.py:629
  2.4 3.0 %collective-permute-start = (bf16[544,128]{1,0:T(8,128)(2,1)S(1)}, bf16[544,128]{1,0:T(8,128)(2,1)S(1)}, u32[]{:S(2)}, u32[]{:S(2)}) collective-permute-start(bf16[544,128]{1,0:T(8,128)(2,1)S(1)} %get-tuple-element.43.own_packed_ref), channel_id=1, source_target_pairs={{0,4},{4,0},{1,5},{5,1},{2,6},{6,2},{3,7},{7,3},{8,12},{12,8},{9,1... | collective-permute-start | bytes 417800 | tf_op jit(solution)/shard_map/ppermute | solution.py:645
  5.4 1.6 %collective-permute-start.1 = (bf16[2,64,256]{2,1,0:T(8,128)(2,1)S(1)}, bf16[2,64,256]{2,1,0:T(8,128)(2,1)S(1)}, u32[]{:S(2)}, u32[]{:S(2)}) collective-permute-start(bf16[2,64,256]{2,1,0:T(8,128)(2,1)S(1)} %get-tuple-element.44), channel_id=1, source_target_pairs={{0,1},{1,2},{2,3},{3,0},{4,5},{5,6},{6,7},{7,4},{8,9},{9,10},{10,1... | collective-permute-start | bytes 196616 | tf_op jit(solution)/shard_map/ppermute | solution.py:650
  7.0 1.8 %forward.1 = (bf16[512,256]{1,0:T(8,128)(2,1)S(1)}, f32[8,128,256]{2,1,0:T(8,128)S(1)}, bf16[272,2048]{1,0:T(8,128)(2,1)S(1)}, f32[512,512]{1,0:T(8,128)S(1)}, b...) custom-call(bf16[8,64,256]{2,1,0:T(8,128)(2,1)} %bitcast.11, ...), custom_call_target="tpu_custom_call" | custom-call | bytes 5400000 | tf_op jit(solution)/shard_map/forward/pallas_call | solution.py:629
  8.8 2.7 %collective-permute-done.1.border_ref = bf16[2,64,256]{2,1,0:T(8,128)(2,1)S(1)} collective-permute-done((bf16[2,64,256]{2,1,0:T(8,128)(2,1)S(1)}, bf16[2,64,256]{2,1,0:T(8,128)(2,1)S(1)}, u32[]{:S(2)}, u32[]{:S(2)}) %collective-permute-start.1) | collective-permute-done | bytes 65568 | tf_op jit(solution)/shard_map/ppermute | solution.py:650
  11.5 0.0 collective-permute-done.packed_ref
  11.5 1.1 %backward.1 = (f32[120,128]{1,0:T(8,128)S(1)}, f32[120,128]{1,0:T(8,128)S(1)}, bf16[8,128,256]{2,1,0:T(8,128)(2,1)S(1)}, bf16[512,256]{1,0:T(8,128)(2,1)S(1)}) custom-call(bf16[512,256]{1,0:T(8,128)(2,1)S(1)} %get-tuple-element.39.grad_ref, bf16[544,128]{1,0:T(8,128)(2,1)S(1)} %get-tuple-element.43.own_packed_ref, ...), custom_call_target="tpu_custom_call" | custom-call | bytes 7200000 | tf_op jit(solution)/shard_map/backward/pallas_call | solution.py:629
  12.6 0.1 collective-permute-start.4
  12.7 0.4 %boundary.1.own_boundary_ref = bf16[512,128]{1,0:T(8,128)(2,1)S(1)} custom-call(bf16[512,256]{1,0:T(8,128)(2,1)S(1)} %get-tuple-element.53.hidden_ref, bf16[384,128]{1,0:T(8,128)(2,1)S(1)} %get-tuple-element.54.late_ref, bf16[256,256]{1,0:T(8,128)(2,1)S(1)} %get-tuple-element.40.own_ref, bf16[256,128]{1,0:T(8,128)(2,1)S(1)} %get-tuple-element.41.chosen_ref), custom_call_target="tpu_custom_call" | custom-call | bytes 1080000 | tf_op jit(solution)/shard_map/boundary/pallas_call | solution.py:629
  13.0 0.3 %collective-permute-start.2 = (bf16[512,128]{1,0:T(8,128)(2,1)S(1)}, bf16[512,128]{1,0:T(8,128)(2,1)S(1)}, u32[]{:S(2)}, u32[]{:S(2)}) collective-permute-start(bf16[512,128]{1,0:T(8,128)(2,1)S(1)} %boundary.1.own_boundary_ref), channel_id=1, source_target_pairs={{0,4},{4,0},{1,5},{5,1},{2,6},{6,2},{3,7},{7,3},{8,12},{12,8},{9,1... | collective-permute-start | bytes 393224 | tf_op jit(solution)/shard_map/ppermute | solution.py:645
  13.4 0.5 %collective-permute-done.4 = f32[120,128]{1,0:T(8,128)S(1)} collective-permute-done((f32[120,128]{1,0:T(8,128)S(1)}, f32[120,128]{1,0:T(8,128)S(1)}, u32[]{:S(2)}, u32[]{:S(2)}) %collective-permute-start.4) | collective-permute-done | bytes 61472 | tf_op jit(solution)/shard_map/ppermute | solution.py:645
  13.9 2.2 %collective-permute-start.5 = (bf16[120,128]{1,0:T(8,128)(2,1)S(1)}, bf16[120,128]{1,0:T(8,128)(2,1)S(1)}, u32[]{:S(2)}, u32[]{:S(2)}) collective-permute-start(bf16[120,128]{1,0:T(8,128)(2,1)S(1)} %fusion), channel_id=1, source_target_pairs={{0,20},{1,21},{2,22},{3,23},{4,16},{5,17},{6,18},{7,19},{8,28},{9,... | collective-permute-start | bytes 92168 | tf_op jit(solution)/shard_map/ppermute | solution.py:661
  16.2 0.5 %collective-permute-start.6 = (bf16[120,128]{1,0:T(8,128)(2,1)S(1)}, bf16[120,128]{1,0:T(8,128)(2,1)S(1)}, u32[]{:S(2)}, u32[]{:S(2)}) collective-permute-start(bf16[120,128]{1,0:T(8,128)(2,1)S(1)} %fusion), channel_id=1, source_target_pairs={{0,16},{1,17},{2,18},{3,19},{4,20},{5,21},{6,22},{7,23},{8,24},{9,... | collective-permute-start | bytes 92168 | tf_op jit(solution)/shard_map/ppermute | solution.py:661
  16.7 0.8 %collective-permute-start.7 = (bf16[120,128]{1,0:T(8,128)(2,1)S(1)}, bf16[120,128]{1,0:T(8,128)(2,1)S(1)}, u32[]{:S(2)}, u32[]{:S(2)}) collective-permute-start(bf16[120,128]{1,0:T(8,128)(2,1)S(1)} %fusion), channel_id=1, source_target_pairs={{0,4},{1,5},{2,6},{3,7},{4,0},{5,1},{6,2},{7,3},{8,12},{9,13},{10,... | collective-permute-start | bytes 92168 | tf_op jit(solution)/shard_map/ppermute | solution.py:661
  17.5 0.2 early.1
  17.6 2.2 %collective-permute-start.3 = (bf16[2,64,256]{2,1,0:T(8,128)(2,1)S(1)}, bf16[2,64,256]{2,1,0:T(8,128)(2,1)S(1)}, u32[]{:S(2)}, u32[]{:S(2)}) collective-permute-start(bf16[2,64,256]{2,1,0:T(8,128)(2,1)S(1)} %early.1), channel_id=1, source_target_pairs={{0,3},{1,0},{2,1},{3,2},{4,7},{5,4},{6,5},{7,6},{8,11},{9,8},{10,9... | collective-permute-start | bytes 196616 | tf_op jit(solution)/shard_map/ppermute | solution.py:650
  19.9 0.5 %hops.1 = (f32[512,512]{1,0:T(8,128)S(1)}, bf16[256,512]{1,0:T(8,128)(2,1)S(1)}) custom-call(bf16[512,256]{1,0:T(8,128)(2,1)S(1)} %get-tuple-element.53.hidden_ref, bf16[544,128]{1,0:T(8,128)(2,1)S(1)} %collective-permute-done.packed_ref, bf16[256,256]{1,0:T(8,128)(2,1)S(1)} %get-tuple-element.40.own_ref, bf16[256,128]{1,0:T(8,128)(2,1)S(1)} %get-tuple-element.55.halo_ref), custom_call_target="tpu_custom_call" | custom-call | bytes 1800000 | tf_op jit(solution)/shard_map/hops/pallas_call | solution.py:629
  20.3 0.0 collective-permute-done.5
  20.3 0.0 collective-permute-done.2.boundary_ref
  20.4 0.0 collective-permute-done.6
  20.4 0.2 collective-permute-done.7
  20.7 0.8 %collective-permute-start.8 = (bf16[120,128]{1,0:T(8,128)(2,1)S(1)}, bf16[120,128]{1,0:T(8,128)(2,1)S(1)}, u32[]{:S(2)}, u32[]{:S(2)}) collective-permute-start(bf16[120,128]{1,0:T(8,128)(2,1)S(1)} %fusion.1), channel_id=1, source_target_pairs={{0,2},{1,3},{2,0},{3,1},{4,6},{5,7},{6,4},{7,5},{8,10},{9,11},{10,... | collective-permute-start | bytes 92168 | tf_op jit(solution)/shard_map/ppermute | solution.py:661
  21.5 1.4 %collective-permute-start.10 = (bf16[120,128]{1,0:T(8,128)(2,1)S(1)}, bf16[120,128]{1,0:T(8,128)(2,1)S(1)}, u32[]{:S(2)}, u32[]{:S(2)}) collective-permute-start(bf16[120,128]{1,0:T(8,128)(2,1)S(1)} %fusion.1), channel_id=1, source_target_pairs={{0,3},{1,2},{2,1},{3,0},{4,7},{5,6},{6,5},{7,4},{8,11},{9,10},{10,... | collective-permute-start | bytes 92168 | tf_op jit(solution)/shard_map/ppermute | solution.py:661
  22.9 1.4 %collective-permute-start.9 = (bf16[120,128]{1,0:T(8,128)(2,1)S(1)}, bf16[120,128]{1,0:T(8,128)(2,1)S(1)}, u32[]{:S(2)}, u32[]{:S(2)}) collective-permute-start(bf16[120,128]{1,0:T(8,128)(2,1)S(1)} %fusion.1), channel_id=1, source_target_pairs={{0,1},{1,0},{2,3},{3,2},{4,5},{5,4},{6,7},{7,6},{8,9},{9,8},{10,11... | collective-permute-start | bytes 92168 | tf_op jit(solution)/shard_map/ppermute | solution.py:661
  24.2 0.0 collective-permute-done.3.early_ref
  24.2 1.3 %finish.1 = (bf16[8,64,256]{2,1,0:T(8,128)(2,1)}, bf16[8,64,256]{2,1,0:T(8,128)(2,1)}) custom-call(bf16[8,64,256]{2,1,0:T(8,128)(2,1)S(1)} %get-tuple-element.42.input_ref, bf16[512,256]{1,0:T(8,128)(2,1)S(1)} %get-tuple-element.53.hidden_ref, bf16[512,128]{1,0:T(8,128)(2,1)S(1)} %boundary.1.own_boundary_ref, ...), custom_call_target="tpu_custom_call" | custom-call | bytes 7200000 | tf_op jit(solution)/shard_map/finish/pallas_call | solution.py:629
  25.5 0.2 collective-permute-done.8
  25.7 1.5 %collective-permute-done.10 = bf16[120,128]{1,0:T(8,128)(2,1)S(1)} collective-permute-done((bf16[120,128]{1,0:T(8,128)(2,1)S(1)}, bf16[120,128]{1,0:T(8,128)(2,1)S(1)}, u32[]{:S(2)}, u32[]{:S(2)}) %collective-permute-start.10) | collective-permute-done | bytes 30752 | tf_op jit(solution)/shard_map/ppermute | solution.py:661
  27.2 0.0 collective-permute-done.9
  27.2 0.1 collective-permute-start.11
  27.3 1.2 %collective-permute-done.11.other_ref = f32[120,128]{1,0:T(8,128)S(1)} collective-permute-done((f32[120,128]{1,0:T(8,128)S(1)}, f32[120,128]{1,0:T(8,128)S(1)}, u32[]{:S(2)}, u32[]{:S(2)}) %collective-permute-start.11) | collective-permute-done | bytes 61472 | tf_op jit(solution)/shard_map/ppermute | solution.py:645
  28.5 0.7 %final.1 = (f32[2,64,128]{2,1,0:T(8,128)}, f32[1,128]{1,0:T(1,128)}, f32[3,64,64]{2,1,0:T(8,128)}, f32[1,64]{1,0:T(1,128)}) custom-call(f32[120,128]{1,0:T(8,128)S(1)} %add_add_fusion.kept_ref, f32[120,128]{1,0:T(8,128)S(1)} %collective-permute-done.11.other_ref), custom_call_target="tpu_custom_call" | custom-call | bytes 3600000 | tf_op jit(solution)/shard_map/final/pallas_call | solution.py:629
  (9 shorter events, 0.1 us)
Async XLA Ops:
  2.4 9.1 %collective-permute-start = (bf16[544,128]{1,0:T(8,128)(2,1)S(1)}, bf16[544,128]{1,0:T(8,128)(2,1)S(1)}, u32[]{:S(2)}, u32[]{:S(2)}) collective-permute-start(bf16[544,128]{1,0:T(8,128)(2,1)S(1)} %get-tuple-element.43.own_packed_ref), channel_id=1, source_target_pairs={{0,4},{4,0},{1,5},{5,1},{2,6},{6,2},{3,7},{7,3},{8,12},{12,8},{9,1... | collective-permute-start | bytes 417800 | tf_op jit(solution)/shard_map/ppermute | solution.py:645
  5.4 6.1 %collective-permute-start.1 = (bf16[2,64,256]{2,1,0:T(8,128)(2,1)S(1)}, bf16[2,64,256]{2,1,0:T(8,128)(2,1)S(1)}, u32[]{:S(2)}, u32[]{:S(2)}) collective-permute-start(bf16[2,64,256]{2,1,0:T(8,128)(2,1)S(1)} %get-tuple-element.44), channel_id=1, source_target_pairs={{0,1},{1,2},{2,3},{3,0},{4,5},{5,6},{6,7},{7,4},{8,9},{9,10},{10,1... | collective-permute-start | bytes 196616 | tf_op jit(solution)/shard_map/ppermute | solution.py:650
  12.6 1.3 %collective-permute-start.4 = (f32[120,128]{1,0:T(8,128)S(1)}, f32[120,128]{1,0:T(8,128)S(1)}, u32[]{:S(2)}, u32[]{:S(2)}) collective-permute-start(f32[120,128]{1,0:T(8,128)S(1)} %get-tuple-element.65), channel_id=1, source_target_pairs={{0,8},{8,0},{16,24},{24,16},{1,9},{9,1},{17,25},{25,17},{2,10},{10... | collective-permute-start | bytes 184328 | tf_op jit(solution)/shard_map/ppermute | solution.py:645
  13.0 7.3 %collective-permute-start.2 = (bf16[512,128]{1,0:T(8,128)(2,1)S(1)}, bf16[512,128]{1,0:T(8,128)(2,1)S(1)}, u32[]{:S(2)}, u32[]{:S(2)}) collective-permute-start(bf16[512,128]{1,0:T(8,128)(2,1)S(1)} %boundary.1.own_boundary_ref), channel_id=1, source_target_pairs={{0,4},{4,0},{1,5},{5,1},{2,6},{6,2},{3,7},{7,3},{8,12},{12,8},{9,1... | collective-permute-start | bytes 393224 | tf_op jit(solution)/shard_map/ppermute | solution.py:645
  13.9 6.4 %collective-permute-start.5 = (bf16[120,128]{1,0:T(8,128)(2,1)S(1)}, bf16[120,128]{1,0:T(8,128)(2,1)S(1)}, u32[]{:S(2)}, u32[]{:S(2)}) collective-permute-start(bf16[120,128]{1,0:T(8,128)(2,1)S(1)} %fusion), channel_id=1, source_target_pairs={{0,20},{1,21},{2,22},{3,23},{4,16},{5,17},{6,18},{7,19},{8,28},{9,... | collective-permute-start | bytes 92168 | tf_op jit(solution)/shard_map/ppermute | solution.py:661
  16.2 4.2 %collective-permute-start.6 = (bf16[120,128]{1,0:T(8,128)(2,1)S(1)}, bf16[120,128]{1,0:T(8,128)(2,1)S(1)}, u32[]{:S(2)}, u32[]{:S(2)}) collective-permute-start(bf16[120,128]{1,0:T(8,128)(2,1)S(1)} %fusion), channel_id=1, source_target_pairs={{0,16},{1,17},{2,18},{3,19},{4,20},{5,21},{6,22},{7,23},{8,24},{9,... | collective-permute-start | bytes 92168 | tf_op jit(solution)/shard_map/ppermute | solution.py:661
  16.7 3.9 %collective-permute-start.7 = (bf16[120,128]{1,0:T(8,128)(2,1)S(1)}, bf16[120,128]{1,0:T(8,128)(2,1)S(1)}, u32[]{:S(2)}, u32[]{:S(2)}) collective-permute-start(bf16[120,128]{1,0:T(8,128)(2,1)S(1)} %fusion), channel_id=1, source_target_pairs={{0,4},{1,5},{2,6},{3,7},{4,0},{5,1},{6,2},{7,3},{8,12},{9,13},{10,... | collective-permute-start | bytes 92168 | tf_op jit(solution)/shard_map/ppermute | solution.py:661
  17.6 6.6 %collective-permute-start.3 = (bf16[2,64,256]{2,1,0:T(8,128)(2,1)S(1)}, bf16[2,64,256]{2,1,0:T(8,128)(2,1)S(1)}, u32[]{:S(2)}, u32[]{:S(2)}) collective-permute-start(bf16[2,64,256]{2,1,0:T(8,128)(2,1)S(1)} %early.1), channel_id=1, source_target_pairs={{0,3},{1,0},{2,1},{3,2},{4,7},{5,4},{6,5},{7,6},{8,11},{9,8},{10,9... | collective-permute-start | bytes 196616 | tf_op jit(solution)/shard_map/ppermute | solution.py:650
  20.7 5.0 %collective-permute-start.8 = (bf16[120,128]{1,0:T(8,128)(2,1)S(1)}, bf16[120,128]{1,0:T(8,128)(2,1)S(1)}, u32[]{:S(2)}, u32[]{:S(2)}) collective-permute-start(bf16[120,128]{1,0:T(8,128)(2,1)S(1)} %fusion.1), channel_id=1, source_target_pairs={{0,2},{1,3},{2,0},{3,1},{4,6},{5,7},{6,4},{7,5},{8,10},{9,11},{10,... | collective-permute-start | bytes 92168 | tf_op jit(solution)/shard_map/ppermute | solution.py:661
  21.5 5.7 %collective-permute-start.10 = (bf16[120,128]{1,0:T(8,128)(2,1)S(1)}, bf16[120,128]{1,0:T(8,128)(2,1)S(1)}, u32[]{:S(2)}, u32[]{:S(2)}) collective-permute-start(bf16[120,128]{1,0:T(8,128)(2,1)S(1)} %fusion.1), channel_id=1, source_target_pairs={{0,3},{1,2},{2,1},{3,0},{4,7},{5,6},{6,5},{7,4},{8,11},{9,10},{10,... | collective-permute-start | bytes 92168 | tf_op jit(solution)/shard_map/ppermute | solution.py:661
  22.9 4.3 %collective-permute-start.9 = (bf16[120,128]{1,0:T(8,128)(2,1)S(1)}, bf16[120,128]{1,0:T(8,128)(2,1)S(1)}, u32[]{:S(2)}, u32[]{:S(2)}) collective-permute-start(bf16[120,128]{1,0:T(8,128)(2,1)S(1)} %fusion.1), channel_id=1, source_target_pairs={{0,1},{1,0},{2,3},{3,2},{4,5},{5,4},{6,7},{7,6},{8,9},{9,8},{10,11... | collective-permute-start | bytes 92168 | tf_op jit(solution)/shard_map/ppermute | solution.py:661
  27.2 1.3 %collective-permute-start.11 = (f32[120,128]{1,0:T(8,128)S(1)}, f32[120,128]{1,0:T(8,128)S(1)}, u32[]{:S(2)}, u32[]{:S(2)}) collective-permute-start(f32[120,128]{1,0:T(8,128)S(1)} %add_add_fusion.kept_ref), channel_id=1, source_target_pairs={{0,8},{8,0},{16,24},{24,16},{1,9},{9,1},{17,25},{25,17},{2,10},{10... | collective-permute-start | bytes 184328 | tf_op jit(solution)/shard_map/ppermute | solution.py:645

commit v8 on v7

--- a/solution.py
+++ b/solution.py
@@ -411,7 +411,7 @@
         preact = mm(taps, jnp.concatenate([earlier, input_ref[t]], 0)) + bias
         gate_step(t, earlier, input_ref, preact, hidden_ref, slopes_ref, right_ref)
     hidden = hidden_ref[DILATION_SIZE * chans :, :]
-    boundary_ref[...] = boundary_rows(hidden, own, chosen_ref[...])
+    boundary_ref[DILATION_SIZE * chans :, :] = boundary_rows(hidden, own, chosen_ref[...])
 
 
 def backward_kernel(
@@ -505,10 +505,9 @@
 
 
 def boundary_kernel(hidden_ref, late_ref, own_ref, chosen_ref, boundary_ref):
-    early_rows = boundary_ref.shape[0] - late_ref.shape[0]
+    early_rows = DILATION_SIZE * chosen_ref.shape[1] // 2
     hidden = hidden_ref[:early_rows, :]
     boundary_ref[:early_rows, :] = boundary_rows(hidden, own_ref[...], chosen_ref[...])
-    boundary_ref[early_rows:, :] = late_ref[...]
 
 
 def hops_kernel(hidden_ref, packed_ref, own_ref, halo_ref, base_ref, spread_ref):
@@ -621,7 +620,7 @@
 DMA = pltpu.SemaphoreType.DMA
 
 
-def call(kernel, name, in_specs, out_shape, args, scratch=(), micros=1.0, space=None):
+def call(kernel, name, in_specs, out_shape, args, scratch=(), micros=1.0, space=None, aliases=None):
     args = [
         pltpu.with_memory_space_constraint(arg, pltpu.HBM) if spec is HBM else arg
         for spec, arg in zip(in_specs, args)
@@ -632,6 +631,7 @@
         in_specs=in_specs,
         out_specs=jax.tree.map(lambda _: space or VMEM, out_shape),
         scratch_shapes=list(scratch),
+        input_output_aliases=aliases or {},
         compiler_params=pltpu.CompilerParams(vmem_limit_bytes=VMEM_BYTES),
         cost_estimate=pl.CostEstimate(
             flops=0, bytes_accessed=int(micros * 3_600_000), transcendentals=0
@@ -750,7 +750,7 @@
             shape((chans, 3 * chans), BF16),
             shape((1, chans), F32),
             shape((chans, 3 * chans), BF16),
-            shape((rows - border_rows, wide), BF16),
+            shape((rows, wide), BF16),
         ),
         (
             sample_input,
@@ -800,7 +800,7 @@
         ),
         micros=2.0,
     )
-    total = kept + swap(given, "dp", 1)
+    total = kept + swap(given.astype(BF16), "dp", 1).astype(F32)
     rounds = groups()
     has_biases = (lax.axis_index("dp") % 2).astype(F32)
     early = call(
@@ -818,6 +818,7 @@
         [VMEM] * 4,
         shape((rows, wide), BF16),
         (hidden, boundary_late, own, chosen),
+        aliases={1: 0},
         micros=0.3,
     )
     first_far = swap(boundary_first, "space", 1)

time: 29.4 us -> 29.4 us (level)
  no operation moved by 1% of the time
where the time goes in v8:
time: 29.4 us; the launch traced here: 29.3 us
  starting transfers between devices  14.5 us (49%)
  Pallas kernels  7.65 us (26%)
  waiting for transfers between devices  6.28 us (21%)
  between operations  0.79 us (3%)
    pallas_call x8, Pallas kernels, call(): pl.pallas_call(kernel, out_shape=out_shape, in_specs=in_specs, out_specs=...  7.65 us
    ppermute x6, starting transfers between devices, flip(): return lax.ppermute(value, AXES, pairs)  7.11 us
    ppermute x2, starting transfers between devices, shift(): lax.ppermute(value, axis, [(source, (source + steps) % count) for source...  3.83 us
    ppermute x4, starting transfers between devices, swap(): lax.ppermute(value, axis, [(source, source ^ bit) for source in range(cou...  3.52 us
    ppermute x2, waiting for transfers between devices, shift(): lax.ppermute(value, axis, [(source, (source + steps) % count) for source...  2.66 us
    ppermute x6, waiting for transfers between devices, flip(): return lax.ppermute(value, AXES, pairs)  1.92 us
    ppermute x4, waiting for transfers between devices, swap(): lax.ppermute(value, axis, [(source, source ^ bit) for source in range(cou...  1.7 us
  transfers between devices with their start and end apart: 12, of which 6 were waited for; matrix products, arithmetic and copies ran while one was open for 0% of the time, Pallas kernels for 14%

profile of v8, /device:TPU:0, one launch (start us, length us, event | category | flops | bytes accessed | tf_op | source)
XLA Modules:
  0.0 29.3 jit_solution(8717548858649493208)
XLA Ops:
  0.6 1.7 %prepare.1 = (bf16[544,128]{1,0:T(8,128)(2,1)S(1)}, bf16[256,256]{1,0:T(8,128)(2,1)S(1)}, bf16[256,128]{1,0:T(8,128)(2,1)S(1)}, bf16[256,128]{1,0:T(8,128)(2,1)S...) custom-call(s32[2,8]{1,0:T(2,128)} %cols_hbm.1, s32[1,2]{1,0:T(1,128)} %counts_hbm.1, ...), custom_call_target="tpu_custom_call" | custom-call | bytes 7200000 | tf_op jit(solution)/shard_map/prepare/pallas_call | solution.py:628
  2.4 3.0 %collective-permute-start = (bf16[544,128]{1,0:T(8,128)(2,1)S(1)}, bf16[544,128]{1,0:T(8,128)(2,1)S(1)}, u32[]{:S(2)}, u32[]{:S(2)}) collective-permute-start(bf16[544,128]{1,0:T(8,128)(2,1)S(1)} %get-tuple-element.43.own_packed_ref), channel_id=1, source_target_pairs={{0,4},{4,0},{1,5},{5,1},{2,6},{6,2},{3,7},{7,3},{8,12},{12,8},{9,1... | collective-permute-start | bytes 417800 | tf_op jit(solution)/shard_map/ppermute | solution.py:645
  5.4 1.6 %collective-permute-start.1 = (bf16[2,64,256]{2,1,0:T(8,128)(2,1)S(1)}, bf16[2,64,256]{2,1,0:T(8,128)(2,1)S(1)}, u32[]{:S(2)}, u32[]{:S(2)}) collective-permute-start(bf16[2,64,256]{2,1,0:T(8,128)(2,1)S(1)} %get-tuple-element.44), channel_id=1, source_target_pairs={{0,1},{1,2},{2,3},{3,0},{4,5},{5,6},{6,7},{7,4},{8,9},{9,10},{10,1... | collective-permute-start | bytes 196616 | tf_op jit(solution)/shard_map/ppermute | solution.py:650
  7.0 1.8 %forward.1 = (bf16[512,256]{1,0:T(8,128)(2,1)S(1)}, f32[8,128,256]{2,1,0:T(8,128)S(1)}, bf16[272,2048]{1,0:T(8,128)(2,1)S(1)}, f32[512,512]{1,0:T(8,128)S(1)}, b...) custom-call(bf16[8,64,256]{2,1,0:T(8,128)(2,1)} %bitcast.11, ...), custom_call_target="tpu_custom_call" | custom-call | bytes 5400000 | tf_op jit(solution)/shard_map/forward/pallas_call | solution.py:628
  8.8 2.7 %collective-permute-done.1.border_ref = bf16[2,64,256]{2,1,0:T(8,128)(2,1)S(1)} collective-permute-done((bf16[2,64,256]{2,1,0:T(8,128)(2,1)S(1)}, bf16[2,64,256]{2,1,0:T(8,128)(2,1)S(1)}, u32[]{:S(2)}, u32[]{:S(2)}) %collective-permute-start.1) | collective-permute-done | bytes 65568 | tf_op jit(solution)/shard_map/ppermute | solution.py:650
  11.5 0.0 collective-permute-done.packed_ref
  11.5 1.1 %backward.1 = (f32[120,128]{1,0:T(8,128)S(1)}, f32[120,128]{1,0:T(8,128)S(1)}, bf16[8,128,256]{2,1,0:T(8,128)(2,1)S(1)}, bf16[512,256]{1,0:T(8,128)(2,1)S(1)}) custom-call(bf16[512,256]{1,0:T(8,128)(2,1)S(1)} %get-tuple-element.39.grad_ref, bf16[544,128]{1,0:T(8,128)(2,1)S(1)} %get-tuple-element.43.own_packed_ref, ...), custom_call_target="tpu_custom_call" | custom-call | bytes 7200000 | tf_op jit(solution)/shard_map/backward/pallas_call | solution.py:628
  12.6 0.1 collective-permute-start.4
  12.7 0.4 %boundary.1.own_boundary_ref = bf16[512,128]{1,0:T(8,128)(2,1)S(1)} custom-call(bf16[512,256]{1,0:T(8,128)(2,1)S(1)} %get-tuple-element.53.hidden_ref, bf16[512,128]{1,0:T(8,128)(2,1)S(1)} %get-tuple-element.54.late_ref, bf16[256,256]{1,0:T(8,128)(2,1)S(1)} %get-tuple-element.40.own_ref, ...), custom_call_target="tpu_custom_call", output_to_operand_aliasing={{}: (1, {})} | custom-call | bytes 1080000 | tf_op jit(solution)/shard_map/boundary/pallas_call | solution.py:628
  13.1 0.3 %collective-permute-start.2 = (bf16[512,128]{1,0:T(8,128)(2,1)S(1)}, bf16[512,128]{1,0:T(8,128)(2,1)S(1)}, u32[]{:S(2)}, u32[]{:S(2)}) collective-permute-start(bf16[512,128]{1,0:T(8,128)(2,1)S(1)} %boundary.1.own_boundary_ref), channel_id=1, source_target_pairs={{0,4},{4,0},{1,5},{5,1},{2,6},{6,2},{3,7},{7,3},{8,12},{12,8},{9,1... | collective-permute-start | bytes 393224 | tf_op jit(solution)/shard_map/ppermute | solution.py:645
  13.4 0.5 %collective-permute-done.4 = bf16[120,128]{1,0:T(8,128)(2,1)S(1)} collective-permute-done((bf16[120,128]{1,0:T(8,128)(2,1)S(1)}, bf16[120,128]{1,0:T(8,128)(2,1)S(1)}, u32[]{:S(2)}, u32[]{:S(2)}) %collective-permute-start.4) | collective-permute-done | bytes 30752 | tf_op jit(solution)/shard_map/ppermute | solution.py:645
  13.9 2.3 %collective-permute-start.5 = (bf16[120,128]{1,0:T(8,128)(2,1)S(1)}, bf16[120,128]{1,0:T(8,128)(2,1)S(1)}, u32[]{:S(2)}, u32[]{:S(2)}) collective-permute-start(bf16[120,128]{1,0:T(8,128)(2,1)S(1)} %fusion), channel_id=1, source_target_pairs={{0,20},{1,21},{2,22},{3,23},{4,16},{5,17},{6,18},{7,19},{8,28},{9,... | collective-permute-start | bytes 92168 | tf_op jit(solution)/shard_map/ppermute | solution.py:661
  16.2 0.5 %collective-permute-start.6 = (bf16[120,128]{1,0:T(8,128)(2,1)S(1)}, bf16[120,128]{1,0:T(8,128)(2,1)S(1)}, u32[]{:S(2)}, u32[]{:S(2)}) collective-permute-start(bf16[120,128]{1,0:T(8,128)(2,1)S(1)} %fusion), channel_id=1, source_target_pairs={{0,16},{1,17},{2,18},{3,19},{4,20},{5,21},{6,22},{7,23},{8,24},{9,... | collective-permute-start | bytes 92168 | tf_op jit(solution)/shard_map/ppermute | solution.py:661
  16.7 0.7 %collective-permute-start.7 = (bf16[120,128]{1,0:T(8,128)(2,1)S(1)}, bf16[120,128]{1,0:T(8,128)(2,1)S(1)}, u32[]{:S(2)}, u32[]{:S(2)}) collective-permute-start(bf16[120,128]{1,0:T(8,128)(2,1)S(1)} %fusion), channel_id=1, source_target_pairs={{0,4},{1,5},{2,6},{3,7},{4,0},{5,1},{6,2},{7,3},{8,12},{9,13},{10,... | collective-permute-start | bytes 92168 | tf_op jit(solution)/shard_map/ppermute | solution.py:661
  17.5 0.2 early.1
  17.6 2.3 %collective-permute-start.3 = (bf16[2,64,256]{2,1,0:T(8,128)(2,1)S(1)}, bf16[2,64,256]{2,1,0:T(8,128)(2,1)S(1)}, u32[]{:S(2)}, u32[]{:S(2)}) collective-permute-start(bf16[2,64,256]{2,1,0:T(8,128)(2,1)S(1)} %early.1), channel_id=1, source_target_pairs={{0,3},{1,0},{2,1},{3,2},{4,7},{5,4},{6,5},{7,6},{8,11},{9,8},{10,9... | collective-permute-start | bytes 196616 | tf_op jit(solution)/shard_map/ppermute | solution.py:650
  19.9 0.4 %hops.1 = (f32[512,512]{1,0:T(8,128)S(1)}, bf16[256,512]{1,0:T(8,128)(2,1)S(1)}) custom-call(bf16[512,256]{1,0:T(8,128)(2,1)S(1)} %get-tuple-element.53.hidden_ref, bf16[544,128]{1,0:T(8,128)(2,1)S(1)} %collective-permute-done.packed_ref, bf16[256,256]{1,0:T(8,128)(2,1)S(1)} %get-tuple-element.40.own_ref, bf16[256,128]{1,0:T(8,128)(2,1)S(1)} %get-tuple-element.55.halo_ref), custom_call_target="tpu_custom_call" | custom-call | bytes 1800000 | tf_op jit(solution)/shard_map/hops/pallas_call | solution.py:628
  20.3 0.0 collective-permute-done.5
  20.4 0.0 collective-permute-done.2.boundary_ref
  20.4 0.0 collective-permute-done.6
  20.4 0.2 collective-permute-done.7
  20.7 0.8 %collective-permute-start.8 = (bf16[120,128]{1,0:T(8,128)(2,1)S(1)}, bf16[120,128]{1,0:T(8,128)(2,1)S(1)}, u32[]{:S(2)}, u32[]{:S(2)}) collective-permute-start(bf16[120,128]{1,0:T(8,128)(2,1)S(1)} %fusion.1), channel_id=1, source_target_pairs={{0,2},{1,3},{2,0},{3,1},{4,6},{5,7},{6,4},{7,5},{8,10},{9,11},{10,... | collective-permute-start | bytes 92168 | tf_op jit(solution)/shard_map/ppermute | solution.py:661
  21.5 1.4 %collective-permute-start.10 = (bf16[120,128]{1,0:T(8,128)(2,1)S(1)}, bf16[120,128]{1,0:T(8,128)(2,1)S(1)}, u32[]{:S(2)}, u32[]{:S(2)}) collective-permute-start(bf16[120,128]{1,0:T(8,128)(2,1)S(1)} %fusion.1), channel_id=1, source_target_pairs={{0,3},{1,2},{2,1},{3,0},{4,7},{5,6},{6,5},{7,4},{8,11},{9,10},{10,... | collective-permute-start | bytes 92168 | tf_op jit(solution)/shard_map/ppermute | solution.py:661
  22.9 1.4 %collective-permute-start.9 = (bf16[120,128]{1,0:T(8,128)(2,1)S(1)}, bf16[120,128]{1,0:T(8,128)(2,1)S(1)}, u32[]{:S(2)}, u32[]{:S(2)}) collective-permute-start(bf16[120,128]{1,0:T(8,128)(2,1)S(1)} %fusion.1), channel_id=1, source_target_pairs={{0,1},{1,0},{2,3},{3,2},{4,5},{5,4},{6,7},{7,6},{8,9},{9,8},{10,11... | collective-permute-start | bytes 92168 | tf_op jit(solution)/shard_map/ppermute | solution.py:661
  24.2 0.0 collective-permute-done.3.early_ref
  24.2 1.3 %finish.1 = (bf16[8,64,256]{2,1,0:T(8,128)(2,1)}, bf16[8,64,256]{2,1,0:T(8,128)(2,1)}) custom-call(bf16[8,64,256]{2,1,0:T(8,128)(2,1)S(1)} %get-tuple-element.42.input_ref, bf16[512,256]{1,0:T(8,128)(2,1)S(1)} %get-tuple-element.53.hidden_ref, bf16[512,128]{1,0:T(8,128)(2,1)S(1)} %boundary.1.own_boundary_ref, ...), custom_call_target="tpu_custom_call" | custom-call | bytes 7200000 | tf_op jit(solution)/shard_map/finish/pallas_call | solution.py:628
  25.5 0.2 collective-permute-done.8
  25.7 1.5 %collective-permute-done.10 = bf16[120,128]{1,0:T(8,128)(2,1)S(1)} collective-permute-done((bf16[120,128]{1,0:T(8,128)(2,1)S(1)}, bf16[120,128]{1,0:T(8,128)(2,1)S(1)}, u32[]{:S(2)}, u32[]{:S(2)}) %collective-permute-start.10) | collective-permute-done | bytes 30752 | tf_op jit(solution)/shard_map/ppermute | solution.py:661
  27.2 0.0 collective-permute-done.9
  27.2 0.1 collective-permute-start.11
  27.3 1.2 %collective-permute-done.11.other_ref = f32[120,128]{1,0:T(8,128)S(1)} collective-permute-done((f32[120,128]{1,0:T(8,128)S(1)}, f32[120,128]{1,0:T(8,128)S(1)}, u32[]{:S(2)}, u32[]{:S(2)}) %collective-permute-start.11) | collective-permute-done | bytes 61472 | tf_op jit(solution)/shard_map/ppermute | solution.py:645
  28.6 0.7 %final.1 = (f32[2,64,128]{2,1,0:T(8,128)}, f32[1,128]{1,0:T(1,128)}, f32[3,64,64]{2,1,0:T(8,128)}, f32[1,64]{1,0:T(1,128)}) custom-call(f32[120,128]{1,0:T(8,128)S(1)} %add_add_fusion.kept_ref, f32[120,128]{1,0:T(8,128)S(1)} %collective-permute-done.11.other_ref), custom_call_target="tpu_custom_call" | custom-call | bytes 3600000 | tf_op jit(solution)/shard_map/final/pallas_call | solution.py:628
  (10 shorter events, 0.1 us)
Async XLA Ops:
  2.4 9.1 %collective-permute-start = (bf16[544,128]{1,0:T(8,128)(2,1)S(1)}, bf16[544,128]{1,0:T(8,128)(2,1)S(1)}, u32[]{:S(2)}, u32[]{:S(2)}) collective-permute-start(bf16[544,128]{1,0:T(8,128)(2,1)S(1)} %get-tuple-element.43.own_packed_ref), channel_id=1, source_target_pairs={{0,4},{4,0},{1,5},{5,1},{2,6},{6,2},{3,7},{7,3},{8,12},{12,8},{9,1... | collective-permute-start | bytes 417800 | tf_op jit(solution)/shard_map/ppermute | solution.py:645
  5.4 6.1 %collective-permute-start.1 = (bf16[2,64,256]{2,1,0:T(8,128)(2,1)S(1)}, bf16[2,64,256]{2,1,0:T(8,128)(2,1)S(1)}, u32[]{:S(2)}, u32[]{:S(2)}) collective-permute-start(bf16[2,64,256]{2,1,0:T(8,128)(2,1)S(1)} %get-tuple-element.44), channel_id=1, source_target_pairs={{0,1},{1,2},{2,3},{3,0},{4,5},{5,6},{6,7},{7,4},{8,9},{9,10},{10,1... | collective-permute-start | bytes 196616 | tf_op jit(solution)/shard_map/ppermute | solution.py:650
  12.6 1.3 %collective-permute-start.4 = (bf16[120,128]{1,0:T(8,128)(2,1)S(1)}, bf16[120,128]{1,0:T(8,128)(2,1)S(1)}, u32[]{:S(2)}, u32[]{:S(2)}) collective-permute-start(bf16[120,128]{1,0:T(8,128)(2,1)S(1)} %convert_element_type.36), channel_id=1, source_target_pairs={{0,8},{8,0},{16,24},{24,16},{1,9},{9,1},{17,25},{25,17},{2,10},{10... | collective-permute-start | bytes 92168 | tf_op jit(solution)/shard_map/ppermute | solution.py:645
  13.1 7.3 %collective-permute-start.2 = (bf16[512,128]{1,0:T(8,128)(2,1)S(1)}, bf16[512,128]{1,0:T(8,128)(2,1)S(1)}, u32[]{:S(2)}, u32[]{:S(2)}) collective-permute-start(bf16[512,128]{1,0:T(8,128)(2,1)S(1)} %boundary.1.own_boundary_ref), channel_id=1, source_target_pairs={{0,4},{4,0},{1,5},{5,1},{2,6},{6,2},{3,7},{7,3},{8,12},{12,8},{9,1... | collective-permute-start | bytes 393224 | tf_op jit(solution)/shard_map/ppermute | solution.py:645
  13.9 6.4 %collective-permute-start.5 = (bf16[120,128]{1,0:T(8,128)(2,1)S(1)}, bf16[120,128]{1,0:T(8,128)(2,1)S(1)}, u32[]{:S(2)}, u32[]{:S(2)}) collective-permute-start(bf16[120,128]{1,0:T(8,128)(2,1)S(1)} %fusion), channel_id=1, source_target_pairs={{0,20},{1,21},{2,22},{3,23},{4,16},{5,17},{6,18},{7,19},{8,28},{9,... | collective-permute-start | bytes 92168 | tf_op jit(solution)/shard_map/ppermute | solution.py:661
  16.2 4.2 %collective-permute-start.6 = (bf16[120,128]{1,0:T(8,128)(2,1)S(1)}, bf16[120,128]{1,0:T(8,128)(2,1)S(1)}, u32[]{:S(2)}, u32[]{:S(2)}) collective-permute-start(bf16[120,128]{1,0:T(8,128)(2,1)S(1)} %fusion), channel_id=1, source_target_pairs={{0,16},{1,17},{2,18},{3,19},{4,20},{5,21},{6,22},{7,23},{8,24},{9,... | collective-permute-start | bytes 92168 | tf_op jit(solution)/shard_map/ppermute | solution.py:661
  16.7 3.9 %collective-permute-start.7 = (bf16[120,128]{1,0:T(8,128)(2,1)S(1)}, bf16[120,128]{1,0:T(8,128)(2,1)S(1)}, u32[]{:S(2)}, u32[]{:S(2)}) collective-permute-start(bf16[120,128]{1,0:T(8,128)(2,1)S(1)} %fusion), channel_id=1, source_target_pairs={{0,4},{1,5},{2,6},{3,7},{4,0},{5,1},{6,2},{7,3},{8,12},{9,13},{10,... | collective-permute-start | bytes 92168 | tf_op jit(solution)/shard_map/ppermute | solution.py:661
  17.6 6.6 %collective-permute-start.3 = (bf16[2,64,256]{2,1,0:T(8,128)(2,1)S(1)}, bf16[2,64,256]{2,1,0:T(8,128)(2,1)S(1)}, u32[]{:S(2)}, u32[]{:S(2)}) collective-permute-start(bf16[2,64,256]{2,1,0:T(8,128)(2,1)S(1)} %early.1), channel_id=1, source_target_pairs={{0,3},{1,0},{2,1},{3,2},{4,7},{5,4},{6,5},{7,6},{8,11},{9,8},{10,9... | collective-permute-start | bytes 196616 | tf_op jit(solution)/shard_map/ppermute | solution.py:650
  20.7 5.0 %collective-permute-start.8 = (bf16[120,128]{1,0:T(8,128)(2,1)S(1)}, bf16[120,128]{1,0:T(8,128)(2,1)S(1)}, u32[]{:S(2)}, u32[]{:S(2)}) collective-permute-start(bf16[120,128]{1,0:T(8,128)(2,1)S(1)} %fusion.1), channel_id=1, source_target_pairs={{0,2},{1,3},{2,0},{3,1},{4,6},{5,7},{6,4},{7,5},{8,10},{9,11},{10,... | collective-permute-start | bytes 92168 | tf_op jit(solution)/shard_map/ppermute | solution.py:661
  21.5 5.7 %collective-permute-start.10 = (bf16[120,128]{1,0:T(8,128)(2,1)S(1)}, bf16[120,128]{1,0:T(8,128)(2,1)S(1)}, u32[]{:S(2)}, u32[]{:S(2)}) collective-permute-start(bf16[120,128]{1,0:T(8,128)(2,1)S(1)} %fusion.1), channel_id=1, source_target_pairs={{0,3},{1,2},{2,1},{3,0},{4,7},{5,6},{6,5},{7,4},{8,11},{9,10},{10,... | collective-permute-start | bytes 92168 | tf_op jit(solution)/shard_map/ppermute | solution.py:661
  22.9 4.3 %collective-permute-start.9 = (bf16[120,128]{1,0:T(8,128)(2,1)S(1)}, bf16[120,128]{1,0:T(8,128)(2,1)S(1)}, u32[]{:S(2)}, u32[]{:S(2)}) collective-permute-start(bf16[120,128]{1,0:T(8,128)(2,1)S(1)} %fusion.1), channel_id=1, source_target_pairs={{0,1},{1,0},{2,3},{3,2},{4,5},{5,4},{6,7},{7,6},{8,9},{9,8},{10,11... | collective-permute-start | bytes 92168 | tf_op jit(solution)/shard_map/ppermute | solution.py:661
  27.2 1.3 %collective-permute-start.11 = (f32[120,128]{1,0:T(8,128)S(1)}, f32[120,128]{1,0:T(8,128)S(1)}, u32[]{:S(2)}, u32[]{:S(2)}) collective-permute-start(f32[120,128]{1,0:T(8,128)S(1)} %add_add_fusion.kept_ref), channel_id=1, source_target_pairs={{0,8},{8,0},{16,24},{24,16},{1,9},{9,1},{17,25},{25,17},{2,10},{10... | collective-permute-start | bytes 184328 | tf_op jit(solution)/shard_map/ppermute | solution.py:645
